TPU v7x, 256 devices: a whole 4x4x8 slice. The times are simulated.
256 devices in a mesh: mem: 2 (over z_hi), tx: 16 (over z_lo, y), ty: 8 (over x, core).
Axes of the slice: x: 4, y: 4, z: 8 (z_hi: 2, z_lo: 4; z = z_hi * 4 + z_lo), core: 2. Of those that a mesh axis runs over, the one named last changes fastest.
Arguments:
- static_control: bfloat16 [768, 384, 128], P('tx', 'ty', 'mem'), may hold values from -6 to 6
- member_control: bfloat16 [4, 768, 384, 128], P('mem', 'tx', 'ty'), may hold values from -6 to 6
- perturbations: bfloat16 [4, 768, 384, 128], P('mem', 'tx', 'ty'), may hold values from -2.5 to 2.5
- departures: bfloat16 [768, 384, 128], P('tx', 'ty'), may hold values from -6 to 6
- obs_weight: bfloat16 [768, 384, 128], P('tx', 'ty'), may hold values from 0.25 to 2
- static_kx: bfloat16 [49], replicated, may hold values from 0.08984375 to 0.25976562
- static_ky: bfloat16 [49], replicated, may hold values from 0.08984375 to 0.25976562
- local_kx: bfloat16 [97], replicated, may hold values from 0.059814453 to 0.1796875
- local_ky: bfloat16 [97], replicated, may hold values from 0.059814453 to 0.1796875
- static_vertical: bfloat16 [128, 128], replicated, may hold values from -0.5 to 0.5
- local_vertical: bfloat16 [128, 128], replicated, may hold values from -0.5 to 0.5
Outputs:
- grad_static: bfloat16 [768, 384, 128], P('tx', 'ty', 'mem')
- grad_members: bfloat16 [4, 768, 384, 128], P('mem', 'tx', 'ty')
All inputs are finite; a program needn't handle non-finite values.
Results may differ from a plain program's by a relative error of at most 0.0055.
Values may be sent and summed in bfloat16 or wider, within the bound.
No kernel may reach another device: no remote copies, remote signals or barrier semaphores. Data moves between devices by JAX's collectives and lax.ppermute only.
A program may use at most 64 MiB of HBM per device.

v0:
```python
import functools

import jax
import jax.numpy as jnp
from jax import lax
from jax.experimental import pallas as pl
from jax.experimental.pallas import tpu as pltpu
from jax.sharding import PartitionSpec as P

TILE = 48
SLAB = 32
BF = jnp.bfloat16
F32 = jnp.float32


VMEM = pl.BlockSpec(memory_space=pltpu.VMEM)
ANY = pl.BlockSpec(memory_space=pl.ANY)


def call(kernel, out_shape, args, flops, scratch=(), in_any=(), out_any=(), aliases=None):
    outs = tuple(out_shape)
    moved = sum(a.size * a.dtype.itemsize for a in args)
    moved += sum(o.size * jnp.dtype(o.dtype).itemsize for o in outs)
    return pl.pallas_call(
        kernel,
        out_shape=outs,
        in_specs=[ANY if i in in_any else VMEM for i in range(len(args))],
        out_specs=tuple(ANY if i in out_any else VMEM for i in range(len(outs))),
        scratch_shapes=list(scratch),
        input_output_aliases=aliases or {},
        compiler_params=pltpu.CompilerParams(vmem_limit_bytes=20 << 20),
        cost_estimate=pl.CostEstimate(flops=flops, bytes_accessed=moved, transcendentals=0),
    )(*args)


def shape(*sizes, dtype=BF):
    return jax.ShapeDtypeStruct(sizes, dtype)


def band(row, rows, cols):
    spread = jnp.broadcast_to(row, (rows, row.shape[1]))
    return pltpu.roll(spread, 0, 1, stride=1, stride_axis=0)[:, :cols].astype(BF)


def halves(a):
    return jnp.concatenate([a[: a.shape[0] // 2], a[a.shape[0] // 2 :]], axis=-1)


def unhalves(a):
    n = a.shape[-1] // 2
    return jnp.concatenate([a[..., :n], a[..., n:]], axis=0)


def dot(a, b):
    return jnp.dot(a, b, preferred_element_type=F32)


def along_y(matrix, line, count, store):
    def step(i, carry):
        pair = jnp.concatenate([line(2 * i), line(2 * i + 1)], axis=1)
        out = dot(matrix, pair)
        store(2 * i, out[:, :128])
        store(2 * i + 1, out[:, 128:])
        return carry

    lax.fori_loop(0, count // 2, step, 0, unroll=count // 2)


def along_x(matrix, parts):
    turned = [jnp.swapaxes(p, 0, 1) for p in parts]
    outs = []
    for j in range(0, 16, 2):
        cols = [
            jnp.concatenate([t[j + k] for t in turned], axis=0) if len(turned) > 1 else turned[0][j + k]
            for k in (0, 1)
        ]
        out = dot(matrix, jnp.concatenate(cols, axis=1))
        outs += [out[:, :128].astype(BF), out[:, 128:].astype(BF)]
    return jnp.swapaxes(jnp.stack(outs), 0, 1)


def static_parts(left, own, right):
    swap = jnp.concatenate([own[..., 64:], own[..., :64]], axis=-1)
    first = jnp.concatenate([unhalves(left), swap[..., 64:]], axis=-1)
    last = jnp.concatenate([swap[..., :64], unhalves(right)], axis=-1)
    return jnp.concatenate([first, own, last], axis=0)


def pack_slabs(packed, right_ref, left_ref):
    right_ref[2304:] = packed[:, 16:48].reshape(768, 128)
    left_ref[2304:] = packed[:, :SLAB].reshape(768, 128)


def take_kernel(member_ref, out_ref, sems):
    copies = [
        pltpu.make_async_copy(member_ref.at[0, pl.ds(12 * i, 12)], out_ref.at[pl.ds(12 * i, 12)], sems.at[i])
        for i in range(4)
    ]
    for copy in copies:
        copy.start()
    for copy in copies:
        copy.wait()


def pack_kernel(static_ref, member_ref, after_ref, right_ref, left_ref, own_ref, static, second, sems):
    copies = [
        pltpu.make_async_copy(member_ref.at[1, pl.ds(24 * i, 24)], second.at[pl.ds(24 * i, 24)], sems.at[i])
        for i in range(2)
    ]
    copies += [
        pltpu.make_async_copy(static_ref.at[pl.ds(24 * i, 24)], static.at[pl.ds(24 * i, 24)], sems.at[2 + i])
        for i in range(2)
    ]
    for copy in copies:
        copy.start()
    for copy in copies:
        copy.wait()
    member = second[...].reshape(2304, 128)
    right_ref[:2304] = member
    left_ref[:2304] = member
    packed = halves(static[...])
    own_ref[...] = packed
    pack_slabs(packed, right_ref, left_ref)


def first_y_kernel(row_m, row_s, taps_ref, sent_ref, own_ref, left_ref, right_ref, to_r_ref, to_l_ref, out_ref):
    member = band(taps_ref[row_m : row_m + 1], TILE, 144)
    static = band(taps_ref[row_s : row_s + 1], TILE, 112)

    def member_line(x):
        at = pl.ds(pl.multiple_of(x * TILE, TILE), TILE)
        return jnp.concatenate([left_ref[at], sent_ref[at], right_ref[at]], axis=0)

    def member_store(x, out):
        out = out.astype(BF)
        to_r_ref[x] = out
        to_l_ref[x] = out

    along_y(member, member_line, TILE, member_store)

    def static_line(x):
        at = pl.ds(pl.multiple_of(2304 + x * SLAB, SLAB), SLAB)
        return jnp.concatenate([left_ref[at], own_ref[x], right_ref[at]], axis=0)

    def static_store(x, out):
        out_ref[x] = out.astype(BF)

    along_y(static, static_line, 24, static_store)
    packed = out_ref[...]
    to_r_ref[TILE:] = halves(packed[..., 64:])
    to_l_ref[TILE:] = halves(packed[..., :64])


def first_x_kernel(row, taps_ref, own_ref, left_ref, right_ref, out_ref):
    matrix = band(taps_ref[row : row + 1], TILE, 144)
    for c in range(0, TILE, 16):
        at = slice(c, c + 16)
        out_ref[:, at] = along_x(matrix, [left_ref[:, at], own_ref[:, at], right_ref[:, at]])


def second_y(row, taps_ref, own_ref, left_ref, right_ref, store):
    matrix = band(taps_ref[row : row + 1], TILE, 144)

    def line(x):
        return jnp.concatenate([left_ref[x], own_ref[x], right_ref[x]], axis=0)

    along_y(matrix, line, TILE, store)


def second_x(rows, taps_ref, own_ref, left_ref, right_ref, s_ref, block):
    matrix = band(taps_ref[rows[0] : rows[0] + 1], TILE, 144)
    matrix_s = band(taps_ref[rows[1] : rows[1] + 1], 24, 72)
    for c in range(0, TILE, 16):
        at = slice(c, c + 16)
        b = along_x(matrix, [left_ref[:TILE, at], own_ref[:TILE, at], right_ref[:TILE, at]])
        lines = static_parts(left_ref[TILE:, at], s_ref[:, at], right_ref[TILE:, at])
        block(at, b, along_x(matrix_s, [lines]))


def static_block(static_ref):
    full = static_ref[...]
    cols = jnp.where(lax.axis_index("mem") == 0, full[:, :64], full[:, 64:])
    zero = jnp.zeros_like(cols)
    return jnp.concatenate([jnp.concatenate([cols, zero], axis=1), jnp.concatenate([zero, cols], axis=1)], axis=0)


def dot_t(a, b):
    return lax.dot_general(a, b, (((1,), (1,)), ((), ())), preferred_element_type=F32)


def forward_a_kernel(row, taps_ref, own_ref, left_ref, right_ref, pert_ref, vert_ref, out_ref, filtered):
    def store(x, out):
        filtered[x] = out.astype(BF)

    second_y(row, taps_ref, own_ref, left_ref, right_ref, store)
    vert = vert_ref[...]

    def step(i, carry):
        at = pl.ds(8 * i, 8)
        local = dot_t(filtered[at].reshape(384, 128), vert).reshape(8, TILE, 128)
        out_ref[at] = pert_ref[0, at].astype(F32) * local
        return carry

    lax.fori_loop(0, 6, step, 0, unroll=2)


def forward_b_kernel(
    rows, taps_ref, own_ref, left_ref, right_ref, s_ref, first_ref, pert_ref, vert_ref, static_ref,
    kept_ref, sent_ref
):
    vert = vert_ref[...]
    static_mat = static_block(static_ref)

    def block(at, b, s):
        total = first_ref[:, at]
        total += pert_ref[1, :, at].astype(F32) * dot_t(b.reshape(768, 128), vert).reshape(TILE, 16, 128)
        static = dot_t(s.reshape(384, 128), static_mat)
        total += jnp.concatenate([static[:, :128], static[:, 128:]], axis=0).reshape(TILE, 16, 128)
        kept_ref[:, at] = total
        sent_ref[:, at] = total.astype(BF)

    second_x(rows, taps_ref, own_ref, left_ref, right_ref, s_ref, block)


def residual_kernel(
    kept_ref, came_ref, dep_ref, weight_ref, pert_ref, vert_ref, static_ref,
    a_ref, right_ref, left_ref, own_ref
):
    vert = vert_ref[...]
    static_mat = static_block(static_ref)

    def step(i, carry):
        res = []
        for x in (4 * i, 24 + 4 * i):
            at = pl.ds(x, 4)
            total = kept_ref[at] + came_ref[at].astype(F32)
            r = (weight_ref[at].astype(F32) * (total - dep_ref[at].astype(F32))).astype(BF)
            r32 = r.astype(F32)
            res.append(r.reshape(192, 128))
            first = (pert_ref[0, at].astype(F32) * r32).astype(BF).reshape(192, 128)
            second = (pert_ref[1, at].astype(F32) * r32).astype(BF).reshape(192, 128)
            a_ref[at] = dot(first, vert).astype(BF).reshape(4, TILE, 128)
            back = dot(second, vert).astype(BF)
            cells = pl.ds(pl.multiple_of(x * TILE, 192), 192)
            right_ref[cells] = back
            left_ref[cells] = back
        static = dot(jnp.concatenate(res, axis=1), static_mat).astype(BF)
        own_ref[pl.ds(4 * i, 4)] = static.reshape(4, TILE, 128)
        return carry

    lax.fori_loop(0, 6, step, 0, unroll=2)
    pack_slabs(own_ref[...], right_ref, left_ref)


def last_a_kernel(row, taps_ref, own_ref, left_ref, right_ref, member_ref, out_ref, out, sems):
    def store(x, filtered):
        out[x] = (member_ref[0, x].astype(F32) + filtered.astype(BF).astype(F32)).astype(BF)

    second_y(row, taps_ref, own_ref, left_ref, right_ref, store)
    copies = [
        pltpu.make_async_copy(out.at[pl.ds(12 * i, 12)], out_ref.at[0, pl.ds(12 * i, 12)], sems.at[i])
        for i in range(4)
    ]
    for copy in copies:
        copy.start()
    for copy in copies:
        copy.wait()


def last_b_kernel(
    rows, taps_ref, own_ref, left_ref, right_ref, s_ref, member_ref, control_ref, begun_ref,
    static_out, member_out, static, member, sems
):
    copies = []

    def block(at, b, s):
        i = len(copies) // 2
        member[i] = (member_ref[1, :, at].astype(F32) + b.astype(F32)).astype(BF)
        both = control_ref[:, at].astype(F32) + s.astype(F32)
        static[i] = unhalves(both.astype(BF))
        for copy in (
            pltpu.make_async_copy(member.at[i], member_out.at[1, :, at], sems.at[0, i]),
            pltpu.make_async_copy(static.at[i], static_out.at[:, at], sems.at[1, i]),
        ):
            copy.start()
            copies.append(copy)

    second_x(rows, taps_ref, own_ref, left_ref, right_ref, s_ref, block)
    for copy in copies:
        copy.wait()


def from_left(field, axis):
    size = lax.axis_size(axis)
    return lax.ppermute(field, axis, [(i, i + 1) for i in range(size - 1)])


def from_right(field, axis):
    size = lax.axis_size(axis)
    return lax.ppermute(field, axis, [(i + 1, i) for i in range(size - 1)])


def first_filters(taps, back, a, to_r, to_l, own):
    a_halo = (from_left(a, "tx"), from_right(a, "tx"))
    b_halo = (from_left(to_r, "ty"), from_right(to_l, "ty"))
    tile = (TILE, TILE, 128)
    b_to_r, b_to_l, s = call(
        functools.partial(first_y_kernel, 1 + back, 3 + back),
        (shape(60, TILE, 128), shape(60, TILE, 128), shape(24, TILE, 128)),
        (taps, to_r, own) + b_halo,
        700_000_000,
    )
    b_halo = (from_left(b_to_r, "tx"), from_right(b_to_l, "tx"))
    (a,) = call(functools.partial(first_x_kernel, back), (shape(*tile),), (taps, a) + a_halo, 500_000_000)
    a_halo = (from_left(a, "ty"), from_right(a, "ty"))
    return (a,) + a_halo, (b_to_r,) + b_halo + (s,)


def body(
    static_control,
    member_control,
    perturbations,
    departures,
    obs_weight,
    static_kx,
    static_ky,
    local_kx,
    local_ky,
    static_vertical,
    local_vertical,
):
    rows = []
    for flip in (False, True):
        for taps, start in ((local_kx, 0), (local_ky, 0), (static_kx, 0), (static_ky, SLAB - 24)):
            taps = taps[::-1] if flip else taps
            rows.append(jnp.pad(taps.astype(F32), (start, 256 - start - taps.shape[0])))
    taps = jnp.stack(rows)
    tile = (TILE, TILE, 128)
    sent_shapes = (shape(3072, 128), shape(3072, 128), shape(24, TILE, 128))

    (a,) = call(
        take_kernel, (shape(*tile),), (member_control,), 1_000_000,
        [pltpu.SemaphoreType.DMA((4,))], in_any=(0,),
    )
    to_r, to_l, control = call(
        pack_kernel, sent_shapes, (static_control, member_control, a), 1_000_000,
        [pltpu.VMEM((TILE, TILE, 64), BF), pltpu.VMEM(tile, BF), pltpu.SemaphoreType.DMA((4,))],
        in_any=(0, 1, 2),
    )
    a, b = first_filters(taps, 0, a, to_r, to_l, control)
    (first,) = call(
        functools.partial(forward_a_kernel, 1), (shape(*tile, dtype=F32),),
        (taps,) + a + (perturbations, local_vertical), 800_000_000, [pltpu.VMEM(tile, BF)],
    )
    kept, sent = call(
        functools.partial(forward_b_kernel, (0, 2)), (shape(*tile, dtype=F32), shape(*tile)),
        (taps,) + b + (first, perturbations, local_vertical, static_vertical), 1_000_000_000,
    )
    size = lax.axis_size("mem")
    came = lax.ppermute(sent, "mem", [(i, size - 1 - i) for i in range(size)])
    a, to_r, to_l, own = call(
        residual_kernel, (shape(*tile),) + sent_shapes,
        (kept, came, departures, obs_weight, perturbations, local_vertical, static_vertical), 400_000_000,
    )
    a, b = first_filters(taps, 4, a, to_r, to_l, own)
    (begun,) = call(
        functools.partial(last_a_kernel, 5), (shape(2, *tile),), (taps,) + a + (member_control,), 500_000_000,
        [pltpu.VMEM(tile, BF), pltpu.SemaphoreType.DMA((4,))], out_any=(0,),
    )
    args = (taps,) + b + (member_control, control, begun)
    return tuple(call(
        functools.partial(last_b_kernel, (4, 6)), (shape(TILE, TILE, 64), shape(2, *tile)), args, 700_000_000,
        [pltpu.VMEM((3, TILE, 16, 64), BF), pltpu.VMEM((3, TILE, 16, 128), BF), pltpu.SemaphoreType.DMA((2, 3))],
        in_any=(len(args) - 1,), out_any=(0, 1), aliases={len(args) - 1: 1},
    ))


def solution(mesh):
    return jax.shard_map(
        body,
        mesh=mesh,
        in_specs=(
            P("tx", "ty", "mem"),
            P("mem", "tx", "ty", None),
            P("mem", "tx", "ty", None),
            P("tx", "ty", None),
            P("tx", "ty", None),
            P(),
            P(),
            P(),
            P(),
            P(),
            P(),
        ),
        out_specs=(P("tx", "ty", "mem"), P("mem", "tx", "ty", None)),
        check_vma=False,
    )
```

profile of v0, /device:TPU:25, one launch (start us, length us, event | category | flops | bytes accessed | tf_op | source)
XLA Modules:
  0.0 130.4 jit_solution(918918637364364617)
XLA Ops:
  0.6 0.0 copy-start
  0.6 1.3 copy-done
  1.9 0.8 shard_map.122.after_ref.own_ref
  2.7 0.3 copy-done.3
  3.0 1.5 %shard_map.123 = (bf16[3072,128]{1,0:T(8,128)(2,1)S(1)}, bf16[3072,128]{1,0:T(8,128)(2,1)}, bf16[24,48,128]{2,1,0:T(8,128)(2,1)S(1)}) custom-call(bf16[48,48,64]{2,1,0:T(8,128)(2,1)S(1)} %copy-done.3, bf16[2,48,48,128]{3,2,1,0:T(8,128)(2,1)S(1)} %copy-done, bf16[48,48,128]{2,1,0:T(8,128)(2,1)S(1)} %shard_map.122.after_ref.own_ref), custom_call_target="tpu_custom_call" | custom-call | flops 1000000 | bytes 3932160 | tf_op jit(solution)/shard_map/pallas_call | solution.py:24
  4.4 3.7 %collective-permute-start = (bf16[3072,128]{1,0:T(8,128)(2,1)S(1)}, bf16[3072,128]{1,0:T(8,128)(2,1)S(1)}, u32[]{:S(2)}, u32[]{:S(2)}) collective-permute-start(bf16[3072,128]{1,0:T(8,128)(2,1)S(1)} %get-tuple-element.17.sent_ref), channel_id=1, source_target_pairs={{0,1},{1,2},{2,3},{3,4},{4,5},{5,6},{6,7},{8,9},{9,10},{10,11},{11... | collective-permute-start | bytes 2359304 | tf_op jit(solution)/shard_map/ppermute | solution.py:295
  8.1 1.9 %collective-permute-start.1 = (bf16[3072,128]{1,0:T(8,128)(2,1)}, bf16[3072,128]{1,0:T(8,128)(2,1)S(1)}, u32[]{:S(2)}, u32[]{:S(2)}) collective-permute-start(bf16[3072,128]{1,0:T(8,128)(2,1)} %get-tuple-element.19), channel_id=1, source_target_pairs={{1,0},{2,1},{3,2},{4,3},{5,4},{6,5},{7,6},{9,8},{10,9},{11,10},{12... | collective-permute-start | bytes 2359304 | tf_op jit(solution)/shard_map/ppermute | solution.py:300
  10.1 3.2 %collective-permute-start.4 = (bf16[48,48,128]{2,1,0:T(8,128)(2,1)S(1)}, bf16[48,48,128]{2,1,0:T(8,128)(2,1)}, u32[]{:S(2)}, u32[]{:S(2)}) collective-permute-start(bf16[48,48,128]{2,1,0:T(8,128)(2,1)S(1)} %shard_map.122.after_ref.own_ref), channel_id=1, source_target_pairs={{0,8},{8,16},{16,24},{24,32},{32,40},{40,48},{48,56},{56,64},{64,7... | collective-permute-start | bytes 1769480 | tf_op jit(solution)/shard_map/ppermute | solution.py:295
  13.3 2.1 %collective-permute-start.5 = (bf16[48,48,128]{2,1,0:T(8,128)(2,1)S(1)}, bf16[48,48,128]{2,1,0:T(8,128)(2,1)}, u32[]{:S(2)}, u32[]{:S(2)}) collective-permute-start(bf16[48,48,128]{2,1,0:T(8,128)(2,1)S(1)} %shard_map.122.after_ref.own_ref), channel_id=1, source_target_pairs={{8,0},{16,8},{24,16},{32,24},{40,32},{48,40},{56,48},{64,56},{72,6... | collective-permute-start | bytes 1769480 | tf_op jit(solution)/shard_map/ppermute | solution.py:300
  15.4 0.0 copy-done.8
  15.4 0.1 rev.12
  15.5 0.0 copy-done.9
  15.5 0.1 rev.13
  15.6 0.0 copy-done.10
  15.6 0.1 rev.14
  15.7 0.1 pad.38
  15.8 0.1 rev.15
  16.0 0.1 pad.42
  16.1 1.0 collective-permute-done.left_ref
  17.0 5.0 %collective-permute-done.1.right_ref = bf16[3072,128]{1,0:T(8,128)(2,1)S(1)} collective-permute-done((bf16[3072,128]{1,0:T(8,128)(2,1)}, bf16[3072,128]{1,0:T(8,128)(2,1)S(1)}, u32[]{:S(2)}, u32[]{:S(2)}) %collective-permute-start.1) | collective-permute-done | bytes 786464 | tf_op jit(solution)/shard_map/ppermute | solution.py:300
  22.0 0.6 shard_map.124
  22.7 3.2 %collective-permute-start.2 = (bf16[60,48,128]{2,1,0:T(8,128)(2,1)S(1)}, bf16[60,48,128]{2,1,0:T(8,128)(2,1)S(1)}, u32[]{:S(2)}, u32[]{:S(2)}) collective-permute-start(bf16[60,48,128]{2,1,0:T(8,128)(2,1)S(1)} %get-tuple-element.20.own_ref), channel_id=1, source_target_pairs={{0,8},{8,16},{16,24},{24,32},{32,40},{40,48},{48,56},{56,64},{64,7... | collective-permute-start | bytes 2211848 | tf_op jit(solution)/shard_map/ppermute | solution.py:295
  25.9 0.0 copy-start.2
  25.9 0.0 copy-start.6
  25.9 2.2 %collective-permute-start.3 = (bf16[60,48,128]{2,1,0:T(8,128)(2,1)S(1)}, bf16[60,48,128]{2,1,0:T(8,128)(2,1)S(1)}, u32[]{:S(2)}, u32[]{:S(2)}) collective-permute-start(bf16[60,48,128]{2,1,0:T(8,128)(2,1)S(1)} %get-tuple-element.21), channel_id=1, source_target_pairs={{8,0},{16,8},{24,16},{32,24},{40,32},{48,40},{56,48},{64,56},{72,6... | collective-permute-start | bytes 2211848 | tf_op jit(solution)/shard_map/ppermute | solution.py:300
  28.1 0.0 collective-permute-done.4.left_ref
  28.1 4.5 %collective-permute-done.5.right_ref = bf16[48,48,128]{2,1,0:T(8,128)(2,1)} collective-permute-done((bf16[48,48,128]{2,1,0:T(8,128)(2,1)S(1)}, bf16[48,48,128]{2,1,0:T(8,128)(2,1)}, u32[]{:S(2)}, u32[]{:S(2)}) %collective-permute-start.5) | collective-permute-done | bytes 589856 | tf_op jit(solution)/shard_map/ppermute | solution.py:300
  32.6 2.2 %shard_map.125.own_ref = bf16[48,48,128]{2,1,0:T(8,128)(2,1)S(1)} custom-call(f32[8,256]{1,0:T(8,128)S(1)} %stack.46.taps_ref, bf16[48,48,128]{2,1,0:T(8,128)(2,1)S(1)} %shard_map.122.after_ref.own_ref, bf16[48,48,128]{2,1,0:T(8,128)(2,1)} %collective-permute-done.4.left_ref, bf16[48,48,128]{2,1,0:T(8,128)(2,1)} %collective-permute-done.5.right_ref), custom_call_target="tpu_custom_call" | custom-call | flops 500000000 | bytes 2367488 | tf_op jit(solution)/shard_map/pallas_call | solution.py:24
  34.8 0.0 copy-start.7
  34.8 3.5 %collective-permute-start.6 = (bf16[48,48,128]{2,1,0:T(8,128)(2,1)S(1)}, bf16[48,48,128]{2,1,0:T(8,128)(2,1)S(1)}, u32[]{:S(2)}, u32[]{:S(2)}) collective-permute-start(bf16[48,48,128]{2,1,0:T(8,128)(2,1)S(1)} %shard_map.125.own_ref), channel_id=1, source_target_pairs={{0,1},{1,2},{2,3},{3,4},{4,5},{5,6},{6,7},{8,9},{9,10},{10,11},{11... | collective-permute-start | bytes 1769480 | tf_op jit(solution)/shard_map/ppermute | solution.py:295
  38.4 1.9 %collective-permute-start.7 = (bf16[48,48,128]{2,1,0:T(8,128)(2,1)S(1)}, bf16[48,48,128]{2,1,0:T(8,128)(2,1)S(1)}, u32[]{:S(2)}, u32[]{:S(2)}) collective-permute-start(bf16[48,48,128]{2,1,0:T(8,128)(2,1)S(1)} %shard_map.125.own_ref), channel_id=1, source_target_pairs={{1,0},{2,1},{3,2},{4,3},{5,4},{6,5},{7,6},{9,8},{10,9},{11,10},{12... | collective-permute-start | bytes 1769480 | tf_op jit(solution)/shard_map/ppermute | solution.py:300
  40.3 4.9 %collective-permute-done.6.left_ref = bf16[48,48,128]{2,1,0:T(8,128)(2,1)S(1)} collective-permute-done((bf16[48,48,128]{2,1,0:T(8,128)(2,1)S(1)}, bf16[48,48,128]{2,1,0:T(8,128)(2,1)S(1)}, u32[]{:S(2)}, u32[]{:S(2)}) %collective-permute-start.6) | collective-permute-done | bytes 589856 | tf_op jit(solution)/shard_map/ppermute | solution.py:295
  45.2 4.4 %collective-permute-done.7.right_ref = bf16[48,48,128]{2,1,0:T(8,128)(2,1)S(1)} collective-permute-done((bf16[48,48,128]{2,1,0:T(8,128)(2,1)S(1)}, bf16[48,48,128]{2,1,0:T(8,128)(2,1)S(1)}, u32[]{:S(2)}, u32[]{:S(2)}) %collective-permute-start.7) | collective-permute-done | bytes 589856 | tf_op jit(solution)/shard_map/ppermute | solution.py:300
  49.6 0.0 copy-done.2
  49.6 1.1 shard_map.126.first_ref
  50.6 0.0 collective-permute-done.2.left_ref
  50.6 0.0 collective-permute-done.3.right_ref
  50.7 0.0 copy-start.4
  50.7 0.0 copy-start.5
  50.7 1.8 %shard_map.127 = (f32[48,48,128]{2,1,0:T(8,128)S(1)}, bf16[48,48,128]{2,1,0:T(8,128)(2,1)S(1)}) custom-call(f32[8,256]{1,0:T(8,128)S(1)} %stack.46.taps_ref, bf16[60,48,128]{2,1,0:T(8,128)(2,1)S(1)} %get-tuple-element.20.own_ref, bf16[60,48,128]{2,1,0:T(8,128)(2,1)S(1)} %collective-permute-done.2.left_ref, ...), custom_call_target="tpu_custom_call" | custom-call | flops 1000000000 | bytes 6709248 | tf_op jit(solution)/shard_map/pallas_call | solution.py:24
  52.5 6.1 %collective-permute-start.8 = (bf16[48,48,128]{2,1,0:T(8,128)(2,1)S(1)}, bf16[48,48,128]{2,1,0:T(8,128)(2,1)S(1)}, u32[]{:S(2)}, u32[]{:S(2)}) collective-permute-start(bf16[48,48,128]{2,1,0:T(8,128)(2,1)S(1)} %get-tuple-element.24), channel_id=1, source_target_pairs={{0,128},{128,0},{1,129},{129,1},{2,130},{130,2},{3,131},{131,3},{4... | collective-permute-start | bytes 1769480 | tf_op jit(solution)/shard_map/ppermute | solution.py:360
  58.6 22.0 %collective-permute-done.8.came_ref = bf16[48,48,128]{2,1,0:T(8,128)(2,1)S(1)} collective-permute-done((bf16[48,48,128]{2,1,0:T(8,128)(2,1)S(1)}, bf16[48,48,128]{2,1,0:T(8,128)(2,1)S(1)}, u32[]{:S(2)}, u32[]{:S(2)}) %collective-permute-start.8) | collective-permute-done | bytes 589856 | tf_op jit(solution)/shard_map/ppermute | solution.py:360
  80.6 1.2 shard_map.128
  81.9 1.9 %collective-permute-start.9 = (bf16[3072,128]{1,0:T(8,128)(2,1)S(1)}, bf16[3072,128]{1,0:T(8,128)(2,1)S(1)}, u32[]{:S(2)}, u32[]{:S(2)}) collective-permute-start(bf16[3072,128]{1,0:T(8,128)(2,1)S(1)} %get-tuple-element.25.sent_ref), channel_id=1, source_target_pairs={{0,1},{1,2},{2,3},{3,4},{4,5},{5,6},{6,7},{8,9},{9,10},{10,11},{11... | collective-permute-start | bytes 2359304 | tf_op jit(solution)/shard_map/ppermute | solution.py:295
  83.8 2.5 %collective-permute-start.10 = (bf16[3072,128]{1,0:T(8,128)(2,1)S(1)}, bf16[3072,128]{1,0:T(8,128)(2,1)S(1)}, u32[]{:S(2)}, u32[]{:S(2)}) collective-permute-start(bf16[3072,128]{1,0:T(8,128)(2,1)S(1)} %get-tuple-element.27), channel_id=1, source_target_pairs={{1,0},{2,1},{3,2},{4,3},{5,4},{6,5},{7,6},{9,8},{10,9},{11,10},{12... | collective-permute-start | bytes 2359304 | tf_op jit(solution)/shard_map/ppermute | solution.py:300
  86.2 4.8 %collective-permute-start.13 = (bf16[48,48,128]{2,1,0:T(8,128)(2,1)S(1)}, bf16[48,48,128]{2,1,0:T(8,128)(2,1)S(1)}, u32[]{:S(2)}, u32[]{:S(2)}) collective-permute-start(bf16[48,48,128]{2,1,0:T(8,128)(2,1)S(1)} %get-tuple-element.31.own_ref), channel_id=1, source_target_pairs={{0,8},{8,16},{16,24},{24,32},{32,40},{40,48},{48,56},{56,64},{64,7... | collective-permute-start | bytes 1769480 | tf_op jit(solution)/shard_map/ppermute | solution.py:295
  91.0 1.9 %collective-permute-start.14 = (bf16[48,48,128]{2,1,0:T(8,128)(2,1)S(1)}, bf16[48,48,128]{2,1,0:T(8,128)(2,1)S(1)}, u32[]{:S(2)}, u32[]{:S(2)}) collective-permute-start(bf16[48,48,128]{2,1,0:T(8,128)(2,1)S(1)} %get-tuple-element.31.own_ref), channel_id=1, source_target_pairs={{8,0},{16,8},{24,16},{32,24},{40,32},{48,40},{56,48},{64,56},{72,6... | collective-permute-start | bytes 1769480 | tf_op jit(solution)/shard_map/ppermute | solution.py:300
  93.0 0.0 collective-permute-done.9.left_ref
  93.0 7.3 %collective-permute-done.10.right_ref = bf16[3072,128]{1,0:T(8,128)(2,1)S(1)} collective-permute-done((bf16[3072,128]{1,0:T(8,128)(2,1)S(1)}, bf16[3072,128]{1,0:T(8,128)(2,1)S(1)}, u32[]{:S(2)}, u32[]{:S(2)}) %collective-permute-start.10) | collective-permute-done | bytes 786464 | tf_op jit(solution)/shard_map/ppermute | solution.py:300
  100.3 0.6 shard_map.129
  100.9 2.4 %collective-permute-start.11 = (bf16[60,48,128]{2,1,0:T(8,128)(2,1)S(1)}, bf16[60,48,128]{2,1,0:T(8,128)(2,1)S(1)}, u32[]{:S(2)}, u32[]{:S(2)}) collective-permute-start(bf16[60,48,128]{2,1,0:T(8,128)(2,1)S(1)} %get-tuple-element.28.own_ref), channel_id=1, source_target_pairs={{0,8},{8,16},{16,24},{24,32},{32,40},{40,48},{48,56},{56,64},{64,7... | collective-permute-start | bytes 2211848 | tf_op jit(solution)/shard_map/ppermute | solution.py:295
  103.4 0.0 copy-start.1
  103.4 3.0 %collective-permute-start.12 = (bf16[60,48,128]{2,1,0:T(8,128)(2,1)S(1)}, bf16[60,48,128]{2,1,0:T(8,128)(2,1)S(1)}, u32[]{:S(2)}, u32[]{:S(2)}) collective-permute-start(bf16[60,48,128]{2,1,0:T(8,128)(2,1)S(1)} %get-tuple-element.29), channel_id=1, source_target_pairs={{8,0},{16,8},{24,16},{32,24},{40,32},{48,40},{56,48},{64,56},{72,6... | collective-permute-start | bytes 2211848 | tf_op jit(solution)/shard_map/ppermute | solution.py:300
  106.4 0.0 collective-permute-done.13.left_ref
  106.4 4.1 %collective-permute-done.14.right_ref = bf16[48,48,128]{2,1,0:T(8,128)(2,1)S(1)} collective-permute-done((bf16[48,48,128]{2,1,0:T(8,128)(2,1)S(1)}, bf16[48,48,128]{2,1,0:T(8,128)(2,1)S(1)}, u32[]{:S(2)}, u32[]{:S(2)}) %collective-permute-start.14) | collective-permute-done | bytes 589856 | tf_op jit(solution)/shard_map/ppermute | solution.py:300
  110.5 1.0 shard_map.130.own_ref
  111.4 4.0 %collective-permute-start.15 = (bf16[48,48,128]{2,1,0:T(8,128)(2,1)S(1)}, bf16[48,48,128]{2,1,0:T(8,128)(2,1)S(1)}, u32[]{:S(2)}, u32[]{:S(2)}) collective-permute-start(bf16[48,48,128]{2,1,0:T(8,128)(2,1)S(1)} %shard_map.130.own_ref), channel_id=1, source_target_pairs={{0,1},{1,2},{2,3},{3,4},{4,5},{5,6},{6,7},{8,9},{9,10},{10,11},{11... | collective-permute-start | bytes 1769480 | tf_op jit(solution)/shard_map/ppermute | solution.py:295
  115.5 1.9 %collective-permute-start.16 = (bf16[48,48,128]{2,1,0:T(8,128)(2,1)S(1)}, bf16[48,48,128]{2,1,0:T(8,128)(2,1)S(1)}, u32[]{:S(2)}, u32[]{:S(2)}) collective-permute-start(bf16[48,48,128]{2,1,0:T(8,128)(2,1)S(1)} %shard_map.130.own_ref), channel_id=1, source_target_pairs={{1,0},{2,1},{3,2},{4,3},{5,4},{6,5},{7,6},{9,8},{10,9},{11,10},{12... | collective-permute-start | bytes 1769480 | tf_op jit(solution)/shard_map/ppermute | solution.py:300
  117.4 4.9 %collective-permute-done.15.left_ref = bf16[48,48,128]{2,1,0:T(8,128)(2,1)S(1)} collective-permute-done((bf16[48,48,128]{2,1,0:T(8,128)(2,1)S(1)}, bf16[48,48,128]{2,1,0:T(8,128)(2,1)S(1)}, u32[]{:S(2)}, u32[]{:S(2)}) %collective-permute-start.15) | collective-permute-done | bytes 589856 | tf_op jit(solution)/shard_map/ppermute | solution.py:295
  122.3 4.4 %collective-permute-done.16.right_ref = bf16[48,48,128]{2,1,0:T(8,128)(2,1)S(1)} collective-permute-done((bf16[48,48,128]{2,1,0:T(8,128)(2,1)S(1)}, bf16[48,48,128]{2,1,0:T(8,128)(2,1)S(1)}, u32[]{:S(2)}, u32[]{:S(2)}) %collective-permute-start.16) | collective-permute-done | bytes 589856 | tf_op jit(solution)/shard_map/ppermute | solution.py:300
  126.7 1.3 shard_map.131.begun_ref
  128.0 0.0 collective-permute-done.11.left_ref
  128.0 0.0 collective-permute-done.12.right_ref
  128.0 2.4 %shard_map.132 = (bf16[48,48,64]{2,1,0:T(8,128)(2,1)}, bf16[2,48,48,128]{3,2,1,0:T(8,128)(2,1)}) custom-call(f32[8,256]{1,0:T(8,128)S(1)} %stack.46.taps_ref, bf16[60,48,128]{2,1,0:T(8,128)(2,1)S(1)} %get-tuple-element.28.own_ref, bf16[60,48,128]{2,1,0:T(8,128)(2,1)S(1)} %collective-permute-done.11.left_ref, ...), custom_call_target="tpu_custom_call", output_to_operand_aliasing={{1}: (7, {})} | custom-call | flops 700000000 | bytes 6643712 | tf_op jit(solution)/shard_map/pallas_call | solution.py:24
  (27 shorter events, 0.1 us)
Async XLA Ops:
  0.6 1.3 copy-start
  1.9 1.1 copy-start.3
  3.0 12.4 %copy-start.8 = (bf16[97]{0:T(256)(128)(2,1)S(1)}, bf16[97]{0:T(256)(128)(2,1)}, u32[]{:S(2)}) copy-start(bf16[97]{0:T(256)(128)(2,1)} %param.18) | copy-start | bytes 586
  3.0 12.5 %copy-start.9 = (bf16[97]{0:T(256)(128)(2,1)S(1)}, bf16[97]{0:T(256)(128)(2,1)}, u32[]{:S(2)}) copy-start(bf16[97]{0:T(256)(128)(2,1)} %param.19) | copy-start | bytes 586
  3.0 12.6 %copy-start.10 = (bf16[49]{0:T(256)(128)(2,1)S(1)}, bf16[49]{0:T(256)(128)(2,1)}, u32[]{:S(2)}) copy-start(bf16[49]{0:T(256)(128)(2,1)} %param.16) | copy-start | bytes 298
  3.0 12.7 %copy-start.11 = (bf16[49]{0:T(256)(128)(2,1)S(1)}, bf16[49]{0:T(256)(128)(2,1)}, u32[]{:S(2)}) copy-start(bf16[49]{0:T(256)(128)(2,1)} %param.17) | copy-start | bytes 298
  4.4 12.6 %collective-permute-start = (bf16[3072,128]{1,0:T(8,128)(2,1)S(1)}, bf16[3072,128]{1,0:T(8,128)(2,1)S(1)}, u32[]{:S(2)}, u32[]{:S(2)}) collective-permute-start(bf16[3072,128]{1,0:T(8,128)(2,1)S(1)} %get-tuple-element.17.sent_ref), channel_id=1, source_target_pairs={{0,1},{1,2},{2,3},{3,4},{4,5},{5,6},{6,7},{8,9},{9,10},{10,11},{11... | collective-permute-start | bytes 2359304 | tf_op jit(solution)/shard_map/ppermute | solution.py:295
  8.1 13.9 %collective-permute-start.1 = (bf16[3072,128]{1,0:T(8,128)(2,1)}, bf16[3072,128]{1,0:T(8,128)(2,1)S(1)}, u32[]{:S(2)}, u32[]{:S(2)}) collective-permute-start(bf16[3072,128]{1,0:T(8,128)(2,1)} %get-tuple-element.19), channel_id=1, source_target_pairs={{1,0},{2,1},{3,2},{4,3},{5,4},{6,5},{7,6},{9,8},{10,9},{11,10},{12... | collective-permute-start | bytes 2359304 | tf_op jit(solution)/shard_map/ppermute | solution.py:300
  10.1 18.1 %collective-permute-start.4 = (bf16[48,48,128]{2,1,0:T(8,128)(2,1)S(1)}, bf16[48,48,128]{2,1,0:T(8,128)(2,1)}, u32[]{:S(2)}, u32[]{:S(2)}) collective-permute-start(bf16[48,48,128]{2,1,0:T(8,128)(2,1)S(1)} %shard_map.122.after_ref.own_ref), channel_id=1, source_target_pairs={{0,8},{8,16},{16,24},{24,32},{32,40},{40,48},{48,56},{56,64},{64,7... | collective-permute-start | bytes 1769480 | tf_op jit(solution)/shard_map/ppermute | solution.py:295
  13.3 19.4 %collective-permute-start.5 = (bf16[48,48,128]{2,1,0:T(8,128)(2,1)S(1)}, bf16[48,48,128]{2,1,0:T(8,128)(2,1)}, u32[]{:S(2)}, u32[]{:S(2)}) collective-permute-start(bf16[48,48,128]{2,1,0:T(8,128)(2,1)S(1)} %shard_map.122.after_ref.own_ref), channel_id=1, source_target_pairs={{8,0},{16,8},{24,16},{32,24},{40,32},{48,40},{56,48},{64,56},{72,6... | collective-permute-start | bytes 1769480 | tf_op jit(solution)/shard_map/ppermute | solution.py:300
  22.7 28.0 %collective-permute-start.2 = (bf16[60,48,128]{2,1,0:T(8,128)(2,1)S(1)}, bf16[60,48,128]{2,1,0:T(8,128)(2,1)S(1)}, u32[]{:S(2)}, u32[]{:S(2)}) collective-permute-start(bf16[60,48,128]{2,1,0:T(8,128)(2,1)S(1)} %get-tuple-element.20.own_ref), channel_id=1, source_target_pairs={{0,8},{8,16},{16,24},{24,32},{32,40},{40,48},{48,56},{56,64},{64,7... | collective-permute-start | bytes 2211848 | tf_op jit(solution)/shard_map/ppermute | solution.py:295
  25.9 23.7 %copy-start.2 = (bf16[2,48,48,128]{3,2,1,0:T(8,128)(2,1)S(1)}, bf16[2,48,48,128]{3,2,1,0:T(8,128)(2,1)}, u32[]{:S(2)}) copy-start(bf16[2,48,48,128]{3,2,1,0:T(8,128)(2,1)} %pert_ref.5) | copy-start | bytes 3538948
  25.9 23.6 %copy-start.6 = (bf16[128,128]{1,0:T(8,128)(2,1)S(1)}, bf16[128,128]{1,0:T(8,128)(2,1)}, u32[]{:S(2)}) copy-start(bf16[128,128]{1,0:T(8,128)(2,1)} %vert_ref.5) | copy-start | bytes 98308
  25.9 24.7 %collective-permute-start.3 = (bf16[60,48,128]{2,1,0:T(8,128)(2,1)S(1)}, bf16[60,48,128]{2,1,0:T(8,128)(2,1)S(1)}, u32[]{:S(2)}, u32[]{:S(2)}) collective-permute-start(bf16[60,48,128]{2,1,0:T(8,128)(2,1)S(1)} %get-tuple-element.21), channel_id=1, source_target_pairs={{8,0},{16,8},{24,16},{32,24},{40,32},{48,40},{56,48},{64,56},{72,6... | collective-permute-start | bytes 2211848 | tf_op jit(solution)/shard_map/ppermute | solution.py:300
  34.8 15.8 %copy-start.7 = (bf16[128,128]{1,0:T(8,128)(2,1)S(1)}, bf16[128,128]{1,0:T(8,128)(2,1)}, u32[]{:S(2)}) copy-start(bf16[128,128]{1,0:T(8,128)(2,1)} %static_ref.5) | copy-start | bytes 98308
  34.8 10.3 %collective-permute-start.6 = (bf16[48,48,128]{2,1,0:T(8,128)(2,1)S(1)}, bf16[48,48,128]{2,1,0:T(8,128)(2,1)S(1)}, u32[]{:S(2)}, u32[]{:S(2)}) collective-permute-start(bf16[48,48,128]{2,1,0:T(8,128)(2,1)S(1)} %shard_map.125.own_ref), channel_id=1, source_target_pairs={{0,1},{1,2},{2,3},{3,4},{4,5},{5,6},{6,7},{8,9},{9,10},{10,11},{11... | collective-permute-start | bytes 1769480 | tf_op jit(solution)/shard_map/ppermute | solution.py:295
  38.4 11.2 %collective-permute-start.7 = (bf16[48,48,128]{2,1,0:T(8,128)(2,1)S(1)}, bf16[48,48,128]{2,1,0:T(8,128)(2,1)S(1)}, u32[]{:S(2)}, u32[]{:S(2)}) collective-permute-start(bf16[48,48,128]{2,1,0:T(8,128)(2,1)S(1)} %shard_map.125.own_ref), channel_id=1, source_target_pairs={{1,0},{2,1},{3,2},{4,3},{5,4},{6,5},{7,6},{9,8},{10,9},{11,10},{12... | collective-permute-start | bytes 1769480 | tf_op jit(solution)/shard_map/ppermute | solution.py:300
  50.7 29.9 %copy-start.4 = (bf16[48,48,128]{2,1,0:T(8,128)(2,1)S(1)}, bf16[48,48,128]{2,1,0:T(8,128)(2,1)}, u32[]{:S(2)}) copy-start(bf16[48,48,128]{2,1,0:T(8,128)(2,1)} %dep_ref.1) | copy-start | bytes 1769476
  50.7 29.9 %copy-start.5 = (bf16[48,48,128]{2,1,0:T(8,128)(2,1)S(1)}, bf16[48,48,128]{2,1,0:T(8,128)(2,1)}, u32[]{:S(2)}) copy-start(bf16[48,48,128]{2,1,0:T(8,128)(2,1)} %weight_ref.1) | copy-start | bytes 1769476
  52.5 28.1 %collective-permute-start.8 = (bf16[48,48,128]{2,1,0:T(8,128)(2,1)S(1)}, bf16[48,48,128]{2,1,0:T(8,128)(2,1)S(1)}, u32[]{:S(2)}, u32[]{:S(2)}) collective-permute-start(bf16[48,48,128]{2,1,0:T(8,128)(2,1)S(1)} %get-tuple-element.24), channel_id=1, source_target_pairs={{0,128},{128,0},{1,129},{129,1},{2,130},{130,2},{3,131},{131,3},{4... | collective-permute-start | bytes 1769480 | tf_op jit(solution)/shard_map/ppermute | solution.py:360
  81.9 11.1 %collective-permute-start.9 = (bf16[3072,128]{1,0:T(8,128)(2,1)S(1)}, bf16[3072,128]{1,0:T(8,128)(2,1)S(1)}, u32[]{:S(2)}, u32[]{:S(2)}) collective-permute-start(bf16[3072,128]{1,0:T(8,128)(2,1)S(1)} %get-tuple-element.25.sent_ref), channel_id=1, source_target_pairs={{0,1},{1,2},{2,3},{3,4},{4,5},{5,6},{6,7},{8,9},{9,10},{10,11},{11... | collective-permute-start | bytes 2359304 | tf_op jit(solution)/shard_map/ppermute | solution.py:295
  83.8 16.5 %collective-permute-start.10 = (bf16[3072,128]{1,0:T(8,128)(2,1)S(1)}, bf16[3072,128]{1,0:T(8,128)(2,1)S(1)}, u32[]{:S(2)}, u32[]{:S(2)}) collective-permute-start(bf16[3072,128]{1,0:T(8,128)(2,1)S(1)} %get-tuple-element.27), channel_id=1, source_target_pairs={{1,0},{2,1},{3,2},{4,3},{5,4},{6,5},{7,6},{9,8},{10,9},{11,10},{12... | collective-permute-start | bytes 2359304 | tf_op jit(solution)/shard_map/ppermute | solution.py:300
  86.2 20.1 %collective-permute-start.13 = (bf16[48,48,128]{2,1,0:T(8,128)(2,1)S(1)}, bf16[48,48,128]{2,1,0:T(8,128)(2,1)S(1)}, u32[]{:S(2)}, u32[]{:S(2)}) collective-permute-start(bf16[48,48,128]{2,1,0:T(8,128)(2,1)S(1)} %get-tuple-element.31.own_ref), channel_id=1, source_target_pairs={{0,8},{8,16},{16,24},{24,32},{32,40},{40,48},{48,56},{56,64},{64,7... | collective-permute-start | bytes 1769480 | tf_op jit(solution)/shard_map/ppermute | solution.py:295
  91.0 19.4 %collective-permute-start.14 = (bf16[48,48,128]{2,1,0:T(8,128)(2,1)S(1)}, bf16[48,48,128]{2,1,0:T(8,128)(2,1)S(1)}, u32[]{:S(2)}, u32[]{:S(2)}) collective-permute-start(bf16[48,48,128]{2,1,0:T(8,128)(2,1)S(1)} %get-tuple-element.31.own_ref), channel_id=1, source_target_pairs={{8,0},{16,8},{24,16},{32,24},{40,32},{48,40},{56,48},{64,56},{72,6... | collective-permute-start | bytes 1769480 | tf_op jit(solution)/shard_map/ppermute | solution.py:300
  100.9 27.1 %collective-permute-start.11 = (bf16[60,48,128]{2,1,0:T(8,128)(2,1)S(1)}, bf16[60,48,128]{2,1,0:T(8,128)(2,1)S(1)}, u32[]{:S(2)}, u32[]{:S(2)}) collective-permute-start(bf16[60,48,128]{2,1,0:T(8,128)(2,1)S(1)} %get-tuple-element.28.own_ref), channel_id=1, source_target_pairs={{0,8},{8,16},{16,24},{24,32},{32,40},{40,48},{48,56},{56,64},{64,7... | collective-permute-start | bytes 2211848 | tf_op jit(solution)/shard_map/ppermute | solution.py:295
  103.4 23.3 %copy-start.1 = (bf16[2,48,48,128]{3,2,1,0:T(8,128)(2,1)S(1)}, bf16[2,48,48,128]{3,2,1,0:T(8,128)(2,1)}, u32[]{:S(2)}) copy-start(bf16[2,48,48,128]{3,2,1,0:T(8,128)(2,1)} %member_ref.7) | copy-start | bytes 3538948
  103.4 24.6 %collective-permute-start.12 = (bf16[60,48,128]{2,1,0:T(8,128)(2,1)S(1)}, bf16[60,48,128]{2,1,0:T(8,128)(2,1)S(1)}, u32[]{:S(2)}, u32[]{:S(2)}) collective-permute-start(bf16[60,48,128]{2,1,0:T(8,128)(2,1)S(1)} %get-tuple-element.29), channel_id=1, source_target_pairs={{8,0},{16,8},{24,16},{32,24},{40,32},{48,40},{56,48},{64,56},{72,6... | collective-permute-start | bytes 2211848 | tf_op jit(solution)/shard_map/ppermute | solution.py:300
  111.4 10.9 %collective-permute-start.15 = (bf16[48,48,128]{2,1,0:T(8,128)(2,1)S(1)}, bf16[48,48,128]{2,1,0:T(8,128)(2,1)S(1)}, u32[]{:S(2)}, u32[]{:S(2)}) collective-permute-start(bf16[48,48,128]{2,1,0:T(8,128)(2,1)S(1)} %shard_map.130.own_ref), channel_id=1, source_target_pairs={{0,1},{1,2},{2,3},{3,4},{4,5},{5,6},{6,7},{8,9},{9,10},{10,11},{11... | collective-permute-start | bytes 1769480 | tf_op jit(solution)/shard_map/ppermute | solution.py:295
  115.5 11.2 %collective-permute-start.16 = (bf16[48,48,128]{2,1,0:T(8,128)(2,1)S(1)}, bf16[48,48,128]{2,1,0:T(8,128)(2,1)S(1)}, u32[]{:S(2)}, u32[]{:S(2)}) collective-permute-start(bf16[48,48,128]{2,1,0:T(8,128)(2,1)S(1)} %shard_map.130.own_ref), channel_id=1, source_target_pairs={{1,0},{2,1},{3,2},{4,3},{5,4},{6,5},{7,6},{9,8},{10,9},{11,10},{12... | collective-permute-start | bytes 1769480 | tf_op jit(solution)/shard_map/ppermute | solution.py:300
where the time goes:
time: 131 us; the launch traced here: 130 us
  waiting for transfers between devices  62.4 us (48%)
  starting transfers between devices  50.3 us (38%)
  Pallas kernels  14.4 us (11%)
  local copies, waits for them, and re-layouts  2.24 us (2%)
    ppermute x8, waiting for transfers between devices, from_right(): return lax.ppermute(field, axis, [(i + 1, i) for i in range(size - 1)])  29.7 us
    ppermute x8, starting transfers between devices, from_left(): return lax.ppermute(field, axis, [(i, i + 1) for i in range(size - 1)])  26.8 us
    ppermute x1, waiting for transfers between devices, body(): came = lax.ppermute(sent, 'mem', [(i, size - 1 - i) for i in range(size)])  22 us
    ppermute x8, starting transfers between devices, from_right(): return lax.ppermute(field, axis, [(i + 1, i) for i in range(size - 1)])  17.4 us
    pallas_call x11, Pallas kernels, call(): pl.pallas_call(kernel, out_shape=outs, in_specs=[ANY if i in in_any else...  14.4 us
    ppermute x8, waiting for transfers between devices, from_left(): return lax.ppermute(field, axis, [(i, i + 1) for i in range(size - 1)])  10.7 us
    ppermute x1, starting transfers between devices, body(): came = lax.ppermute(sent, 'mem', [(i, size - 1 - i) for i in range(size)])  6.09 us
  transfers between devices with their start and end apart: 17, of which 10 were waited for; matrix products, arithmetic and copies ran while one was open for 0% of the time, Pallas kernels for 5%

commit v1 on v0

--- a/solution.py
+++ b/solution.py
@@ -42,6 +42,34 @@
     return pltpu.roll(spread, 0, 1, stride=1, stride_axis=0)[:, :cols].astype(BF)
 
 
+def place(axis):
+    at = lax.axis_index(axis)
+    return at % 2 == 1, (at == 0) | (at == lax.axis_size(axis) - 1)
+
+
+def band_swapped(row, axis):
+    spread = jnp.broadcast_to(row, (TILE, row.shape[1]))
+    plain = pltpu.roll(spread, 0, 1, stride=1, stride_axis=0)
+    right = pltpu.roll(spread, row.shape[1] - 96, 1, stride=1, stride_axis=0)
+    left = pltpu.roll(spread, 96, 1, stride=1, stride_axis=0)
+    lane = lax.broadcasted_iota(jnp.int32, plain.shape, 1)
+    odd, end = place(axis)
+    turned = jnp.where(lane < 48, right, jnp.where(lane < 96, plain, left))
+    both = jnp.where(jnp.full(plain.shape, odd.astype(jnp.int32)) == 1, plain, turned)
+    keep = (lane < 96) | (jnp.full(plain.shape, end.astype(jnp.int32)) == 0)
+    return jnp.where(keep, both, 0.0)[:, :144].astype(BF)
+
+
+def pick(odd, a, b):
+    return jnp.where(odd, a, b)
+
+
+def sides(even, odd_swap, axis):
+    odd, end = place(axis)
+    outer = pick(end, jnp.zeros_like(odd_swap), odd_swap)
+    return pick(odd, even, outer), pick(odd, outer, even)
+
+
 def halves(a):
     return jnp.concatenate([a[: a.shape[0] // 2], a[a.shape[0] // 2 :]], axis=-1)
 
@@ -86,9 +114,12 @@
     return jnp.concatenate([first, own, last], axis=0)
 
 
-def pack_slabs(packed, right_ref, left_ref):
-    right_ref[2304:] = packed[:, 16:48].reshape(768, 128)
-    left_ref[2304:] = packed[:, :SLAB].reshape(768, 128)
+def pack_slabs(packed, even_ref, odd_ref):
+    right = packed[:, 16:48].reshape(768, 128)
+    left = packed[:, :SLAB].reshape(768, 128)
+    odd, _ = place("ty")
+    even_ref[2304:] = pick(odd, left, right)
+    odd_ref[2304:] = pick(odd, right, left)
 
 
 def take_kernel(member_ref, out_ref, sems):
@@ -102,7 +133,7 @@
         copy.wait()
 
 
-def pack_kernel(static_ref, member_ref, after_ref, right_ref, left_ref, own_ref, static, second, sems):
+def pack_kernel(static_ref, member_ref, after_ref, even_ref, odd_ref, own_ref, static, second, sems):
     copies = [
         pltpu.make_async_copy(member_ref.at[1, pl.ds(24 * i, 24)], second.at[pl.ds(24 * i, 24)], sems.at[i])
         for i in range(2)
@@ -116,64 +147,69 @@
     for copy in copies:
         copy.wait()
     member = second[...].reshape(2304, 128)
-    right_ref[:2304] = member
-    left_ref[:2304] = member
+    even_ref[:2304] = member
+    odd_ref[:2304] = member
     packed = halves(static[...])
     own_ref[...] = packed
-    pack_slabs(packed, right_ref, left_ref)
-
-
-def first_y_kernel(row_m, row_s, taps_ref, sent_ref, own_ref, left_ref, right_ref, to_r_ref, to_l_ref, out_ref):
-    member = band(taps_ref[row_m : row_m + 1], TILE, 144)
+    pack_slabs(packed, even_ref, odd_ref)
+
+
+def first_y_kernel(row_m, row_s, taps_ref, sent_ref, own_ref, even_ref, odd_ref, to_even_ref, to_odd_ref, out_ref):
+    member = band_swapped(taps_ref[row_m : row_m + 1], "ty")
     static = band(taps_ref[row_s : row_s + 1], TILE, 112)
 
     def member_line(x):
         at = pl.ds(pl.multiple_of(x * TILE, TILE), TILE)
-        return jnp.concatenate([left_ref[at], sent_ref[at], right_ref[at]], axis=0)
+        return jnp.concatenate([even_ref[at], sent_ref[at], odd_ref[at]], axis=0)
 
     def member_store(x, out):
         out = out.astype(BF)
-        to_r_ref[x] = out
-        to_l_ref[x] = out
+        to_even_ref[x] = out
+        to_odd_ref[x] = out
 
     along_y(member, member_line, TILE, member_store)
 
     def static_line(x):
         at = pl.ds(pl.multiple_of(2304 + x * SLAB, SLAB), SLAB)
-        return jnp.concatenate([left_ref[at], own_ref[x], right_ref[at]], axis=0)
+        left, right = sides(even_ref[at], odd_ref[at], "ty")
+        return jnp.concatenate([left, own_ref[x], right], axis=0)
 
     def static_store(x, out):
         out_ref[x] = out.astype(BF)
 
     along_y(static, static_line, 24, static_store)
     packed = out_ref[...]
-    to_r_ref[TILE:] = halves(packed[..., 64:])
-    to_l_ref[TILE:] = halves(packed[..., :64])
-
-
-def first_x_kernel(row, taps_ref, own_ref, left_ref, right_ref, out_ref):
-    matrix = band(taps_ref[row : row + 1], TILE, 144)
+    right = halves(packed[..., 64:])
+    left = halves(packed[..., :64])
+    odd, _ = place("tx")
+    to_even_ref[TILE:] = pick(odd, left, right)
+    to_odd_ref[TILE:] = pick(odd, right, left)
+
+
+def first_x_kernel(row, taps_ref, own_ref, even_ref, odd_ref, out_ref):
+    matrix = band_swapped(taps_ref[row : row + 1], "tx")
     for c in range(0, TILE, 16):
         at = slice(c, c + 16)
-        out_ref[:, at] = along_x(matrix, [left_ref[:, at], own_ref[:, at], right_ref[:, at]])
-
-
-def second_y(row, taps_ref, own_ref, left_ref, right_ref, store):
-    matrix = band(taps_ref[row : row + 1], TILE, 144)
+        out_ref[:, at] = along_x(matrix, [even_ref[:, at], own_ref[:, at], odd_ref[:, at]])
+
+
+def second_y(row, taps_ref, own_ref, even_ref, odd_ref, store):
+    matrix = band_swapped(taps_ref[row : row + 1], "ty")
 
     def line(x):
-        return jnp.concatenate([left_ref[x], own_ref[x], right_ref[x]], axis=0)
+        return jnp.concatenate([even_ref[x], own_ref[x], odd_ref[x]], axis=0)
 
     along_y(matrix, line, TILE, store)
 
 
-def second_x(rows, taps_ref, own_ref, left_ref, right_ref, s_ref, block):
-    matrix = band(taps_ref[rows[0] : rows[0] + 1], TILE, 144)
+def second_x(rows, taps_ref, own_ref, even_ref, odd_ref, s_ref, block):
+    matrix = band_swapped(taps_ref[rows[0] : rows[0] + 1], "tx")
     matrix_s = band(taps_ref[rows[1] : rows[1] + 1], 24, 72)
     for c in range(0, TILE, 16):
         at = slice(c, c + 16)
-        b = along_x(matrix, [left_ref[:TILE, at], own_ref[:TILE, at], right_ref[:TILE, at]])
-        lines = static_parts(left_ref[TILE:, at], s_ref[:, at], right_ref[TILE:, at])
+        b = along_x(matrix, [even_ref[:TILE, at], own_ref[:TILE, at], odd_ref[:TILE, at]])
+        left, right = sides(even_ref[TILE:, at], odd_ref[TILE:, at], "tx")
+        lines = static_parts(left, s_ref[:, at], right)
         block(at, b, along_x(matrix_s, [lines]))
 
 
@@ -188,11 +224,11 @@
     return lax.dot_general(a, b, (((1,), (1,)), ((), ())), preferred_element_type=F32)
 
 
-def forward_a_kernel(row, taps_ref, own_ref, left_ref, right_ref, pert_ref, vert_ref, out_ref, filtered):
+def forward_a_kernel(row, taps_ref, own_ref, even_ref, odd_ref, pert_ref, vert_ref, out_ref, filtered):
     def store(x, out):
         filtered[x] = out.astype(BF)
 
-    second_y(row, taps_ref, own_ref, left_ref, right_ref, store)
+    second_y(row, taps_ref, own_ref, even_ref, odd_ref, store)
     vert = vert_ref[...]
 
     def step(i, carry):
@@ -205,7 +241,7 @@
 
 
 def forward_b_kernel(
-    rows, taps_ref, own_ref, left_ref, right_ref, s_ref, first_ref, pert_ref, vert_ref, static_ref,
+    rows, taps_ref, own_ref, even_ref, odd_ref, s_ref, first_ref, pert_ref, vert_ref, static_ref,
     kept_ref, sent_ref
 ):
     vert = vert_ref[...]
@@ -219,12 +255,12 @@
         kept_ref[:, at] = total
         sent_ref[:, at] = total.astype(BF)
 
-    second_x(rows, taps_ref, own_ref, left_ref, right_ref, s_ref, block)
+    second_x(rows, taps_ref, own_ref, even_ref, odd_ref, s_ref, block)
 
 
 def residual_kernel(
     kept_ref, came_ref, dep_ref, weight_ref, pert_ref, vert_ref, static_ref,
-    a_ref, right_ref, left_ref, own_ref
+    a_ref, even_ref, odd_ref, own_ref
 ):
     vert = vert_ref[...]
     static_mat = static_block(static_ref)
@@ -242,21 +278,21 @@
             a_ref[at] = dot(first, vert).astype(BF).reshape(4, TILE, 128)
             back = dot(second, vert).astype(BF)
             cells = pl.ds(pl.multiple_of(x * TILE, 192), 192)
-            right_ref[cells] = back
-            left_ref[cells] = back
+            even_ref[cells] = back
+            odd_ref[cells] = back
         static = dot(jnp.concatenate(res, axis=1), static_mat).astype(BF)
         own_ref[pl.ds(4 * i, 4)] = static.reshape(4, TILE, 128)
         return carry
 
     lax.fori_loop(0, 6, step, 0, unroll=2)
-    pack_slabs(own_ref[...], right_ref, left_ref)
-
-
-def last_a_kernel(row, taps_ref, own_ref, left_ref, right_ref, member_ref, out_ref, out, sems):
+    pack_slabs(own_ref[...], even_ref, odd_ref)
+
+
+def last_a_kernel(row, taps_ref, own_ref, even_ref, odd_ref, member_ref, out_ref, out, sems):
     def store(x, filtered):
         out[x] = (member_ref[0, x].astype(F32) + filtered.astype(BF).astype(F32)).astype(BF)
 
-    second_y(row, taps_ref, own_ref, left_ref, right_ref, store)
+    second_y(row, taps_ref, own_ref, even_ref, odd_ref, store)
     copies = [
         pltpu.make_async_copy(out.at[pl.ds(12 * i, 12)], out_ref.at[0, pl.ds(12 * i, 12)], sems.at[i])
         for i in range(4)
@@ -268,7 +304,7 @@
 
 
 def last_b_kernel(
-    rows, taps_ref, own_ref, left_ref, right_ref, s_ref, member_ref, control_ref, begun_ref,
+    rows, taps_ref, own_ref, even_ref, odd_ref, s_ref, member_ref, control_ref, begun_ref,
     static_out, member_out, static, member, sems
 ):
     copies = []
@@ -285,35 +321,43 @@
             copy.start()
             copies.append(copy)
 
-    second_x(rows, taps_ref, own_ref, left_ref, right_ref, s_ref, block)
+    second_x(rows, taps_ref, own_ref, even_ref, odd_ref, s_ref, block)
     for copy in copies:
         copy.wait()
 
 
-def from_left(field, axis):
-    size = lax.axis_size(axis)
-    return lax.ppermute(field, axis, [(i, i + 1) for i in range(size - 1)])
-
-
-def from_right(field, axis):
-    size = lax.axis_size(axis)
-    return lax.ppermute(field, axis, [(i + 1, i) for i in range(size - 1)])
-
-
-def first_filters(taps, back, a, to_r, to_l, own):
-    a_halo = (from_left(a, "tx"), from_right(a, "tx"))
-    b_halo = (from_left(to_r, "ty"), from_right(to_l, "ty"))
+def swaps_y(even, odd):
+    n = lax.axis_size("ty")
+    first = [(i, i ^ 1) for i in range(n)]
+    second = [(i, (i + 1) % n if i % 2 else (i - 1) % n) for i in range(n)]
+    return lax.ppermute(even, "ty", first), lax.ppermute(odd, "ty", second)
+
+
+def swaps_x(even, odd):
+    n, m = lax.axis_size("tx"), lax.axis_size("ty")
+    first = [(i, i ^ 1) for i in range(n)]
+    second = []
+    for i in range(n):
+        other = i + 1 if i % 2 else i - 1
+        for j in range(m):
+            second.append((i * m + j, i * m + (j ^ 1) if i in (0, n - 1) else other * m + j))
+    return lax.ppermute(even, "tx", first), lax.ppermute(odd, ("tx", "ty"), second)
+
+
+def first_filters(taps, back, a, to_even, to_odd, own):
+    a_halo = swaps_x(a, a)
+    b_halo = swaps_y(to_even, to_odd)
     tile = (TILE, TILE, 128)
-    b_to_r, b_to_l, s = call(
+    b_to_even, b_to_odd, s = call(
         functools.partial(first_y_kernel, 1 + back, 3 + back),
         (shape(60, TILE, 128), shape(60, TILE, 128), shape(24, TILE, 128)),
-        (taps, to_r, own) + b_halo,
+        (taps, to_even, own) + b_halo,
         700_000_000,
     )
-    b_halo = (from_left(b_to_r, "tx"), from_right(b_to_l, "tx"))
+    b_halo = swaps_x(b_to_even, b_to_odd)
     (a,) = call(functools.partial(first_x_kernel, back), (shape(*tile),), (taps, a) + a_halo, 500_000_000)
-    a_halo = (from_left(a, "ty"), from_right(a, "ty"))
-    return (a,) + a_halo, (b_to_r,) + b_halo + (s,)
+    a_halo = swaps_y(a, a)
+    return (a,) + a_halo, (b_to_even,) + b_halo + (s,)
 
 
 def body(
@@ -342,12 +386,12 @@
         take_kernel, (shape(*tile),), (member_control,), 1_000_000,
         [pltpu.SemaphoreType.DMA((4,))], in_any=(0,),
     )
-    to_r, to_l, control = call(
+    to_even, to_odd, control = call(
         pack_kernel, sent_shapes, (static_control, member_control, a), 1_000_000,
         [pltpu.VMEM((TILE, TILE, 64), BF), pltpu.VMEM(tile, BF), pltpu.SemaphoreType.DMA((4,))],
         in_any=(0, 1, 2),
     )
-    a, b = first_filters(taps, 0, a, to_r, to_l, control)
+    a, b = first_filters(taps, 0, a, to_even, to_odd, control)
     (first,) = call(
         functools.partial(forward_a_kernel, 1), (shape(*tile, dtype=F32),),
         (taps,) + a + (perturbations, local_vertical), 800_000_000, [pltpu.VMEM(tile, BF)],
@@ -358,11 +402,11 @@
     )
     size = lax.axis_size("mem")
     came = lax.ppermute(sent, "mem", [(i, size - 1 - i) for i in range(size)])
-    a, to_r, to_l, own = call(
+    a, to_even, to_odd, own = call(
         residual_kernel, (shape(*tile),) + sent_shapes,
         (kept, came, departures, obs_weight, perturbations, local_vertical, static_vertical), 400_000_000,
     )
-    a, b = first_filters(taps, 4, a, to_r, to_l, own)
+    a, b = first_filters(taps, 4, a, to_even, to_odd, own)
     (begun,) = call(
         functools.partial(last_a_kernel, 5), (shape(2, *tile),), (taps,) + a + (member_control,), 500_000_000,
         [pltpu.VMEM(tile, BF), pltpu.SemaphoreType.DMA((4,))], out_any=(0,),

time: 131 us -> 114 us (0.87)
  the two profiles are of different devices: /device:TPU:25 before, /device:TPU:32 now
where the time goes in v1:
time: 114 us
  waiting for transfers between devices  73.2 us (64%)
  starting transfers between devices  22.8 us (20%)
  Pallas kernels  14.5 us (13%)
  local copies, waits for them, and re-layouts  2.23 us (2%)
    ppermute x8, waiting for transfers between devices, swaps_y(): return (lax.ppermute(even, 'ty', first), lax.ppermute(odd, 'ty', second))  34.9 us
    ppermute x1, waiting for transfers between devices, body(): came = lax.ppermute(sent, 'mem', [(i, size - 1 - i) for i in range(size)])  25.3 us
    pallas_call x11, Pallas kernels, call(): pl.pallas_call(kernel, out_shape=outs, in_specs=[ANY if i in in_any else...  14.5 us
    ppermute x4, waiting for transfers between devices, swaps_x(): lax.ppermute(odd, ('tx', 'ty'), second)  7.52 us
    ppermute x8, starting transfers between devices, swaps_y(): return (lax.ppermute(even, 'ty', first), lax.ppermute(odd, 'ty', second))  7.11 us
    ppermute x1, starting transfers between devices, body(): came = lax.ppermute(sent, 'mem', [(i, size - 1 - i) for i in range(size)])  6.38 us
    ppermute x4, starting transfers between devices, swaps_x(): lax.ppermute(odd, ('tx', 'ty'), second)  5.94 us
    ppermute x4, waiting for transfers between devices, swaps_x(): lax.ppermute(even, 'tx', first)  5.57 us
  transfers between devices with their start and end apart: 17, of which 13 were waited for; matrix products, arithmetic and copies ran while one was open for 1% of the time, Pallas kernels for 6%

profile of v1, /device:TPU:32, one launch (start us, length us, event | category | flops | bytes accessed | tf_op | source)
XLA Modules:
  0.0 113.8 jit_solution(14641619108389973811)
XLA Ops:
  0.6 0.0 copy-start
  0.6 1.3 %copy-done = bf16[2,48,48,128]{3,2,1,0:T(8,128)(2,1)S(1)} copy-done((bf16[2,48,48,128]{3,2,1,0:T(8,128)(2,1)S(1)}, bf16[2,48,48,128]{3,2,1,0:T(8,128)(2,1)}, u32[]{:S(2)}) %copy-start) | copy-done | bytes 1179672
  1.9 0.8 shard_map.122.after_ref.own_ref
  2.7 0.3 copy-done.3
  3.0 1.5 %shard_map.123 = (bf16[3072,128]{1,0:T(8,128)(2,1)S(1)}, bf16[3072,128]{1,0:T(8,128)(2,1)}, bf16[24,48,128]{2,1,0:T(8,128)(2,1)S(1)}) custom-call(bf16[48,48,64]{2,1,0:T(8,128)(2,1)S(1)} %copy-done.3, bf16[2,48,48,128]{3,2,1,0:T(8,128)(2,1)S(1)} %copy-done, bf16[48,48,128]{2,1,0:T(8,128)(2,1)S(1)} %shard_map.122.after_ref.own_ref), custom_call_target="tpu_custom_call" | custom-call | flops 1000000 | bytes 3932160 | tf_op jit(solution)/shard_map/pallas_call | solution.py:24
  4.5 0.1 collective-permute-start
  4.6 2.9 %collective-permute-start.1 = (bf16[3072,128]{1,0:T(8,128)(2,1)}, bf16[3072,128]{1,0:T(8,128)(2,1)S(1)}, u32[]{:S(2)}, u32[]{:S(2)}) collective-permute-start(bf16[3072,128]{1,0:T(8,128)(2,1)} %get-tuple-element.19), channel_id=1, source_target_pairs={{0,7},{1,2},{2,1},{3,4},{4,3},{5,6},{6,5},{7,0},{8,15},{9,10},{10,... | collective-permute-start | bytes 2359304 | tf_op jit(solution)/shard_map/ppermute | solution.py:333
  7.4 1.6 %collective-permute-start.4 = (bf16[48,48,128]{2,1,0:T(8,128)(2,1)S(1)}, bf16[48,48,128]{2,1,0:T(8,128)(2,1)}, u32[]{:S(2)}, u32[]{:S(2)}) collective-permute-start(bf16[48,48,128]{2,1,0:T(8,128)(2,1)S(1)} %shard_map.122.after_ref.own_ref), channel_id=1, source_target_pairs={{0,8},{8,0},{16,24},{24,16},{32,40},{40,32},{48,56},{56,48},{64,72... | collective-permute-start | bytes 1769480 | tf_op jit(solution)/shard_map/ppermute | solution.py:344
  9.0 1.7 %collective-permute-start.5 = (bf16[48,48,128]{2,1,0:T(8,128)(2,1)S(1)}, bf16[48,48,128]{2,1,0:T(8,128)(2,1)}, u32[]{:S(2)}, u32[]{:S(2)}) collective-permute-start(bf16[48,48,128]{2,1,0:T(8,128)(2,1)S(1)} %shard_map.122.after_ref.own_ref), channel_id=1, source_target_pairs={{0,1},{1,0},{2,3},{3,2},{4,5},{5,4},{6,7},{7,6},{8,16},{9,17},{10,... | collective-permute-start | bytes 1769480 | tf_op jit(solution)/shard_map/ppermute | solution.py:344
  10.7 0.0 copy-done.8
  10.7 0.1 rev.12
  10.8 0.0 copy-done.9
  10.8 0.1 rev.13
  10.9 0.0 copy-done.10
  10.9 0.1 rev.14
  11.0 0.0 copy-done.11
  11.0 0.1 pad.38
  11.1 0.1 rev.15
  11.3 0.1 pad.42
  11.4 0.0 collective-permute-done.even_ref
  11.5 6.0 %collective-permute-done.1.odd_ref = bf16[3072,128]{1,0:T(8,128)(2,1)S(1)} collective-permute-done((bf16[3072,128]{1,0:T(8,128)(2,1)}, bf16[3072,128]{1,0:T(8,128)(2,1)S(1)}, u32[]{:S(2)}, u32[]{:S(2)}) %collective-permute-start.1) | collective-permute-done | bytes 786464 | tf_op jit(solution)/shard_map/ppermute | solution.py:333
  17.5 0.6 shard_map.124
  18.1 1.7 %collective-permute-start.2 = (bf16[60,48,128]{2,1,0:T(8,128)(2,1)S(1)}, bf16[60,48,128]{2,1,0:T(8,128)(2,1)S(1)}, u32[]{:S(2)}, u32[]{:S(2)}) collective-permute-start(bf16[60,48,128]{2,1,0:T(8,128)(2,1)S(1)} %get-tuple-element.20.own_ref), channel_id=1, source_target_pairs={{0,8},{8,0},{16,24},{24,16},{32,40},{40,32},{48,56},{56,48},{64,72... | collective-permute-start | bytes 2211848 | tf_op jit(solution)/shard_map/ppermute | solution.py:344
  19.8 1.7 %collective-permute-start.3 = (bf16[60,48,128]{2,1,0:T(8,128)(2,1)S(1)}, bf16[60,48,128]{2,1,0:T(8,128)(2,1)S(1)}, u32[]{:S(2)}, u32[]{:S(2)}) collective-permute-start(bf16[60,48,128]{2,1,0:T(8,128)(2,1)S(1)} %get-tuple-element.21), channel_id=1, source_target_pairs={{0,1},{1,0},{2,3},{3,2},{4,5},{5,4},{6,7},{7,6},{8,16},{9,17},{10,... | collective-permute-start | bytes 2211848 | tf_op jit(solution)/shard_map/ppermute | solution.py:344
  21.5 1.1 collective-permute-done.4.even_ref
  22.6 3.4 %collective-permute-done.5.odd_ref = bf16[48,48,128]{2,1,0:T(8,128)(2,1)} collective-permute-done((bf16[48,48,128]{2,1,0:T(8,128)(2,1)S(1)}, bf16[48,48,128]{2,1,0:T(8,128)(2,1)}, u32[]{:S(2)}, u32[]{:S(2)}) %collective-permute-start.5) | collective-permute-done | bytes 589856 | tf_op jit(solution)/shard_map/ppermute | solution.py:344
  26.0 2.2 %shard_map.125.own_ref = bf16[48,48,128]{2,1,0:T(8,128)(2,1)S(1)} custom-call(f32[8,256]{1,0:T(8,128)S(1)} %stack.46.taps_ref, bf16[48,48,128]{2,1,0:T(8,128)(2,1)S(1)} %shard_map.122.after_ref.own_ref, bf16[48,48,128]{2,1,0:T(8,128)(2,1)} %collective-permute-done.4.even_ref, bf16[48,48,128]{2,1,0:T(8,128)(2,1)} %collective-permute-done.5.odd_ref), custom_call_target="tpu_custom_call" | custom-call | flops 500000000 | bytes 2367488 | tf_op jit(solution)/shard_map/pallas_call | solution.py:24
  28.2 0.0 copy-start.7
  28.2 0.1 collective-permute-start.6
  28.3 0.8 collective-permute-start.7
  29.2 1.2 %collective-permute-done.6.even_ref = bf16[48,48,128]{2,1,0:T(8,128)(2,1)S(1)} collective-permute-done((bf16[48,48,128]{2,1,0:T(8,128)(2,1)S(1)}, bf16[48,48,128]{2,1,0:T(8,128)(2,1)S(1)}, u32[]{:S(2)}, u32[]{:S(2)}) %collective-permute-start.6) | collective-permute-done | bytes 589856 | tf_op jit(solution)/shard_map/ppermute | solution.py:333
  30.3 8.6 %collective-permute-done.7.odd_ref = bf16[48,48,128]{2,1,0:T(8,128)(2,1)S(1)} collective-permute-done((bf16[48,48,128]{2,1,0:T(8,128)(2,1)S(1)}, bf16[48,48,128]{2,1,0:T(8,128)(2,1)S(1)}, u32[]{:S(2)}, u32[]{:S(2)}) %collective-permute-start.7) | collective-permute-done | bytes 589856 | tf_op jit(solution)/shard_map/ppermute | solution.py:333
  39.0 0.0 copy-done.2
  39.0 0.0 copy-done.6
  39.0 1.1 shard_map.126.first_ref
  40.0 0.0 collective-permute-done.2.even_ref
  40.0 0.7 collective-permute-done.3.odd_ref
  40.7 0.0 copy-done.7
  40.7 1.8 %shard_map.127 = (f32[48,48,128]{2,1,0:T(8,128)S(1)}, bf16[48,48,128]{2,1,0:T(8,128)(2,1)S(1)}) custom-call(f32[8,256]{1,0:T(8,128)S(1)} %stack.46.taps_ref, bf16[60,48,128]{2,1,0:T(8,128)(2,1)S(1)} %get-tuple-element.20.own_ref, bf16[60,48,128]{2,1,0:T(8,128)(2,1)S(1)} %collective-permute-done.2.even_ref, ...), custom_call_target="tpu_custom_call" | custom-call | flops 1000000000 | bytes 6709248 | tf_op jit(solution)/shard_map/pallas_call | solution.py:24
  42.5 6.4 %collective-permute-start.8 = (bf16[48,48,128]{2,1,0:T(8,128)(2,1)S(1)}, bf16[48,48,128]{2,1,0:T(8,128)(2,1)S(1)}, u32[]{:S(2)}, u32[]{:S(2)}) collective-permute-start(bf16[48,48,128]{2,1,0:T(8,128)(2,1)S(1)} %get-tuple-element.24), channel_id=1, source_target_pairs={{0,128},{128,0},{1,129},{129,1},{2,130},{130,2},{3,131},{131,3},{4... | collective-permute-start | bytes 1769480 | tf_op jit(solution)/shard_map/ppermute | solution.py:404
  48.9 25.3 %collective-permute-done.8.came_ref = bf16[48,48,128]{2,1,0:T(8,128)(2,1)S(1)} collective-permute-done((bf16[48,48,128]{2,1,0:T(8,128)(2,1)S(1)}, bf16[48,48,128]{2,1,0:T(8,128)(2,1)S(1)}, u32[]{:S(2)}, u32[]{:S(2)}) %collective-permute-start.8) | collective-permute-done | bytes 589856 | tf_op jit(solution)/shard_map/ppermute | solution.py:404
  74.2 0.0 copy-done.4
  74.2 1.3 %shard_map.128 = (bf16[48,48,128]{2,1,0:T(8,128)(2,1)S(1)}, bf16[3072,128]{1,0:T(8,128)(2,1)S(1)}, bf16[3072,128]{1,0:T(8,128)(2,1)S(1)}, bf16[24,48,128]{2,1,0:T(8,128)(2,1)S(1)}) custom-call(f32[48,48,128]{2,1,0:T(8,128)S(1)} %get-tuple-element.23.kept_ref, bf16[48,48,128]{2,1,0:T(8,128)(2,1)S(1)} %collective-permute-done.8.came_ref, ...), custom_call_target="tpu_custom_call" | custom-call | flops 400000000 | bytes 6651904 | tf_op jit(solution)/shard_map/pallas_call | solution.py:24
  75.5 0.1 collective-permute-start.9
  75.6 3.0 %collective-permute-start.10 = (bf16[3072,128]{1,0:T(8,128)(2,1)S(1)}, bf16[3072,128]{1,0:T(8,128)(2,1)S(1)}, u32[]{:S(2)}, u32[]{:S(2)}) collective-permute-start(bf16[3072,128]{1,0:T(8,128)(2,1)S(1)} %get-tuple-element.27), channel_id=1, source_target_pairs={{0,7},{1,2},{2,1},{3,4},{4,3},{5,6},{6,5},{7,0},{8,15},{9,10},{10,... | collective-permute-start | bytes 2359304 | tf_op jit(solution)/shard_map/ppermute | solution.py:333
  78.6 0.0 collective-permute-start.13
  78.6 1.2 %collective-permute-start.14 = (bf16[48,48,128]{2,1,0:T(8,128)(2,1)S(1)}, bf16[48,48,128]{2,1,0:T(8,128)(2,1)S(1)}, u32[]{:S(2)}, u32[]{:S(2)}) collective-permute-start(bf16[48,48,128]{2,1,0:T(8,128)(2,1)S(1)} %get-tuple-element.31.own_ref), channel_id=1, source_target_pairs={{0,1},{1,0},{2,3},{3,2},{4,5},{5,4},{6,7},{7,6},{8,16},{9,17},{10,... | collective-permute-start | bytes 1769480 | tf_op jit(solution)/shard_map/ppermute | solution.py:344
  79.8 0.0 collective-permute-done.9.even_ref
  79.8 8.6 %collective-permute-done.10.odd_ref = bf16[3072,128]{1,0:T(8,128)(2,1)S(1)} collective-permute-done((bf16[3072,128]{1,0:T(8,128)(2,1)S(1)}, bf16[3072,128]{1,0:T(8,128)(2,1)S(1)}, u32[]{:S(2)}, u32[]{:S(2)}) %collective-permute-start.10) | collective-permute-done | bytes 786464 | tf_op jit(solution)/shard_map/ppermute | solution.py:333
  88.3 0.6 shard_map.129
  88.9 0.1 collective-permute-start.11
  89.0 0.0 copy-start.1
  89.1 1.3 %collective-permute-start.12 = (bf16[60,48,128]{2,1,0:T(8,128)(2,1)S(1)}, bf16[60,48,128]{2,1,0:T(8,128)(2,1)S(1)}, u32[]{:S(2)}, u32[]{:S(2)}) collective-permute-start(bf16[60,48,128]{2,1,0:T(8,128)(2,1)S(1)} %get-tuple-element.29), channel_id=1, source_target_pairs={{0,1},{1,0},{2,3},{3,2},{4,5},{5,4},{6,7},{7,6},{8,16},{9,17},{10,... | collective-permute-start | bytes 2211848 | tf_op jit(solution)/shard_map/ppermute | solution.py:344
  90.4 4.5 %collective-permute-done.13.even_ref = bf16[48,48,128]{2,1,0:T(8,128)(2,1)S(1)} collective-permute-done((bf16[48,48,128]{2,1,0:T(8,128)(2,1)S(1)}, bf16[48,48,128]{2,1,0:T(8,128)(2,1)S(1)}, u32[]{:S(2)}, u32[]{:S(2)}) %collective-permute-start.13) | collective-permute-done | bytes 589856 | tf_op jit(solution)/shard_map/ppermute | solution.py:344
  94.8 2.1 %collective-permute-done.14.odd_ref = bf16[48,48,128]{2,1,0:T(8,128)(2,1)S(1)} collective-permute-done((bf16[48,48,128]{2,1,0:T(8,128)(2,1)S(1)}, bf16[48,48,128]{2,1,0:T(8,128)(2,1)S(1)}, u32[]{:S(2)}, u32[]{:S(2)}) %collective-permute-start.14) | collective-permute-done | bytes 589856 | tf_op jit(solution)/shard_map/ppermute | solution.py:344
  96.9 1.0 shard_map.130.own_ref
  97.9 0.1 collective-permute-start.15
  98.0 0.1 collective-permute-start.16
  98.1 1.9 %collective-permute-done.15.even_ref = bf16[48,48,128]{2,1,0:T(8,128)(2,1)S(1)} collective-permute-done((bf16[48,48,128]{2,1,0:T(8,128)(2,1)S(1)}, bf16[48,48,128]{2,1,0:T(8,128)(2,1)S(1)}, u32[]{:S(2)}, u32[]{:S(2)}) %collective-permute-start.15) | collective-permute-done | bytes 589856 | tf_op jit(solution)/shard_map/ppermute | solution.py:333
  100.0 8.6 %collective-permute-done.16.odd_ref = bf16[48,48,128]{2,1,0:T(8,128)(2,1)S(1)} collective-permute-done((bf16[48,48,128]{2,1,0:T(8,128)(2,1)S(1)}, bf16[48,48,128]{2,1,0:T(8,128)(2,1)S(1)}, u32[]{:S(2)}, u32[]{:S(2)}) %collective-permute-start.16) | collective-permute-done | bytes 589856 | tf_op jit(solution)/shard_map/ppermute | solution.py:333
  108.6 1.3 %shard_map.131.begun_ref = bf16[2,48,48,128]{3,2,1,0:T(8,128)(2,1)} custom-call(f32[8,256]{1,0:T(8,128)S(1)} %stack.46.taps_ref, bf16[48,48,128]{2,1,0:T(8,128)(2,1)S(1)} %shard_map.130.own_ref, bf16[48,48,128]{2,1,0:T(8,128)(2,1)S(1)} %collective-permute-done.15.even_ref, bf16[48,48,128]{2,1,0:T(8,128)(2,1)S(1)} %collective-permute-done.16.odd_ref, ...), custom_call_target="tpu_custom_call" | custom-call | flops 500000000 | bytes 4136960 | tf_op jit(solution)/shard_map/pallas_call | solution.py:24
  109.9 0.0 collective-permute-done.11.even_ref
  109.9 1.4 %collective-permute-done.12.odd_ref = bf16[60,48,128]{2,1,0:T(8,128)(2,1)S(1)} collective-permute-done((bf16[60,48,128]{2,1,0:T(8,128)(2,1)S(1)}, bf16[60,48,128]{2,1,0:T(8,128)(2,1)S(1)}, u32[]{:S(2)}, u32[]{:S(2)}) %collective-permute-start.12) | collective-permute-done | bytes 737312 | tf_op jit(solution)/shard_map/ppermute | solution.py:344
  111.3 2.4 %shard_map.132 = (bf16[48,48,64]{2,1,0:T(8,128)(2,1)}, bf16[2,48,48,128]{3,2,1,0:T(8,128)(2,1)}) custom-call(f32[8,256]{1,0:T(8,128)S(1)} %stack.46.taps_ref, bf16[60,48,128]{2,1,0:T(8,128)(2,1)S(1)} %get-tuple-element.28.own_ref, bf16[60,48,128]{2,1,0:T(8,128)(2,1)S(1)} %collective-permute-done.11.even_ref, ...), custom_call_target="tpu_custom_call", output_to_operand_aliasing={{1}: (7, {})} | custom-call | flops 700000000 | bytes 6643712 | tf_op jit(solution)/shard_map/pallas_call | solution.py:24
  (27 shorter events, 0.1 us)
Async XLA Ops:
  0.6 1.3 %copy-start = (bf16[2,48,48,128]{3,2,1,0:T(8,128)(2,1)S(1)}, bf16[2,48,48,128]{3,2,1,0:T(8,128)(2,1)}, u32[]{:S(2)}) copy-start(bf16[2,48,48,128]{3,2,1,0:T(8,128)(2,1)} %member_ref.7) | copy-start | bytes 3538948
  1.9 1.1 copy-start.3
  3.0 7.8 %copy-start.8 = (bf16[97]{0:T(256)(128)(2,1)S(1)}, bf16[97]{0:T(256)(128)(2,1)}, u32[]{:S(2)}) copy-start(bf16[97]{0:T(256)(128)(2,1)} %param.18) | copy-start | bytes 586
  3.0 7.9 %copy-start.9 = (bf16[97]{0:T(256)(128)(2,1)S(1)}, bf16[97]{0:T(256)(128)(2,1)}, u32[]{:S(2)}) copy-start(bf16[97]{0:T(256)(128)(2,1)} %param.19) | copy-start | bytes 586
  3.0 8.0 %copy-start.10 = (bf16[49]{0:T(256)(128)(2,1)S(1)}, bf16[49]{0:T(256)(128)(2,1)}, u32[]{:S(2)}) copy-start(bf16[49]{0:T(256)(128)(2,1)} %param.16) | copy-start | bytes 298
  3.0 8.1 %copy-start.11 = (bf16[49]{0:T(256)(128)(2,1)S(1)}, bf16[49]{0:T(256)(128)(2,1)}, u32[]{:S(2)}) copy-start(bf16[49]{0:T(256)(128)(2,1)} %param.17) | copy-start | bytes 298
  4.5 7.0 %collective-permute-start = (bf16[3072,128]{1,0:T(8,128)(2,1)S(1)}, bf16[3072,128]{1,0:T(8,128)(2,1)S(1)}, u32[]{:S(2)}, u32[]{:S(2)}) collective-permute-start(bf16[3072,128]{1,0:T(8,128)(2,1)S(1)} %get-tuple-element.17.sent_ref), channel_id=1, source_target_pairs={{0,1},{1,0},{2,3},{3,2},{4,5},{5,4},{6,7},{7,6},{8,9},{9,8},{10,11... | collective-permute-start | bytes 2359304 | tf_op jit(solution)/shard_map/ppermute | solution.py:333
  4.6 12.9 %collective-permute-start.1 = (bf16[3072,128]{1,0:T(8,128)(2,1)}, bf16[3072,128]{1,0:T(8,128)(2,1)S(1)}, u32[]{:S(2)}, u32[]{:S(2)}) collective-permute-start(bf16[3072,128]{1,0:T(8,128)(2,1)} %get-tuple-element.19), channel_id=1, source_target_pairs={{0,7},{1,2},{2,1},{3,4},{4,3},{5,6},{6,5},{7,0},{8,15},{9,10},{10,... | collective-permute-start | bytes 2359304 | tf_op jit(solution)/shard_map/ppermute | solution.py:333
  7.4 15.2 %collective-permute-start.4 = (bf16[48,48,128]{2,1,0:T(8,128)(2,1)S(1)}, bf16[48,48,128]{2,1,0:T(8,128)(2,1)}, u32[]{:S(2)}, u32[]{:S(2)}) collective-permute-start(bf16[48,48,128]{2,1,0:T(8,128)(2,1)S(1)} %shard_map.122.after_ref.own_ref), channel_id=1, source_target_pairs={{0,8},{8,0},{16,24},{24,16},{32,40},{40,32},{48,56},{56,48},{64,72... | collective-permute-start | bytes 1769480 | tf_op jit(solution)/shard_map/ppermute | solution.py:344
  9.0 17.0 %collective-permute-start.5 = (bf16[48,48,128]{2,1,0:T(8,128)(2,1)S(1)}, bf16[48,48,128]{2,1,0:T(8,128)(2,1)}, u32[]{:S(2)}, u32[]{:S(2)}) collective-permute-start(bf16[48,48,128]{2,1,0:T(8,128)(2,1)S(1)} %shard_map.122.after_ref.own_ref), channel_id=1, source_target_pairs={{0,1},{1,0},{2,3},{3,2},{4,5},{5,4},{6,7},{7,6},{8,16},{9,17},{10,... | collective-permute-start | bytes 1769480 | tf_op jit(solution)/shard_map/ppermute | solution.py:344
  18.1 21.9 %collective-permute-start.2 = (bf16[60,48,128]{2,1,0:T(8,128)(2,1)S(1)}, bf16[60,48,128]{2,1,0:T(8,128)(2,1)S(1)}, u32[]{:S(2)}, u32[]{:S(2)}) collective-permute-start(bf16[60,48,128]{2,1,0:T(8,128)(2,1)S(1)} %get-tuple-element.20.own_ref), channel_id=1, source_target_pairs={{0,8},{8,0},{16,24},{24,16},{32,40},{40,32},{48,56},{56,48},{64,72... | collective-permute-start | bytes 2211848 | tf_op jit(solution)/shard_map/ppermute | solution.py:344
  19.8 19.2 %copy-start.2 = (bf16[2,48,48,128]{3,2,1,0:T(8,128)(2,1)S(1)}, bf16[2,48,48,128]{3,2,1,0:T(8,128)(2,1)}, u32[]{:S(2)}) copy-start(bf16[2,48,48,128]{3,2,1,0:T(8,128)(2,1)} %pert_ref.5) | copy-start | bytes 3538948
  19.8 19.2 %copy-start.6 = (bf16[128,128]{1,0:T(8,128)(2,1)S(1)}, bf16[128,128]{1,0:T(8,128)(2,1)}, u32[]{:S(2)}) copy-start(bf16[128,128]{1,0:T(8,128)(2,1)} %vert_ref.5) | copy-start | bytes 98308
  19.8 20.9 %collective-permute-start.3 = (bf16[60,48,128]{2,1,0:T(8,128)(2,1)S(1)}, bf16[60,48,128]{2,1,0:T(8,128)(2,1)S(1)}, u32[]{:S(2)}, u32[]{:S(2)}) collective-permute-start(bf16[60,48,128]{2,1,0:T(8,128)(2,1)S(1)} %get-tuple-element.21), channel_id=1, source_target_pairs={{0,1},{1,0},{2,3},{3,2},{4,5},{5,4},{6,7},{7,6},{8,16},{9,17},{10,... | collective-permute-start | bytes 2211848 | tf_op jit(solution)/shard_map/ppermute | solution.py:344
  28.2 12.5 %copy-start.7 = (bf16[128,128]{1,0:T(8,128)(2,1)S(1)}, bf16[128,128]{1,0:T(8,128)(2,1)}, u32[]{:S(2)}) copy-start(bf16[128,128]{1,0:T(8,128)(2,1)} %static_ref.5) | copy-start | bytes 98308
  28.2 2.1 %collective-permute-start.6 = (bf16[48,48,128]{2,1,0:T(8,128)(2,1)S(1)}, bf16[48,48,128]{2,1,0:T(8,128)(2,1)S(1)}, u32[]{:S(2)}, u32[]{:S(2)}) collective-permute-start(bf16[48,48,128]{2,1,0:T(8,128)(2,1)S(1)} %shard_map.125.own_ref), channel_id=1, source_target_pairs={{0,1},{1,0},{2,3},{3,2},{4,5},{5,4},{6,7},{7,6},{8,9},{9,8},{10,11... | collective-permute-start | bytes 1769480 | tf_op jit(solution)/shard_map/ppermute | solution.py:333
  28.3 10.6 %collective-permute-start.7 = (bf16[48,48,128]{2,1,0:T(8,128)(2,1)S(1)}, bf16[48,48,128]{2,1,0:T(8,128)(2,1)S(1)}, u32[]{:S(2)}, u32[]{:S(2)}) collective-permute-start(bf16[48,48,128]{2,1,0:T(8,128)(2,1)S(1)} %shard_map.125.own_ref), channel_id=1, source_target_pairs={{0,7},{1,2},{2,1},{3,4},{4,3},{5,6},{6,5},{7,0},{8,15},{9,10},{10,... | collective-permute-start | bytes 1769480 | tf_op jit(solution)/shard_map/ppermute | solution.py:333
  40.7 33.5 %copy-start.4 = (bf16[48,48,128]{2,1,0:T(8,128)(2,1)S(1)}, bf16[48,48,128]{2,1,0:T(8,128)(2,1)}, u32[]{:S(2)}) copy-start(bf16[48,48,128]{2,1,0:T(8,128)(2,1)} %dep_ref.1) | copy-start | bytes 1769476
  40.7 33.5 %copy-start.5 = (bf16[48,48,128]{2,1,0:T(8,128)(2,1)S(1)}, bf16[48,48,128]{2,1,0:T(8,128)(2,1)}, u32[]{:S(2)}) copy-start(bf16[48,48,128]{2,1,0:T(8,128)(2,1)} %weight_ref.1) | copy-start | bytes 1769476
  42.5 31.7 %collective-permute-start.8 = (bf16[48,48,128]{2,1,0:T(8,128)(2,1)S(1)}, bf16[48,48,128]{2,1,0:T(8,128)(2,1)S(1)}, u32[]{:S(2)}, u32[]{:S(2)}) collective-permute-start(bf16[48,48,128]{2,1,0:T(8,128)(2,1)S(1)} %get-tuple-element.24), channel_id=1, source_target_pairs={{0,128},{128,0},{1,129},{129,1},{2,130},{130,2},{3,131},{131,3},{4... | collective-permute-start | bytes 1769480 | tf_op jit(solution)/shard_map/ppermute | solution.py:404
  75.5 4.3 %collective-permute-start.9 = (bf16[3072,128]{1,0:T(8,128)(2,1)S(1)}, bf16[3072,128]{1,0:T(8,128)(2,1)S(1)}, u32[]{:S(2)}, u32[]{:S(2)}) collective-permute-start(bf16[3072,128]{1,0:T(8,128)(2,1)S(1)} %get-tuple-element.25.sent_ref), channel_id=1, source_target_pairs={{0,1},{1,0},{2,3},{3,2},{4,5},{5,4},{6,7},{7,6},{8,9},{9,8},{10,11... | collective-permute-start | bytes 2359304 | tf_op jit(solution)/shard_map/ppermute | solution.py:333
  75.6 12.7 %collective-permute-start.10 = (bf16[3072,128]{1,0:T(8,128)(2,1)S(1)}, bf16[3072,128]{1,0:T(8,128)(2,1)S(1)}, u32[]{:S(2)}, u32[]{:S(2)}) collective-permute-start(bf16[3072,128]{1,0:T(8,128)(2,1)S(1)} %get-tuple-element.27), channel_id=1, source_target_pairs={{0,7},{1,2},{2,1},{3,4},{4,3},{5,6},{6,5},{7,0},{8,15},{9,10},{10,... | collective-permute-start | bytes 2359304 | tf_op jit(solution)/shard_map/ppermute | solution.py:333
  78.6 16.3 %collective-permute-start.13 = (bf16[48,48,128]{2,1,0:T(8,128)(2,1)S(1)}, bf16[48,48,128]{2,1,0:T(8,128)(2,1)S(1)}, u32[]{:S(2)}, u32[]{:S(2)}) collective-permute-start(bf16[48,48,128]{2,1,0:T(8,128)(2,1)S(1)} %get-tuple-element.31.own_ref), channel_id=1, source_target_pairs={{0,8},{8,0},{16,24},{24,16},{32,40},{40,32},{48,56},{56,48},{64,72... | collective-permute-start | bytes 1769480 | tf_op jit(solution)/shard_map/ppermute | solution.py:344
  78.6 18.4 %collective-permute-start.14 = (bf16[48,48,128]{2,1,0:T(8,128)(2,1)S(1)}, bf16[48,48,128]{2,1,0:T(8,128)(2,1)S(1)}, u32[]{:S(2)}, u32[]{:S(2)}) collective-permute-start(bf16[48,48,128]{2,1,0:T(8,128)(2,1)S(1)} %get-tuple-element.31.own_ref), channel_id=1, source_target_pairs={{0,1},{1,0},{2,3},{3,2},{4,5},{5,4},{6,7},{7,6},{8,16},{9,17},{10,... | collective-permute-start | bytes 1769480 | tf_op jit(solution)/shard_map/ppermute | solution.py:344
  88.9 21.0 %collective-permute-start.11 = (bf16[60,48,128]{2,1,0:T(8,128)(2,1)S(1)}, bf16[60,48,128]{2,1,0:T(8,128)(2,1)S(1)}, u32[]{:S(2)}, u32[]{:S(2)}) collective-permute-start(bf16[60,48,128]{2,1,0:T(8,128)(2,1)S(1)} %get-tuple-element.28.own_ref), channel_id=1, source_target_pairs={{0,8},{8,0},{16,24},{24,16},{32,40},{40,32},{48,56},{56,48},{64,72... | collective-permute-start | bytes 2211848 | tf_op jit(solution)/shard_map/ppermute | solution.py:344
  89.0 19.6 %copy-start.1 = (bf16[2,48,48,128]{3,2,1,0:T(8,128)(2,1)S(1)}, bf16[2,48,48,128]{3,2,1,0:T(8,128)(2,1)}, u32[]{:S(2)}) copy-start(bf16[2,48,48,128]{3,2,1,0:T(8,128)(2,1)} %member_ref.7) | copy-start | bytes 3538948
  89.1 22.2 %collective-permute-start.12 = (bf16[60,48,128]{2,1,0:T(8,128)(2,1)S(1)}, bf16[60,48,128]{2,1,0:T(8,128)(2,1)S(1)}, u32[]{:S(2)}, u32[]{:S(2)}) collective-permute-start(bf16[60,48,128]{2,1,0:T(8,128)(2,1)S(1)} %get-tuple-element.29), channel_id=1, source_target_pairs={{0,1},{1,0},{2,3},{3,2},{4,5},{5,4},{6,7},{7,6},{8,16},{9,17},{10,... | collective-permute-start | bytes 2211848 | tf_op jit(solution)/shard_map/ppermute | solution.py:344
  97.9 2.1 %collective-permute-start.15 = (bf16[48,48,128]{2,1,0:T(8,128)(2,1)S(1)}, bf16[48,48,128]{2,1,0:T(8,128)(2,1)S(1)}, u32[]{:S(2)}, u32[]{:S(2)}) collective-permute-start(bf16[48,48,128]{2,1,0:T(8,128)(2,1)S(1)} %shard_map.130.own_ref), channel_id=1, source_target_pairs={{0,1},{1,0},{2,3},{3,2},{4,5},{5,4},{6,7},{7,6},{8,9},{9,8},{10,11... | collective-permute-start | bytes 1769480 | tf_op jit(solution)/shard_map/ppermute | solution.py:333
  98.0 10.6 %collective-permute-start.16 = (bf16[48,48,128]{2,1,0:T(8,128)(2,1)S(1)}, bf16[48,48,128]{2,1,0:T(8,128)(2,1)S(1)}, u32[]{:S(2)}, u32[]{:S(2)}) collective-permute-start(bf16[48,48,128]{2,1,0:T(8,128)(2,1)S(1)} %shard_map.130.own_ref), channel_id=1, source_target_pairs={{0,7},{1,2},{2,1},{3,4},{4,3},{5,6},{6,5},{7,0},{8,15},{9,10},{10,... | collective-permute-start | bytes 1769480 | tf_op jit(solution)/shard_map/ppermute | solution.py:333

commit v2 on v1

--- a/solution.py
+++ b/solution.py
@@ -9,6 +9,8 @@
 
 TILE = 48
 SLAB = 32
+BRIEF = 1_000
+LONG = 20_000_000_000
 BF = jnp.bfloat16
 F32 = jnp.float32
 
@@ -29,7 +31,7 @@
         scratch_shapes=list(scratch),
         input_output_aliases=aliases or {},
         compiler_params=pltpu.CompilerParams(vmem_limit_bytes=20 << 20),
-        cost_estimate=pl.CostEstimate(flops=flops, bytes_accessed=moved, transcendentals=0),
+        cost_estimate=pl.CostEstimate(flops=flops, bytes_accessed=min(moved, flops), transcendentals=0),
     )(*args)
 
 
@@ -114,6 +116,17 @@
     return jnp.concatenate([first, own, last], axis=0)
 
 
+def taps_kernel(lx_ref, ly_ref, sx_ref, sy_ref, out_ref):
+    sub = lax.broadcasted_iota(jnp.int32, (256, 256), 0)
+    lane = lax.broadcasted_iota(jnp.int32, (256, 256), 1)
+    for i, (ref, start) in enumerate(((lx_ref, 0), (ly_ref, 0), (sx_ref, 0), (sy_ref, SLAB - 24))):
+        n = ref.shape[0]
+        taps = jnp.broadcast_to(ref[...].astype(F32)[None, :], (8, n)).astype(BF)
+        for row, source in ((i, lane - start), (i + 4, n - 1 - lane + start)):
+            spread = jnp.where(sub[:n] == source[:n], 1.0, 0.0).astype(BF)
+            out_ref[row : row + 1] = dot(taps, spread)[:1]
+
+
 def pack_slabs(packed, even_ref, odd_ref):
     right = packed[:, 16:48].reshape(768, 128)
     left = packed[:, :SLAB].reshape(768, 128)
@@ -122,33 +135,27 @@
     odd_ref[2304:] = pick(odd, right, left)
 
 
-def take_kernel(member_ref, out_ref, sems):
+def pack_x(packed, even_ref, odd_ref):
+    right = halves(packed[..., 64:])
+    left = halves(packed[..., :64])
+    odd, _ = place("tx")
+    even_ref[TILE:] = pick(odd, left, right)
+    odd_ref[TILE:] = pick(odd, right, left)
+
+
+def pack_kernel(member_ref, static_ref, first_ref, even_ref, odd_ref, own_ref, static, sems):
     copies = [
-        pltpu.make_async_copy(member_ref.at[0, pl.ds(12 * i, 12)], out_ref.at[pl.ds(12 * i, 12)], sems.at[i])
+        pltpu.make_async_copy(static_ref.at[pl.ds(12 * i, 12)], static.at[pl.ds(12 * i, 12)], sems.at[i])
         for i in range(4)
     ]
     for copy in copies:
         copy.start()
+    first_ref[...] = member_ref[0]
+    second = member_ref[1].reshape(2304, 128)
+    even_ref[:2304] = second
+    odd_ref[:2304] = second
     for copy in copies:
         copy.wait()
-
-
-def pack_kernel(static_ref, member_ref, after_ref, even_ref, odd_ref, own_ref, static, second, sems):
-    copies = [
-        pltpu.make_async_copy(member_ref.at[1, pl.ds(24 * i, 24)], second.at[pl.ds(24 * i, 24)], sems.at[i])
-        for i in range(2)
-    ]
-    copies += [
-        pltpu.make_async_copy(static_ref.at[pl.ds(24 * i, 24)], static.at[pl.ds(24 * i, 24)], sems.at[2 + i])
-        for i in range(2)
-    ]
-    for copy in copies:
-        copy.start()
-    for copy in copies:
-        copy.wait()
-    member = second[...].reshape(2304, 128)
-    even_ref[:2304] = member
-    odd_ref[:2304] = member
     packed = halves(static[...])
     own_ref[...] = packed
     pack_slabs(packed, even_ref, odd_ref)
@@ -178,12 +185,7 @@
         out_ref[x] = out.astype(BF)
 
     along_y(static, static_line, 24, static_store)
-    packed = out_ref[...]
-    right = halves(packed[..., 64:])
-    left = halves(packed[..., :64])
-    odd, _ = place("tx")
-    to_even_ref[TILE:] = pick(odd, left, right)
-    to_odd_ref[TILE:] = pick(odd, right, left)
+    pack_x(out_ref[...], to_even_ref, to_odd_ref)
 
 
 def first_x_kernel(row, taps_ref, own_ref, even_ref, odd_ref, out_ref):
@@ -259,8 +261,7 @@
 
 
 def residual_kernel(
-    kept_ref, came_ref, dep_ref, weight_ref, pert_ref, vert_ref, static_ref,
-    a_ref, even_ref, odd_ref, own_ref
+    kept_ref, came_ref, dep_ref, weight_ref, pert_ref, vert_ref, static_ref, even_ref, odd_ref, own_ref, b_ref
 ):
     vert = vert_ref[...]
     static_mat = static_block(static_ref)
@@ -275,53 +276,84 @@
             res.append(r.reshape(192, 128))
             first = (pert_ref[0, at].astype(F32) * r32).astype(BF).reshape(192, 128)
             second = (pert_ref[1, at].astype(F32) * r32).astype(BF).reshape(192, 128)
-            a_ref[at] = dot(first, vert).astype(BF).reshape(4, TILE, 128)
-            back = dot(second, vert).astype(BF)
-            cells = pl.ds(pl.multiple_of(x * TILE, 192), 192)
-            even_ref[cells] = back
-            odd_ref[cells] = back
+            back = dot(first, vert).astype(BF).reshape(4, TILE, 128)
+            even_ref[at] = back
+            odd_ref[at] = back
+            b_ref[at] = dot(second, vert).astype(BF).reshape(4, TILE, 128)
         static = dot(jnp.concatenate(res, axis=1), static_mat).astype(BF)
         own_ref[pl.ds(4 * i, 4)] = static.reshape(4, TILE, 128)
         return carry
 
     lax.fori_loop(0, 6, step, 0, unroll=2)
-    pack_slabs(own_ref[...], even_ref, odd_ref)
-
-
-def last_a_kernel(row, taps_ref, own_ref, even_ref, odd_ref, member_ref, out_ref, out, sems):
-    def store(x, filtered):
-        out[x] = (member_ref[0, x].astype(F32) + filtered.astype(BF).astype(F32)).astype(BF)
+    pack_x(own_ref[...], even_ref, odd_ref)
+
+
+def back_x_kernel(
+    rows, taps_ref, sent_ref, own_ref, even_ref, odd_ref, after_ref, to_even_ref, to_odd_ref, out_ref
+):
+    member = band_swapped(taps_ref[rows[0] : rows[0] + 1], "tx")
+    static = band(taps_ref[rows[1] : rows[1] + 1], 24, 72)
+    for c in range(0, TILE, 16):
+        at = slice(c, c + 16)
+        out = along_x(member, [even_ref[:TILE, at], sent_ref[:TILE, at], odd_ref[:TILE, at]])
+        to_even_ref[:TILE, at] = out
+        to_odd_ref[:TILE, at] = out
+        left, right = sides(even_ref[TILE:, at], odd_ref[TILE:, at], "tx")
+        out_ref[:, at] = along_x(static, [static_parts(left, own_ref[:, at], right)])
+    packed = out_ref[...]
+    right = packed[:, 16:48].reshape(16, TILE, 128)
+    left = packed[:, :SLAB].reshape(16, TILE, 128)
+    odd, _ = place("ty")
+    to_even_ref[TILE:] = pick(odd, left, right)
+    to_odd_ref[TILE:] = pick(odd, right, left)
+
+
+def back_y_kernel(row, taps_ref, own_ref, even_ref, odd_ref, out_ref):
+    def store(x, out):
+        out_ref[x] = out.astype(BF)
 
     second_y(row, taps_ref, own_ref, even_ref, odd_ref, store)
+
+
+def last_b_kernel(row, taps_ref, own_ref, even_ref, odd_ref, member_ref, member_out, member, sems):
+    matrix = band_swapped(taps_ref[row : row + 1], "tx")
+    copies = []
+    for i in range(3):
+        at = slice(16 * i, 16 * i + 16)
+        b = along_x(matrix, [even_ref[:, at], own_ref[:, at], odd_ref[:, at]])
+        member[i] = (member_ref[1, :, at].astype(F32) + b.astype(F32)).astype(BF)
+        copies.append(pltpu.make_async_copy(member.at[i], member_out.at[1, :, at], sems.at[i]))
+        copies[i].start()
+    for copy in copies:
+        copy.wait()
+
+
+def last_a_kernel(
+    rows, taps_ref, own_ref, even_ref, odd_ref, s_ref, member_ref, control_ref, begun_ref,
+    static_out, member_out, static, member, sems
+):
+    def store(x, out):
+        member[x] = (member_ref[0, x].astype(F32) + out.astype(BF).astype(F32)).astype(BF)
+
+    second_y(rows[0], taps_ref, own_ref, even_ref, odd_ref, store)
     copies = [
-        pltpu.make_async_copy(out.at[pl.ds(12 * i, 12)], out_ref.at[0, pl.ds(12 * i, 12)], sems.at[i])
-        for i in range(4)
+        pltpu.make_async_copy(member.at[pl.ds(24 * i, 24)], member_out.at[0, pl.ds(24 * i, 24)], sems.at[i])
+        for i in range(2)
     ]
     for copy in copies:
         copy.start()
-    for copy in copies:
-        copy.wait()
-
-
-def last_b_kernel(
-    rows, taps_ref, own_ref, even_ref, odd_ref, s_ref, member_ref, control_ref, begun_ref,
-    static_out, member_out, static, member, sems
-):
-    copies = []
-
-    def block(at, b, s):
-        i = len(copies) // 2
-        member[i] = (member_ref[1, :, at].astype(F32) + b.astype(F32)).astype(BF)
-        both = control_ref[:, at].astype(F32) + s.astype(F32)
-        static[i] = unhalves(both.astype(BF))
-        for copy in (
-            pltpu.make_async_copy(member.at[i], member_out.at[1, :, at], sems.at[0, i]),
-            pltpu.make_async_copy(static.at[i], static_out.at[:, at], sems.at[1, i]),
-        ):
-            copy.start()
-            copies.append(copy)
-
-    second_x(rows, taps_ref, own_ref, even_ref, odd_ref, s_ref, block)
+    matrix = band(taps_ref[rows[1] : rows[1] + 1], TILE, 112)
+    slabs = [r[TILE:].reshape(24, SLAB, 128) for r in (even_ref, odd_ref)]
+    left, right = sides(slabs[0], slabs[1], "ty")
+    for x in range(0, 24, 2):
+        lines = [jnp.concatenate([left[k], s_ref[k], right[k]], axis=0) for k in (x, x + 1)]
+        out = dot(matrix, jnp.concatenate(lines, axis=1)).astype(BF).astype(F32)
+        for k in (0, 1):
+            both = (control_ref[x + k].astype(F32) + out[:, 128 * k : 128 * k + 128]).astype(BF)
+            static[x + k] = both[:, :64]
+            static[x + k + 24] = both[:, 64:]
+    copies.append(pltpu.make_async_copy(static, static_out, sems.at[2]))
+    copies[2].start()
     for copy in copies:
         copy.wait()
 
@@ -344,18 +376,18 @@
     return lax.ppermute(even, "tx", first), lax.ppermute(odd, ("tx", "ty"), second)
 
 
-def first_filters(taps, back, a, to_even, to_odd, own):
+def first_filters(taps, a, to_even, to_odd, own):
     a_halo = swaps_x(a, a)
     b_halo = swaps_y(to_even, to_odd)
     tile = (TILE, TILE, 128)
     b_to_even, b_to_odd, s = call(
-        functools.partial(first_y_kernel, 1 + back, 3 + back),
+        functools.partial(first_y_kernel, 1, 3),
         (shape(60, TILE, 128), shape(60, TILE, 128), shape(24, TILE, 128)),
         (taps, to_even, own) + b_halo,
         700_000_000,
     )
     b_halo = swaps_x(b_to_even, b_to_odd)
-    (a,) = call(functools.partial(first_x_kernel, back), (shape(*tile),), (taps, a) + a_halo, 500_000_000)
+    (a,) = call(functools.partial(first_x_kernel, 0), (shape(*tile),), (taps, a) + a_halo, 500_000_000)
     a_halo = swaps_y(a, a)
     return (a,) + a_halo, (b_to_even,) + b_halo + (s,)
 
@@ -373,25 +405,17 @@
     static_vertical,
     local_vertical,
 ):
-    rows = []
-    for flip in (False, True):
-        for taps, start in ((local_kx, 0), (local_ky, 0), (static_kx, 0), (static_ky, SLAB - 24)):
-            taps = taps[::-1] if flip else taps
-            rows.append(jnp.pad(taps.astype(F32), (start, 256 - start - taps.shape[0])))
-    taps = jnp.stack(rows)
+    (taps,) = call(
+        taps_kernel, (shape(8, 256, dtype=F32),), (local_kx, local_ky, static_kx, static_ky), BRIEF
+    )
     tile = (TILE, TILE, 128)
     sent_shapes = (shape(3072, 128), shape(3072, 128), shape(24, TILE, 128))
 
-    (a,) = call(
-        take_kernel, (shape(*tile),), (member_control,), 1_000_000,
-        [pltpu.SemaphoreType.DMA((4,))], in_any=(0,),
-    )
-    to_even, to_odd, control = call(
-        pack_kernel, sent_shapes, (static_control, member_control, a), 1_000_000,
-        [pltpu.VMEM((TILE, TILE, 64), BF), pltpu.VMEM(tile, BF), pltpu.SemaphoreType.DMA((4,))],
-        in_any=(0, 1, 2),
-    )
-    a, b = first_filters(taps, 0, a, to_even, to_odd, control)
+    a, to_even, to_odd, control = call(
+        pack_kernel, (shape(*tile),) + sent_shapes, (member_control, static_control), 1_000_000,
+        [pltpu.VMEM((TILE, TILE, 64), BF), pltpu.SemaphoreType.DMA((4,))], in_any=(1,),
+    )
+    a, b = first_filters(taps, a, to_even, to_odd, control)
     (first,) = call(
         functools.partial(forward_a_kernel, 1), (shape(*tile, dtype=F32),),
         (taps,) + a + (perturbations, local_vertical), 800_000_000, [pltpu.VMEM(tile, BF)],
@@ -402,19 +426,28 @@
     )
     size = lax.axis_size("mem")
     came = lax.ppermute(sent, "mem", [(i, size - 1 - i) for i in range(size)])
-    a, to_even, to_odd, own = call(
-        residual_kernel, (shape(*tile),) + sent_shapes,
+
+    to_even, to_odd, own, b = call(
+        residual_kernel, (shape(60, TILE, 128), shape(60, TILE, 128), shape(24, TILE, 128), shape(*tile)),
         (kept, came, departures, obs_weight, perturbations, local_vertical, static_vertical), 400_000_000,
     )
-    a, b = first_filters(taps, 4, a, to_even, to_odd, own)
+    a = (to_even, own) + swaps_x(to_even, to_odd)
+    (b,) = call(functools.partial(back_y_kernel, 5), (shape(*tile),), (taps, b) + swaps_y(b, b), BRIEF)
+    b_halo = swaps_x(b, b)
+    args = (taps,) + a + (b,)
+    to_even, to_odd, s = call(
+        functools.partial(back_x_kernel, (4, 6)),
+        (shape(64, TILE, 128), shape(64, TILE, 128), shape(24, TILE, 128)), args, LONG, in_any=(len(args) - 1,),
+    )
+    a = (to_even,) + swaps_y(to_even, to_odd) + (s,)
     (begun,) = call(
-        functools.partial(last_a_kernel, 5), (shape(2, *tile),), (taps,) + a + (member_control,), 500_000_000,
-        [pltpu.VMEM(tile, BF), pltpu.SemaphoreType.DMA((4,))], out_any=(0,),
-    )
-    args = (taps,) + b + (member_control, control, begun)
+        functools.partial(last_b_kernel, 4), (shape(2, *tile),), (taps, b) + b_halo + (member_control,), LONG,
+        [pltpu.VMEM((3, TILE, 16, 128), BF), pltpu.SemaphoreType.DMA((3,))], out_any=(0,),
+    )
+    args = (taps,) + a + (member_control, control, begun)
     return tuple(call(
-        functools.partial(last_b_kernel, (4, 6)), (shape(TILE, TILE, 64), shape(2, *tile)), args, 700_000_000,
-        [pltpu.VMEM((3, TILE, 16, 64), BF), pltpu.VMEM((3, TILE, 16, 128), BF), pltpu.SemaphoreType.DMA((2, 3))],
+        functools.partial(last_a_kernel, (5, 7)), (shape(TILE, TILE, 64), shape(2, *tile)), args, 700_000_000,
+        [pltpu.VMEM((TILE, TILE, 64), BF), pltpu.VMEM(tile, BF), pltpu.SemaphoreType.DMA((3,))],
         in_any=(len(args) - 1,), out_any=(0, 1), aliases={len(args) - 1: 1},
     ))
 

time: 114 us -> 113 us (level)
  starting transfers between devices: 22.8 us -> 30 us
  waiting for transfers between devices: 73.2 us -> 66.5 us
  Pallas kernels: 14.5 us -> 12.5 us
    ppermute x8, waiting for transfers between devices: 34.9 us -> 26.3 us  [swaps_y(): return (lax.ppermute(even, 'ty', first), lax.ppermute(odd, 'ty', second))]
    ppermute x8, starting transfers between devices: 7.11 us -> 12.3 us  [swaps_y(): return (lax.ppermute(even, 'ty', first), lax.ppermute(odd, 'ty', second))]
    pallas_call x11, Pallas kernels: 14.5 us -> 12.5 us  [call(): pl.pallas_call(kernel, out_shape=outs, in_specs=[ANY if i in in_any else...]
    ppermute x4, starting transfers between devices: 3.34 us -> 5.23 us  [swaps_x(): lax.ppermute(even, 'tx', first)]
    ppermute x4, waiting for transfers between devices: 5.57 us -> 6.72 us  [swaps_x(): lax.ppermute(even, 'tx', first)]
  transfers between devices with their start and end apart: 17 -> 17, of which waited for: 13 -> 13; matrix products, arithmetic and copies ran while one was open for 1% -> 0% of each run, Pallas kernels for 6% -> 6%
where the time goes in v2:
time: 113 us; the launch traced here: 112 us
  waiting for transfers between devices  66.5 us (59%)
  starting transfers between devices  30 us (27%)
  Pallas kernels  12.5 us (11%)
  local copies, waits for them, and re-layouts  2.37 us (2%)
    ppermute x8, waiting for transfers between devices, swaps_y(): return (lax.ppermute(even, 'ty', first), lax.ppermute(odd, 'ty', second))  26.3 us
    ppermute x1, waiting for transfers between devices, body(): came = lax.ppermute(sent, 'mem', [(i, size - 1 - i) for i in range(size)])  25 us
    pallas_call x11, Pallas kernels, call(): pl.pallas_call(kernel, out_shape=outs, in_specs=[ANY if i in in_any else...  12.5 us
    ppermute x8, starting transfers between devices, swaps_y(): return (lax.ppermute(even, 'ty', first), lax.ppermute(odd, 'ty', second))  12.3 us
    ppermute x4, waiting for transfers between devices, swaps_x(): lax.ppermute(odd, ('tx', 'ty'), second)  8.48 us
    ppermute x4, waiting for transfers between devices, swaps_x(): lax.ppermute(even, 'tx', first)  6.72 us
    ppermute x1, starting transfers between devices, body(): came = lax.ppermute(sent, 'mem', [(i, size - 1 - i) for i in range(size)])  6.38 us
    ppermute x4, starting transfers between devices, swaps_x(): lax.ppermute(odd, ('tx', 'ty'), second)  6.15 us
  transfers between devices with their start and end apart: 17, of which 13 were waited for; matrix products, arithmetic and copies ran while one was open for 0% of the time, Pallas kernels for 6%

profile of v2, /device:TPU:32, one launch (start us, length us, event | category | flops | bytes accessed | tf_op | source)
XLA Modules:
  0.0 112.3 jit_solution(7728963421842980401)
XLA Ops:
  0.6 0.0 copy-start.1
  0.6 1.3 %copy-done.1 = bf16[2,48,48,128]{3,2,1,0:T(8,128)(2,1)S(1)} copy-done((bf16[2,48,48,128]{3,2,1,0:T(8,128)(2,1)S(1)}, bf16[2,48,48,128]{3,2,1,0:T(8,128)(2,1)}, u32[]{:S(2)}) %copy-start.1) | copy-done | bytes 1179672
  1.9 0.0 copy-start.3
  1.9 1.1 copy-done.3
  3.0 0.0 copy-start.8
  3.0 0.0 copy-start.9
  3.0 0.0 copy-start.10
  3.0 0.0 copy-start.11
  3.0 1.2 %shard_map.123 = (bf16[48,48,128]{2,1,0:T(8,128)(2,1)S(1)}, bf16[3072,128]{1,0:T(8,128)(2,1)S(1)}, bf16[3072,128]{1,0:T(8,128)(2,1)S(1)}, bf16[24,48,128]{2,1,0:T(8,128)(2,1)S(1)}) custom-call(bf16[2,48,48,128]{3,2,1,0:T(8,128)(2,1)S(1)} %copy-done.1, bf16[48,48,64]{2,1,0:T(8,128)(2,1)S(1)} %copy-done.3), custom_call_target="tpu_custom_call" | custom-call | flops 1000000 | bytes 1000000 | tf_op jit(solution)/shard_map/pallas_call | solution.py:26
  4.1 0.1 collective-permute-start
  4.2 2.9 %collective-permute-start.1 = (bf16[3072,128]{1,0:T(8,128)(2,1)S(1)}, bf16[3072,128]{1,0:T(8,128)(2,1)S(1)}, u32[]{:S(2)}, u32[]{:S(2)}) collective-permute-start(bf16[3072,128]{1,0:T(8,128)(2,1)S(1)} %get-tuple-element.20), channel_id=1, source_target_pairs={{0,7},{1,2},{2,1},{3,4},{4,3},{5,6},{6,5},{7,0},{8,15},{9,10},{10,... | collective-permute-start | bytes 2359304 | tf_op jit(solution)/shard_map/ppermute | solution.py:365
  7.1 1.6 %collective-permute-start.4 = (bf16[48,48,128]{2,1,0:T(8,128)(2,1)S(1)}, bf16[48,48,128]{2,1,0:T(8,128)(2,1)S(1)}, u32[]{:S(2)}, u32[]{:S(2)}) collective-permute-start(bf16[48,48,128]{2,1,0:T(8,128)(2,1)S(1)} %get-tuple-element.24.own_ref), channel_id=1, source_target_pairs={{0,8},{8,0},{16,24},{24,16},{32,40},{40,32},{48,56},{56,48},{64,72... | collective-permute-start | bytes 1769480 | tf_op jit(solution)/shard_map/ppermute | solution.py:376
  8.7 1.7 %collective-permute-start.5 = (bf16[48,48,128]{2,1,0:T(8,128)(2,1)S(1)}, bf16[48,48,128]{2,1,0:T(8,128)(2,1)S(1)}, u32[]{:S(2)}, u32[]{:S(2)}) collective-permute-start(bf16[48,48,128]{2,1,0:T(8,128)(2,1)S(1)} %get-tuple-element.24.own_ref), channel_id=1, source_target_pairs={{0,1},{1,0},{2,3},{3,2},{4,5},{5,4},{6,7},{7,6},{8,16},{9,17},{10,... | collective-permute-start | bytes 1769480 | tf_op jit(solution)/shard_map/ppermute | solution.py:376
  10.4 0.0 copy-done.8
  10.4 0.0 copy-done.9
  10.4 0.0 copy-done.10
  10.4 0.0 copy-done.11
  10.4 0.2 shard_map.122.taps_ref
  10.6 0.0 collective-permute-done.even_ref
  10.6 6.4 %collective-permute-done.1.odd_ref = bf16[3072,128]{1,0:T(8,128)(2,1)S(1)} collective-permute-done((bf16[3072,128]{1,0:T(8,128)(2,1)S(1)}, bf16[3072,128]{1,0:T(8,128)(2,1)S(1)}, u32[]{:S(2)}, u32[]{:S(2)}) %collective-permute-start.1) | collective-permute-done | bytes 786464 | tf_op jit(solution)/shard_map/ppermute | solution.py:365
  17.0 0.6 shard_map.124
  17.6 1.7 %collective-permute-start.2 = (bf16[60,48,128]{2,1,0:T(8,128)(2,1)S(1)}, bf16[60,48,128]{2,1,0:T(8,128)(2,1)S(1)}, u32[]{:S(2)}, u32[]{:S(2)}) collective-permute-start(bf16[60,48,128]{2,1,0:T(8,128)(2,1)S(1)} %get-tuple-element.21.own_ref), channel_id=1, source_target_pairs={{0,8},{8,0},{16,24},{24,16},{32,40},{40,32},{48,56},{56,48},{64,72... | collective-permute-start | bytes 2211848 | tf_op jit(solution)/shard_map/ppermute | solution.py:376
  19.3 1.7 %collective-permute-start.3 = (bf16[60,48,128]{2,1,0:T(8,128)(2,1)S(1)}, bf16[60,48,128]{2,1,0:T(8,128)(2,1)S(1)}, u32[]{:S(2)}, u32[]{:S(2)}) collective-permute-start(bf16[60,48,128]{2,1,0:T(8,128)(2,1)S(1)} %get-tuple-element.22), channel_id=1, source_target_pairs={{0,1},{1,0},{2,3},{3,2},{4,5},{5,4},{6,7},{7,6},{8,16},{9,17},{10,... | collective-permute-start | bytes 2211848 | tf_op jit(solution)/shard_map/ppermute | solution.py:376
  21.0 1.5 %collective-permute-done.4.even_ref = bf16[48,48,128]{2,1,0:T(8,128)(2,1)S(1)} collective-permute-done((bf16[48,48,128]{2,1,0:T(8,128)(2,1)S(1)}, bf16[48,48,128]{2,1,0:T(8,128)(2,1)S(1)}, u32[]{:S(2)}, u32[]{:S(2)}) %collective-permute-start.4) | collective-permute-done | bytes 589856 | tf_op jit(solution)/shard_map/ppermute | solution.py:376
  22.5 3.4 %collective-permute-done.5.odd_ref = bf16[48,48,128]{2,1,0:T(8,128)(2,1)S(1)} collective-permute-done((bf16[48,48,128]{2,1,0:T(8,128)(2,1)S(1)}, bf16[48,48,128]{2,1,0:T(8,128)(2,1)S(1)}, u32[]{:S(2)}, u32[]{:S(2)}) %collective-permute-start.5) | collective-permute-done | bytes 589856 | tf_op jit(solution)/shard_map/ppermute | solution.py:376
  25.9 1.0 shard_map.125.own_ref
  26.9 0.0 copy-start.7
  26.9 0.1 collective-permute-start.6
  27.0 0.5 collective-permute-start.7
  27.5 1.5 %collective-permute-done.6.even_ref = bf16[48,48,128]{2,1,0:T(8,128)(2,1)S(1)} collective-permute-done((bf16[48,48,128]{2,1,0:T(8,128)(2,1)S(1)}, bf16[48,48,128]{2,1,0:T(8,128)(2,1)S(1)}, u32[]{:S(2)}, u32[]{:S(2)}) %collective-permute-start.6) | collective-permute-done | bytes 589856 | tf_op jit(solution)/shard_map/ppermute | solution.py:365
  29.0 8.6 %collective-permute-done.7.odd_ref = bf16[48,48,128]{2,1,0:T(8,128)(2,1)S(1)} collective-permute-done((bf16[48,48,128]{2,1,0:T(8,128)(2,1)S(1)}, bf16[48,48,128]{2,1,0:T(8,128)(2,1)S(1)}, u32[]{:S(2)}, u32[]{:S(2)}) %collective-permute-start.7) | collective-permute-done | bytes 589856 | tf_op jit(solution)/shard_map/ppermute | solution.py:365
  37.6 0.0 copy-done
  37.6 0.0 copy-done.6
  37.6 1.1 shard_map.126.first_ref
  38.7 0.0 collective-permute-done.2.even_ref
  38.7 1.7 %collective-permute-done.3.odd_ref = bf16[60,48,128]{2,1,0:T(8,128)(2,1)S(1)} collective-permute-done((bf16[60,48,128]{2,1,0:T(8,128)(2,1)S(1)}, bf16[60,48,128]{2,1,0:T(8,128)(2,1)S(1)}, u32[]{:S(2)}, u32[]{:S(2)}) %collective-permute-start.3) | collective-permute-done | bytes 737312 | tf_op jit(solution)/shard_map/ppermute | solution.py:376
  40.4 0.0 copy-done.7
  40.4 1.8 %shard_map.127 = (f32[48,48,128]{2,1,0:T(8,128)S(1)}, bf16[48,48,128]{2,1,0:T(8,128)(2,1)S(1)}) custom-call(f32[8,256]{1,0:T(8,128)S(1)} %shard_map.122.taps_ref, bf16[60,48,128]{2,1,0:T(8,128)(2,1)S(1)} %get-tuple-element.21.own_ref, bf16[60,48,128]{2,1,0:T(8,128)(2,1)S(1)} %collective-permute-done.2.even_ref, ...), custom_call_target="tpu_custom_call" | custom-call | flops 1000000000 | bytes 6709248 | tf_op jit(solution)/shard_map/pallas_call | solution.py:26
  42.2 6.4 %collective-permute-start.8 = (bf16[48,48,128]{2,1,0:T(8,128)(2,1)S(1)}, bf16[48,48,128]{2,1,0:T(8,128)(2,1)S(1)}, u32[]{:S(2)}, u32[]{:S(2)}) collective-permute-start(bf16[48,48,128]{2,1,0:T(8,128)(2,1)S(1)} %get-tuple-element.26), channel_id=1, source_target_pairs={{0,128},{128,0},{1,129},{129,1},{2,130},{130,2},{3,131},{131,3},{4... | collective-permute-start | bytes 1769480 | tf_op jit(solution)/shard_map/ppermute | solution.py:428
  48.6 25.0 %collective-permute-done.8.came_ref = bf16[48,48,128]{2,1,0:T(8,128)(2,1)S(1)} collective-permute-done((bf16[48,48,128]{2,1,0:T(8,128)(2,1)S(1)}, bf16[48,48,128]{2,1,0:T(8,128)(2,1)S(1)}, u32[]{:S(2)}, u32[]{:S(2)}) %collective-permute-start.8) | collective-permute-done | bytes 589856 | tf_op jit(solution)/shard_map/ppermute | solution.py:428
  73.6 0.0 copy-done.4
  73.6 0.0 copy-done.5
  73.6 1.3 %shard_map.128 = (bf16[60,48,128]{2,1,0:T(8,128)(2,1)S(1)}, bf16[60,48,128]{2,1,0:T(8,128)(2,1)S(1)}, bf16[24,48,128]{2,1,0:T(8,128)(2,1)S(1)}, bf16[48,48,128]{2,1,0:T(8,128)(2,1)S(1)}) custom-call(f32[48,48,128]{2,1,0:T(8,128)S(1)} %get-tuple-element.25.kept_ref, bf16[48,48,128]{2,1,0:T(8,128)(2,1)S(1)} %collective-permute-done.8.came_ref, ...), custom_call_target="tpu_custom_call" | custom-call | flops 400000000 | bytes 6553600 | tf_op jit(solution)/shard_map/pallas_call | solution.py:26
  74.9 0.1 collective-permute-start.9
  75.0 1.3 %collective-permute-start.10 = (bf16[60,48,128]{2,1,0:T(8,128)(2,1)S(1)}, bf16[60,48,128]{2,1,0:T(8,128)(2,1)S(1)}, u32[]{:S(2)}, u32[]{:S(2)}) collective-permute-start(bf16[60,48,128]{2,1,0:T(8,128)(2,1)S(1)} %get-tuple-element.29), channel_id=1, source_target_pairs={{0,1},{1,0},{2,3},{3,2},{4,5},{5,4},{6,7},{7,6},{8,16},{9,17},{10,... | collective-permute-start | bytes 2211848 | tf_op jit(solution)/shard_map/ppermute | solution.py:376
  76.3 0.0 collective-permute-start.11
  76.3 3.1 %collective-permute-start.12 = (bf16[48,48,128]{2,1,0:T(8,128)(2,1)S(1)}, bf16[48,48,128]{2,1,0:T(8,128)(2,1)S(1)}, u32[]{:S(2)}, u32[]{:S(2)}) collective-permute-start(bf16[48,48,128]{2,1,0:T(8,128)(2,1)S(1)} %get-tuple-element.30.own_ref), channel_id=1, source_target_pairs={{0,7},{1,2},{2,1},{3,4},{4,3},{5,6},{6,5},{7,0},{8,15},{9,10},{10,... | collective-permute-start | bytes 1769480 | tf_op jit(solution)/shard_map/ppermute | solution.py:365
  79.4 0.0 collective-permute-done.11.even_ref
  79.4 7.6 %collective-permute-done.12.odd_ref = bf16[48,48,128]{2,1,0:T(8,128)(2,1)S(1)} collective-permute-done((bf16[48,48,128]{2,1,0:T(8,128)(2,1)S(1)}, bf16[48,48,128]{2,1,0:T(8,128)(2,1)S(1)}, u32[]{:S(2)}, u32[]{:S(2)}) %collective-permute-start.12) | collective-permute-done | bytes 589856 | tf_op jit(solution)/shard_map/ppermute | solution.py:365
  87.0 0.4 shard_map.129.after_ref.own_ref
  87.4 1.9 %collective-permute-start.15 = (bf16[48,48,128]{2,1,0:T(8,128)(2,1)S(1)}, bf16[48,48,128]{2,1,0:T(8,128)(2,1)S(1)}, u32[]{:S(2)}, u32[]{:S(2)}) collective-permute-start(bf16[48,48,128]{2,1,0:T(8,128)(2,1)S(1)} %shard_map.129.after_ref.own_ref), channel_id=1, source_target_pairs={{0,8},{8,0},{16,24},{24,16},{32,40},{40,32},{48,56},{56,48},{64,72... | collective-permute-start | bytes 1769480 | tf_op jit(solution)/shard_map/ppermute | solution.py:376
  89.3 1.4 %collective-permute-start.16 = (bf16[48,48,128]{2,1,0:T(8,128)(2,1)S(1)}, bf16[48,48,128]{2,1,0:T(8,128)(2,1)S(1)}, u32[]{:S(2)}, u32[]{:S(2)}) collective-permute-start(bf16[48,48,128]{2,1,0:T(8,128)(2,1)S(1)} %shard_map.129.after_ref.own_ref), channel_id=1, source_target_pairs={{0,1},{1,0},{2,3},{3,2},{4,5},{5,4},{6,7},{7,6},{8,16},{9,17},{10,... | collective-permute-start | bytes 1769480 | tf_op jit(solution)/shard_map/ppermute | solution.py:376
  90.7 1.9 %collective-permute-done.9.even_ref = bf16[60,48,128]{2,1,0:T(8,128)(2,1)S(1)} collective-permute-done((bf16[60,48,128]{2,1,0:T(8,128)(2,1)S(1)}, bf16[60,48,128]{2,1,0:T(8,128)(2,1)S(1)}, u32[]{:S(2)}, u32[]{:S(2)}) %collective-permute-start.9) | collective-permute-done | bytes 737312 | tf_op jit(solution)/shard_map/ppermute | solution.py:376
  92.6 1.1 collective-permute-done.10.odd_ref
  93.7 1.5 %shard_map.130 = (bf16[64,48,128]{2,1,0:T(8,128)(2,1)S(1)}, bf16[64,48,128]{2,1,0:T(8,128)(2,1)S(1)}, bf16[24,48,128]{2,1,0:T(8,128)(2,1)S(1)}) custom-call(f32[8,256]{1,0:T(8,128)S(1)} %shard_map.122.taps_ref, bf16[60,48,128]{2,1,0:T(8,128)(2,1)S(1)} %get-tuple-element.27.sent_ref, bf16[24,48,128]{2,1,0:T(8,128)(2,1)S(1)} %get-tuple-element.28.own_ref, ...), custom_call_target="tpu_custom_call" | custom-call | flops 20000000000 | bytes 4972544 | tf_op jit(solution)/shard_map/pallas_call | solution.py:26
  95.2 0.1 collective-permute-start.13
  95.3 5.5 %collective-permute-start.14 = (bf16[64,48,128]{2,1,0:T(8,128)(2,1)S(1)}, bf16[64,48,128]{2,1,0:T(8,128)(2,1)S(1)}, u32[]{:S(2)}, u32[]{:S(2)}) collective-permute-start(bf16[64,48,128]{2,1,0:T(8,128)(2,1)S(1)} %get-tuple-element.32), channel_id=1, source_target_pairs={{0,7},{1,2},{2,1},{3,4},{4,3},{5,6},{6,5},{7,0},{8,15},{9,10},{10,... | collective-permute-start | bytes 2359304 | tf_op jit(solution)/shard_map/ppermute | solution.py:365
  100.9 3.2 %collective-permute-done.15.even_ref = bf16[48,48,128]{2,1,0:T(8,128)(2,1)S(1)} collective-permute-done((bf16[48,48,128]{2,1,0:T(8,128)(2,1)S(1)}, bf16[48,48,128]{2,1,0:T(8,128)(2,1)S(1)}, u32[]{:S(2)}, u32[]{:S(2)}) %collective-permute-start.15) | collective-permute-done | bytes 589856 | tf_op jit(solution)/shard_map/ppermute | solution.py:376
  104.1 2.3 %collective-permute-done.16.odd_ref = bf16[48,48,128]{2,1,0:T(8,128)(2,1)S(1)} collective-permute-done((bf16[48,48,128]{2,1,0:T(8,128)(2,1)S(1)}, bf16[48,48,128]{2,1,0:T(8,128)(2,1)S(1)}, u32[]{:S(2)}, u32[]{:S(2)}) %collective-permute-start.16) | collective-permute-done | bytes 589856 | tf_op jit(solution)/shard_map/ppermute | solution.py:376
  106.5 0.0 copy-done.2
  106.5 1.7 %shard_map.131.begun_ref = bf16[2,48,48,128]{3,2,1,0:T(8,128)(2,1)} custom-call(f32[8,256]{1,0:T(8,128)S(1)} %shard_map.122.taps_ref, bf16[48,48,128]{2,1,0:T(8,128)(2,1)S(1)} %shard_map.129.after_ref.own_ref, bf16[48,48,128]{2,1,0:T(8,128)(2,1)S(1)} %collective-permute-done.15.even_ref, bf16[48,48,128]{2,1,0:T(8,128)(2,1)S(1)} %collective-permute-done.16.odd_ref, ...), custom_call_target="tpu_custom_call" | custom-call | flops 20000000000 | bytes 4136960 | tf_op jit(solution)/shard_map/pallas_call | solution.py:26
  108.2 0.0 collective-permute-done.13.even_ref
  108.2 2.3 %collective-permute-done.14.odd_ref = bf16[64,48,128]{2,1,0:T(8,128)(2,1)S(1)} collective-permute-done((bf16[64,48,128]{2,1,0:T(8,128)(2,1)S(1)}, bf16[64,48,128]{2,1,0:T(8,128)(2,1)S(1)}, u32[]{:S(2)}, u32[]{:S(2)}) %collective-permute-start.14) | collective-permute-done | bytes 786464 | tf_op jit(solution)/shard_map/ppermute | solution.py:365
  110.5 1.6 %shard_map.132 = (bf16[48,48,64]{2,1,0:T(8,128)(2,1)}, bf16[2,48,48,128]{3,2,1,0:T(8,128)(2,1)}) custom-call(f32[8,256]{1,0:T(8,128)S(1)} %shard_map.122.taps_ref, bf16[64,48,128]{2,1,0:T(8,128)(2,1)S(1)} %get-tuple-element.31.own_ref, bf16[64,48,128]{2,1,0:T(8,128)(2,1)S(1)} %collective-permute-done.13.even_ref, ...), custom_call_target="tpu_custom_call", output_to_operand_aliasing={{1}: (7, {})} | custom-call | flops 700000000 | bytes 6791168 | tf_op jit(solution)/shard_map/pallas_call | solution.py:26
  (5 shorter events, 0.0 us)
Async XLA Ops:
  0.6 1.3 %copy-start.1 = (bf16[2,48,48,128]{3,2,1,0:T(8,128)(2,1)S(1)}, bf16[2,48,48,128]{3,2,1,0:T(8,128)(2,1)}, u32[]{:S(2)}) copy-start(bf16[2,48,48,128]{3,2,1,0:T(8,128)(2,1)} %member_ref.5) | copy-start | bytes 3538948
  1.9 1.1 copy-start.3
  3.0 7.4 %copy-start.8 = (bf16[97]{0:T(256)(128)(2,1)S(1)}, bf16[97]{0:T(256)(128)(2,1)}, u32[]{:S(2)}) copy-start(bf16[97]{0:T(256)(128)(2,1)} %lx_ref.1) | copy-start | bytes 586
  3.0 7.4 %copy-start.9 = (bf16[97]{0:T(256)(128)(2,1)S(1)}, bf16[97]{0:T(256)(128)(2,1)}, u32[]{:S(2)}) copy-start(bf16[97]{0:T(256)(128)(2,1)} %ly_ref.1) | copy-start | bytes 586
  3.0 7.4 %copy-start.10 = (bf16[49]{0:T(256)(128)(2,1)S(1)}, bf16[49]{0:T(256)(128)(2,1)}, u32[]{:S(2)}) copy-start(bf16[49]{0:T(256)(128)(2,1)} %sx_ref.1) | copy-start | bytes 298
  3.0 7.4 %copy-start.11 = (bf16[49]{0:T(256)(128)(2,1)S(1)}, bf16[49]{0:T(256)(128)(2,1)}, u32[]{:S(2)}) copy-start(bf16[49]{0:T(256)(128)(2,1)} %sy_ref.1) | copy-start | bytes 298
  4.1 6.5 %collective-permute-start = (bf16[3072,128]{1,0:T(8,128)(2,1)S(1)}, bf16[3072,128]{1,0:T(8,128)(2,1)S(1)}, u32[]{:S(2)}, u32[]{:S(2)}) collective-permute-start(bf16[3072,128]{1,0:T(8,128)(2,1)S(1)} %get-tuple-element.18.sent_ref), channel_id=1, source_target_pairs={{0,1},{1,0},{2,3},{3,2},{4,5},{5,4},{6,7},{7,6},{8,9},{9,8},{10,11... | collective-permute-start | bytes 2359304 | tf_op jit(solution)/shard_map/ppermute | solution.py:365
  4.2 12.7 %collective-permute-start.1 = (bf16[3072,128]{1,0:T(8,128)(2,1)S(1)}, bf16[3072,128]{1,0:T(8,128)(2,1)S(1)}, u32[]{:S(2)}, u32[]{:S(2)}) collective-permute-start(bf16[3072,128]{1,0:T(8,128)(2,1)S(1)} %get-tuple-element.20), channel_id=1, source_target_pairs={{0,7},{1,2},{2,1},{3,4},{4,3},{5,6},{6,5},{7,0},{8,15},{9,10},{10,... | collective-permute-start | bytes 2359304 | tf_op jit(solution)/shard_map/ppermute | solution.py:365
  7.1 15.4 %collective-permute-start.4 = (bf16[48,48,128]{2,1,0:T(8,128)(2,1)S(1)}, bf16[48,48,128]{2,1,0:T(8,128)(2,1)S(1)}, u32[]{:S(2)}, u32[]{:S(2)}) collective-permute-start(bf16[48,48,128]{2,1,0:T(8,128)(2,1)S(1)} %get-tuple-element.24.own_ref), channel_id=1, source_target_pairs={{0,8},{8,0},{16,24},{24,16},{32,40},{40,32},{48,56},{56,48},{64,72... | collective-permute-start | bytes 1769480 | tf_op jit(solution)/shard_map/ppermute | solution.py:376
  8.7 17.2 %collective-permute-start.5 = (bf16[48,48,128]{2,1,0:T(8,128)(2,1)S(1)}, bf16[48,48,128]{2,1,0:T(8,128)(2,1)S(1)}, u32[]{:S(2)}, u32[]{:S(2)}) collective-permute-start(bf16[48,48,128]{2,1,0:T(8,128)(2,1)S(1)} %get-tuple-element.24.own_ref), channel_id=1, source_target_pairs={{0,1},{1,0},{2,3},{3,2},{4,5},{5,4},{6,7},{7,6},{8,16},{9,17},{10,... | collective-permute-start | bytes 1769480 | tf_op jit(solution)/shard_map/ppermute | solution.py:376
  17.6 21.1 %collective-permute-start.2 = (bf16[60,48,128]{2,1,0:T(8,128)(2,1)S(1)}, bf16[60,48,128]{2,1,0:T(8,128)(2,1)S(1)}, u32[]{:S(2)}, u32[]{:S(2)}) collective-permute-start(bf16[60,48,128]{2,1,0:T(8,128)(2,1)S(1)} %get-tuple-element.21.own_ref), channel_id=1, source_target_pairs={{0,8},{8,0},{16,24},{24,16},{32,40},{40,32},{48,56},{56,48},{64,72... | collective-permute-start | bytes 2211848 | tf_op jit(solution)/shard_map/ppermute | solution.py:376
  19.2 18.4 %copy-start = (bf16[2,48,48,128]{3,2,1,0:T(8,128)(2,1)S(1)}, bf16[2,48,48,128]{3,2,1,0:T(8,128)(2,1)}, u32[]{:S(2)}) copy-start(bf16[2,48,48,128]{3,2,1,0:T(8,128)(2,1)} %pert_ref.5) | copy-start | bytes 3538948
  19.3 18.4 %copy-start.6 = (bf16[128,128]{1,0:T(8,128)(2,1)S(1)}, bf16[128,128]{1,0:T(8,128)(2,1)}, u32[]{:S(2)}) copy-start(bf16[128,128]{1,0:T(8,128)(2,1)} %vert_ref.5) | copy-start | bytes 98308
  19.3 21.1 %collective-permute-start.3 = (bf16[60,48,128]{2,1,0:T(8,128)(2,1)S(1)}, bf16[60,48,128]{2,1,0:T(8,128)(2,1)S(1)}, u32[]{:S(2)}, u32[]{:S(2)}) collective-permute-start(bf16[60,48,128]{2,1,0:T(8,128)(2,1)S(1)} %get-tuple-element.22), channel_id=1, source_target_pairs={{0,1},{1,0},{2,3},{3,2},{4,5},{5,4},{6,7},{7,6},{8,16},{9,17},{10,... | collective-permute-start | bytes 2211848 | tf_op jit(solution)/shard_map/ppermute | solution.py:376
  26.9 13.5 %copy-start.7 = (bf16[128,128]{1,0:T(8,128)(2,1)S(1)}, bf16[128,128]{1,0:T(8,128)(2,1)}, u32[]{:S(2)}) copy-start(bf16[128,128]{1,0:T(8,128)(2,1)} %static_ref.5) | copy-start | bytes 98308
  26.9 2.1 %collective-permute-start.6 = (bf16[48,48,128]{2,1,0:T(8,128)(2,1)S(1)}, bf16[48,48,128]{2,1,0:T(8,128)(2,1)S(1)}, u32[]{:S(2)}, u32[]{:S(2)}) collective-permute-start(bf16[48,48,128]{2,1,0:T(8,128)(2,1)S(1)} %shard_map.125.own_ref), channel_id=1, source_target_pairs={{0,1},{1,0},{2,3},{3,2},{4,5},{5,4},{6,7},{7,6},{8,9},{9,8},{10,11... | collective-permute-start | bytes 1769480 | tf_op jit(solution)/shard_map/ppermute | solution.py:365
  27.0 10.6 %collective-permute-start.7 = (bf16[48,48,128]{2,1,0:T(8,128)(2,1)S(1)}, bf16[48,48,128]{2,1,0:T(8,128)(2,1)S(1)}, u32[]{:S(2)}, u32[]{:S(2)}) collective-permute-start(bf16[48,48,128]{2,1,0:T(8,128)(2,1)S(1)} %shard_map.125.own_ref), channel_id=1, source_target_pairs={{0,7},{1,2},{2,1},{3,4},{4,3},{5,6},{6,5},{7,0},{8,15},{9,10},{10,... | collective-permute-start | bytes 1769480 | tf_op jit(solution)/shard_map/ppermute | solution.py:365
  40.4 33.2 %copy-start.4 = (bf16[48,48,128]{2,1,0:T(8,128)(2,1)S(1)}, bf16[48,48,128]{2,1,0:T(8,128)(2,1)}, u32[]{:S(2)}) copy-start(bf16[48,48,128]{2,1,0:T(8,128)(2,1)} %dep_ref.1) | copy-start | bytes 1769476
  40.4 33.2 %copy-start.5 = (bf16[48,48,128]{2,1,0:T(8,128)(2,1)S(1)}, bf16[48,48,128]{2,1,0:T(8,128)(2,1)}, u32[]{:S(2)}) copy-start(bf16[48,48,128]{2,1,0:T(8,128)(2,1)} %weight_ref.1) | copy-start | bytes 1769476
  42.2 31.3 %collective-permute-start.8 = (bf16[48,48,128]{2,1,0:T(8,128)(2,1)S(1)}, bf16[48,48,128]{2,1,0:T(8,128)(2,1)S(1)}, u32[]{:S(2)}, u32[]{:S(2)}) collective-permute-start(bf16[48,48,128]{2,1,0:T(8,128)(2,1)S(1)} %get-tuple-element.26), channel_id=1, source_target_pairs={{0,128},{128,0},{1,129},{129,1},{2,130},{130,2},{3,131},{131,3},{4... | collective-permute-start | bytes 1769480 | tf_op jit(solution)/shard_map/ppermute | solution.py:428
  74.9 17.7 %collective-permute-start.9 = (bf16[60,48,128]{2,1,0:T(8,128)(2,1)S(1)}, bf16[60,48,128]{2,1,0:T(8,128)(2,1)S(1)}, u32[]{:S(2)}, u32[]{:S(2)}) collective-permute-start(bf16[60,48,128]{2,1,0:T(8,128)(2,1)S(1)} %get-tuple-element.27.sent_ref), channel_id=1, source_target_pairs={{0,8},{8,0},{16,24},{24,16},{32,40},{40,32},{48,56},{56,48},{64,72... | collective-permute-start | bytes 2211848 | tf_op jit(solution)/shard_map/ppermute | solution.py:376
  75.0 18.7 %collective-permute-start.10 = (bf16[60,48,128]{2,1,0:T(8,128)(2,1)S(1)}, bf16[60,48,128]{2,1,0:T(8,128)(2,1)S(1)}, u32[]{:S(2)}, u32[]{:S(2)}) collective-permute-start(bf16[60,48,128]{2,1,0:T(8,128)(2,1)S(1)} %get-tuple-element.29), channel_id=1, source_target_pairs={{0,1},{1,0},{2,3},{3,2},{4,5},{5,4},{6,7},{7,6},{8,16},{9,17},{10,... | collective-permute-start | bytes 2211848 | tf_op jit(solution)/shard_map/ppermute | solution.py:376
  76.3 3.1 %collective-permute-start.11 = (bf16[48,48,128]{2,1,0:T(8,128)(2,1)S(1)}, bf16[48,48,128]{2,1,0:T(8,128)(2,1)S(1)}, u32[]{:S(2)}, u32[]{:S(2)}) collective-permute-start(bf16[48,48,128]{2,1,0:T(8,128)(2,1)S(1)} %get-tuple-element.30.own_ref), channel_id=1, source_target_pairs={{0,1},{1,0},{2,3},{3,2},{4,5},{5,4},{6,7},{7,6},{8,9},{9,8},{10,11... | collective-permute-start | bytes 1769480 | tf_op jit(solution)/shard_map/ppermute | solution.py:365
  76.3 10.6 %collective-permute-start.12 = (bf16[48,48,128]{2,1,0:T(8,128)(2,1)S(1)}, bf16[48,48,128]{2,1,0:T(8,128)(2,1)S(1)}, u32[]{:S(2)}, u32[]{:S(2)}) collective-permute-start(bf16[48,48,128]{2,1,0:T(8,128)(2,1)S(1)} %get-tuple-element.30.own_ref), channel_id=1, source_target_pairs={{0,7},{1,2},{2,1},{3,4},{4,3},{5,6},{6,5},{7,0},{8,15},{9,10},{10,... | collective-permute-start | bytes 1769480 | tf_op jit(solution)/shard_map/ppermute | solution.py:365
  87.4 16.7 %collective-permute-start.15 = (bf16[48,48,128]{2,1,0:T(8,128)(2,1)S(1)}, bf16[48,48,128]{2,1,0:T(8,128)(2,1)S(1)}, u32[]{:S(2)}, u32[]{:S(2)}) collective-permute-start(bf16[48,48,128]{2,1,0:T(8,128)(2,1)S(1)} %shard_map.129.after_ref.own_ref), channel_id=1, source_target_pairs={{0,8},{8,0},{16,24},{24,16},{32,40},{40,32},{48,56},{56,48},{64,72... | collective-permute-start | bytes 1769480 | tf_op jit(solution)/shard_map/ppermute | solution.py:376
  89.3 17.2 %collective-permute-start.16 = (bf16[48,48,128]{2,1,0:T(8,128)(2,1)S(1)}, bf16[48,48,128]{2,1,0:T(8,128)(2,1)S(1)}, u32[]{:S(2)}, u32[]{:S(2)}) collective-permute-start(bf16[48,48,128]{2,1,0:T(8,128)(2,1)S(1)} %shard_map.129.after_ref.own_ref), channel_id=1, source_target_pairs={{0,1},{1,0},{2,3},{3,2},{4,5},{5,4},{6,7},{7,6},{8,16},{9,17},{10,... | collective-permute-start | bytes 1769480 | tf_op jit(solution)/shard_map/ppermute | solution.py:376
  93.7 12.8 %copy-start.2 = (bf16[2,48,48,128]{3,2,1,0:T(8,128)(2,1)S(1)}, bf16[2,48,48,128]{3,2,1,0:T(8,128)(2,1)}, u32[]{:S(2)}) copy-start(bf16[2,48,48,128]{3,2,1,0:T(8,128)(2,1)} %member_ref.5) | copy-start | bytes 3538948
  95.2 13.0 %collective-permute-start.13 = (bf16[64,48,128]{2,1,0:T(8,128)(2,1)S(1)}, bf16[64,48,128]{2,1,0:T(8,128)(2,1)S(1)}, u32[]{:S(2)}, u32[]{:S(2)}) collective-permute-start(bf16[64,48,128]{2,1,0:T(8,128)(2,1)S(1)} %get-tuple-element.31.own_ref), channel_id=1, source_target_pairs={{0,1},{1,0},{2,3},{3,2},{4,5},{5,4},{6,7},{7,6},{8,9},{9,8},{10,11... | collective-permute-start | bytes 2359304 | tf_op jit(solution)/shard_map/ppermute | solution.py:365
  95.3 15.2 %collective-permute-start.14 = (bf16[64,48,128]{2,1,0:T(8,128)(2,1)S(1)}, bf16[64,48,128]{2,1,0:T(8,128)(2,1)S(1)}, u32[]{:S(2)}, u32[]{:S(2)}) collective-permute-start(bf16[64,48,128]{2,1,0:T(8,128)(2,1)S(1)} %get-tuple-element.32), channel_id=1, source_target_pairs={{0,7},{1,2},{2,1},{3,4},{4,3},{5,6},{6,5},{7,0},{8,15},{9,10},{10,... | collective-permute-start | bytes 2359304 | tf_op jit(solution)/shard_map/ppermute | solution.py:365

commit v3 on v2

--- a/solution.py
+++ b/solution.py
@@ -143,20 +143,12 @@
     odd_ref[TILE:] = pick(odd, right, left)
 
 
-def pack_kernel(member_ref, static_ref, first_ref, even_ref, odd_ref, own_ref, static, sems):
-    copies = [
-        pltpu.make_async_copy(static_ref.at[pl.ds(12 * i, 12)], static.at[pl.ds(12 * i, 12)], sems.at[i])
-        for i in range(4)
-    ]
-    for copy in copies:
-        copy.start()
+def pack_kernel(member_ref, static_ref, first_ref, even_ref, odd_ref, own_ref):
     first_ref[...] = member_ref[0]
     second = member_ref[1].reshape(2304, 128)
     even_ref[:2304] = second
     odd_ref[:2304] = second
-    for copy in copies:
-        copy.wait()
-    packed = halves(static[...])
+    packed = halves(static_ref[...])
     own_ref[...] = packed
     pack_slabs(packed, even_ref, odd_ref)
 
@@ -332,16 +324,12 @@
     rows, taps_ref, own_ref, even_ref, odd_ref, s_ref, member_ref, control_ref, begun_ref,
     static_out, member_out, static, member, sems
 ):
-    def store(x, out):
-        member[x] = (member_ref[0, x].astype(F32) + out.astype(BF).astype(F32)).astype(BF)
-
-    second_y(rows[0], taps_ref, own_ref, even_ref, odd_ref, store)
-    copies = [
-        pltpu.make_async_copy(member.at[pl.ds(24 * i, 24)], member_out.at[0, pl.ds(24 * i, 24)], sems.at[i])
-        for i in range(2)
-    ]
-    for copy in copies:
-        copy.start()
+    copies = []
+
+    def send(source, target):
+        copies.append(pltpu.make_async_copy(source, target, sems.at[len(copies)]))
+        copies[-1].start()
+
     matrix = band(taps_ref[rows[1] : rows[1] + 1], TILE, 112)
     slabs = [r[TILE:].reshape(24, SLAB, 128) for r in (even_ref, odd_ref)]
     left, right = sides(slabs[0], slabs[1], "ty")
@@ -352,8 +340,23 @@
             both = (control_ref[x + k].astype(F32) + out[:, 128 * k : 128 * k + 128]).astype(BF)
             static[x + k] = both[:, :64]
             static[x + k + 24] = both[:, 64:]
-    copies.append(pltpu.make_async_copy(static, static_out, sems.at[2]))
-    copies[2].start()
+        if x % 12 == 10:
+            for part in (pl.ds(x - 10, 12), pl.ds(x + 14, 12)):
+                send(static.at[part], static_out.at[part])
+    matrix = band_swapped(taps_ref[rows[0] : rows[0] + 1], "ty")
+    for first in range(0, TILE, 12):
+
+        def line(x):
+            x = first + x
+            return jnp.concatenate([even_ref[x], own_ref[x], odd_ref[x]], axis=0)
+
+        def store(x, out):
+            x = first + x
+            member[x] = (member_ref[0, x].astype(F32) + out.astype(BF).astype(F32)).astype(BF)
+
+        along_y(matrix, line, 12, store)
+        part = pl.ds(first, 12)
+        send(member.at[part], member_out.at[0, part])
     for copy in copies:
         copy.wait()
 
@@ -412,8 +415,7 @@
     sent_shapes = (shape(3072, 128), shape(3072, 128), shape(24, TILE, 128))
 
     a, to_even, to_odd, control = call(
-        pack_kernel, (shape(*tile),) + sent_shapes, (member_control, static_control), 1_000_000,
-        [pltpu.VMEM((TILE, TILE, 64), BF), pltpu.SemaphoreType.DMA((4,))], in_any=(1,),
+        pack_kernel, (shape(*tile),) + sent_shapes, (member_control, static_control), 1_000_000
     )
     a, b = first_filters(taps, a, to_even, to_odd, control)
     (first,) = call(
@@ -447,7 +449,7 @@
     args = (taps,) + a + (member_control, control, begun)
     return tuple(call(
         functools.partial(last_a_kernel, (5, 7)), (shape(TILE, TILE, 64), shape(2, *tile)), args, 700_000_000,
-        [pltpu.VMEM((TILE, TILE, 64), BF), pltpu.VMEM(tile, BF), pltpu.SemaphoreType.DMA((3,))],
+        [pltpu.VMEM((TILE, TILE, 64), BF), pltpu.VMEM(tile, BF), pltpu.SemaphoreType.DMA((8,))],
         in_any=(len(args) - 1,), out_any=(0, 1), aliases={len(args) - 1: 1},
     ))
 

time: 113 us -> 112 us (level)
  no operation moved by 1% of the time
where the time goes in v3:
time: 112 us; the launch traced here: 111 us
  waiting for transfers between devices  66.5 us (59%)
  starting transfers between devices  30 us (27%)
  Pallas kernels  11.5 us (10%)
  local copies, waits for them, and re-layouts  2.37 us (2%)
    ppermute x8, waiting for transfers between devices, swaps_y(): return (lax.ppermute(even, 'ty', first), lax.ppermute(odd, 'ty', second))  26.3 us
    ppermute x1, waiting for transfers between devices, body(): came = lax.ppermute(sent, 'mem', [(i, size - 1 - i) for i in range(size)])  25 us
    ppermute x8, starting transfers between devices, swaps_y(): return (lax.ppermute(even, 'ty', first), lax.ppermute(odd, 'ty', second))  12.3 us
    pallas_call x11, Pallas kernels, call(): pl.pallas_call(kernel, out_shape=outs, in_specs=[ANY if i in in_any else...  11.5 us
    ppermute x4, waiting for transfers between devices, swaps_x(): lax.ppermute(odd, ('tx', 'ty'), second)  8.49 us
    ppermute x4, waiting for transfers between devices, swaps_x(): lax.ppermute(even, 'tx', first)  6.7 us
    ppermute x1, starting transfers between devices, body(): came = lax.ppermute(sent, 'mem', [(i, size - 1 - i) for i in range(size)])  6.38 us
    ppermute x4, starting transfers between devices, swaps_x(): lax.ppermute(odd, ('tx', 'ty'), second)  6.15 us
  transfers between devices with their start and end apart: 17, of which 13 were waited for; matrix products, arithmetic and copies ran while one was open for 0% of the time, Pallas kernels for 6%

profile of v3, /device:TPU:32, one launch (start us, length us, event | category | flops | bytes accessed | tf_op | source)
XLA Modules:
  0.0 111.4 jit_solution(6390976552453755650)
XLA Ops:
  0.6 0.0 copy-start.1
  0.6 1.3 %copy-done.1 = bf16[2,48,48,128]{3,2,1,0:T(8,128)(2,1)S(1)} copy-done((bf16[2,48,48,128]{3,2,1,0:T(8,128)(2,1)S(1)}, bf16[2,48,48,128]{3,2,1,0:T(8,128)(2,1)}, u32[]{:S(2)}) %copy-start.1) | copy-done | bytes 1179672
  1.9 0.0 copy-start.3
  1.9 1.1 copy-done.3
  3.0 0.0 copy-start.8
  3.0 0.0 copy-start.9
  3.0 0.0 copy-start.10
  3.0 0.0 copy-start.11
  3.0 0.3 shard_map.123
  3.3 0.1 collective-permute-start
  3.4 2.9 %collective-permute-start.1 = (bf16[3072,128]{1,0:T(8,128)(2,1)S(1)}, bf16[3072,128]{1,0:T(8,128)(2,1)S(1)}, u32[]{:S(2)}, u32[]{:S(2)}) collective-permute-start(bf16[3072,128]{1,0:T(8,128)(2,1)S(1)} %get-tuple-element.20), channel_id=1, source_target_pairs={{0,7},{1,2},{2,1},{3,4},{4,3},{5,6},{6,5},{7,0},{8,15},{9,10},{10,... | collective-permute-start | bytes 2359304 | tf_op jit(solution)/shard_map/ppermute | solution.py:368
  6.3 1.6 %collective-permute-start.4 = (bf16[48,48,128]{2,1,0:T(8,128)(2,1)S(1)}, bf16[48,48,128]{2,1,0:T(8,128)(2,1)S(1)}, u32[]{:S(2)}, u32[]{:S(2)}) collective-permute-start(bf16[48,48,128]{2,1,0:T(8,128)(2,1)S(1)} %get-tuple-element.24.own_ref), channel_id=1, source_target_pairs={{0,8},{8,0},{16,24},{24,16},{32,40},{40,32},{48,56},{56,48},{64,72... | collective-permute-start | bytes 1769480 | tf_op jit(solution)/shard_map/ppermute | solution.py:379
  7.9 1.7 %collective-permute-start.5 = (bf16[48,48,128]{2,1,0:T(8,128)(2,1)S(1)}, bf16[48,48,128]{2,1,0:T(8,128)(2,1)S(1)}, u32[]{:S(2)}, u32[]{:S(2)}) collective-permute-start(bf16[48,48,128]{2,1,0:T(8,128)(2,1)S(1)} %get-tuple-element.24.own_ref), channel_id=1, source_target_pairs={{0,1},{1,0},{2,3},{3,2},{4,5},{5,4},{6,7},{7,6},{8,16},{9,17},{10,... | collective-permute-start | bytes 1769480 | tf_op jit(solution)/shard_map/ppermute | solution.py:379
  9.6 0.0 copy-done.8
  9.6 0.0 copy-done.9
  9.6 0.0 copy-done.10
  9.6 0.0 copy-done.11
  9.6 0.2 shard_map.122.taps_ref
  9.8 0.0 collective-permute-done.even_ref
  9.8 6.4 %collective-permute-done.1.odd_ref = bf16[3072,128]{1,0:T(8,128)(2,1)S(1)} collective-permute-done((bf16[3072,128]{1,0:T(8,128)(2,1)S(1)}, bf16[3072,128]{1,0:T(8,128)(2,1)S(1)}, u32[]{:S(2)}, u32[]{:S(2)}) %collective-permute-start.1) | collective-permute-done | bytes 786464 | tf_op jit(solution)/shard_map/ppermute | solution.py:368
  16.1 0.6 shard_map.124
  16.8 1.7 %collective-permute-start.2 = (bf16[60,48,128]{2,1,0:T(8,128)(2,1)S(1)}, bf16[60,48,128]{2,1,0:T(8,128)(2,1)S(1)}, u32[]{:S(2)}, u32[]{:S(2)}) collective-permute-start(bf16[60,48,128]{2,1,0:T(8,128)(2,1)S(1)} %get-tuple-element.21.own_ref), channel_id=1, source_target_pairs={{0,8},{8,0},{16,24},{24,16},{32,40},{40,32},{48,56},{56,48},{64,72... | collective-permute-start | bytes 2211848 | tf_op jit(solution)/shard_map/ppermute | solution.py:379
  18.4 1.7 %collective-permute-start.3 = (bf16[60,48,128]{2,1,0:T(8,128)(2,1)S(1)}, bf16[60,48,128]{2,1,0:T(8,128)(2,1)S(1)}, u32[]{:S(2)}, u32[]{:S(2)}) collective-permute-start(bf16[60,48,128]{2,1,0:T(8,128)(2,1)S(1)} %get-tuple-element.22), channel_id=1, source_target_pairs={{0,1},{1,0},{2,3},{3,2},{4,5},{5,4},{6,7},{7,6},{8,16},{9,17},{10,... | collective-permute-start | bytes 2211848 | tf_op jit(solution)/shard_map/ppermute | solution.py:379
  20.2 1.5 %collective-permute-done.4.even_ref = bf16[48,48,128]{2,1,0:T(8,128)(2,1)S(1)} collective-permute-done((bf16[48,48,128]{2,1,0:T(8,128)(2,1)S(1)}, bf16[48,48,128]{2,1,0:T(8,128)(2,1)S(1)}, u32[]{:S(2)}, u32[]{:S(2)}) %collective-permute-start.4) | collective-permute-done | bytes 589856 | tf_op jit(solution)/shard_map/ppermute | solution.py:379
  21.7 3.4 %collective-permute-done.5.odd_ref = bf16[48,48,128]{2,1,0:T(8,128)(2,1)S(1)} collective-permute-done((bf16[48,48,128]{2,1,0:T(8,128)(2,1)S(1)}, bf16[48,48,128]{2,1,0:T(8,128)(2,1)S(1)}, u32[]{:S(2)}, u32[]{:S(2)}) %collective-permute-start.5) | collective-permute-done | bytes 589856 | tf_op jit(solution)/shard_map/ppermute | solution.py:379
  25.1 1.0 shard_map.125.own_ref
  26.1 0.0 copy-start.7
  26.1 0.1 collective-permute-start.6
  26.2 0.5 collective-permute-start.7
  26.7 1.5 %collective-permute-done.6.even_ref = bf16[48,48,128]{2,1,0:T(8,128)(2,1)S(1)} collective-permute-done((bf16[48,48,128]{2,1,0:T(8,128)(2,1)S(1)}, bf16[48,48,128]{2,1,0:T(8,128)(2,1)S(1)}, u32[]{:S(2)}, u32[]{:S(2)}) %collective-permute-start.6) | collective-permute-done | bytes 589856 | tf_op jit(solution)/shard_map/ppermute | solution.py:368
  28.2 8.6 %collective-permute-done.7.odd_ref = bf16[48,48,128]{2,1,0:T(8,128)(2,1)S(1)} collective-permute-done((bf16[48,48,128]{2,1,0:T(8,128)(2,1)S(1)}, bf16[48,48,128]{2,1,0:T(8,128)(2,1)S(1)}, u32[]{:S(2)}, u32[]{:S(2)}) %collective-permute-start.7) | collective-permute-done | bytes 589856 | tf_op jit(solution)/shard_map/ppermute | solution.py:368
  36.8 0.0 copy-done
  36.8 0.0 copy-done.6
  36.8 1.1 shard_map.126.first_ref
  37.9 0.0 collective-permute-done.2.even_ref
  37.9 1.7 %collective-permute-done.3.odd_ref = bf16[60,48,128]{2,1,0:T(8,128)(2,1)S(1)} collective-permute-done((bf16[60,48,128]{2,1,0:T(8,128)(2,1)S(1)}, bf16[60,48,128]{2,1,0:T(8,128)(2,1)S(1)}, u32[]{:S(2)}, u32[]{:S(2)}) %collective-permute-start.3) | collective-permute-done | bytes 737312 | tf_op jit(solution)/shard_map/ppermute | solution.py:379
  39.6 0.0 copy-done.7
  39.6 1.8 %shard_map.127 = (f32[48,48,128]{2,1,0:T(8,128)S(1)}, bf16[48,48,128]{2,1,0:T(8,128)(2,1)S(1)}) custom-call(f32[8,256]{1,0:T(8,128)S(1)} %shard_map.122.taps_ref, bf16[60,48,128]{2,1,0:T(8,128)(2,1)S(1)} %get-tuple-element.21.own_ref, bf16[60,48,128]{2,1,0:T(8,128)(2,1)S(1)} %collective-permute-done.2.even_ref, ...), custom_call_target="tpu_custom_call" | custom-call | flops 1000000000 | bytes 6709248 | tf_op jit(solution)/shard_map/pallas_call | solution.py:26
  41.4 6.4 %collective-permute-start.8 = (bf16[48,48,128]{2,1,0:T(8,128)(2,1)S(1)}, bf16[48,48,128]{2,1,0:T(8,128)(2,1)S(1)}, u32[]{:S(2)}, u32[]{:S(2)}) collective-permute-start(bf16[48,48,128]{2,1,0:T(8,128)(2,1)S(1)} %get-tuple-element.26), channel_id=1, source_target_pairs={{0,128},{128,0},{1,129},{129,1},{2,130},{130,2},{3,131},{131,3},{4... | collective-permute-start | bytes 1769480 | tf_op jit(solution)/shard_map/ppermute | solution.py:430
  47.8 25.0 %collective-permute-done.8.came_ref = bf16[48,48,128]{2,1,0:T(8,128)(2,1)S(1)} collective-permute-done((bf16[48,48,128]{2,1,0:T(8,128)(2,1)S(1)}, bf16[48,48,128]{2,1,0:T(8,128)(2,1)S(1)}, u32[]{:S(2)}, u32[]{:S(2)}) %collective-permute-start.8) | collective-permute-done | bytes 589856 | tf_op jit(solution)/shard_map/ppermute | solution.py:430
  72.8 0.0 copy-done.4
  72.8 0.0 copy-done.5
  72.8 1.3 %shard_map.128 = (bf16[60,48,128]{2,1,0:T(8,128)(2,1)S(1)}, bf16[60,48,128]{2,1,0:T(8,128)(2,1)S(1)}, bf16[24,48,128]{2,1,0:T(8,128)(2,1)S(1)}, bf16[48,48,128]{2,1,0:T(8,128)(2,1)S(1)}) custom-call(f32[48,48,128]{2,1,0:T(8,128)S(1)} %get-tuple-element.25.kept_ref, bf16[48,48,128]{2,1,0:T(8,128)(2,1)S(1)} %collective-permute-done.8.came_ref, ...), custom_call_target="tpu_custom_call" | custom-call | flops 400000000 | bytes 6553600 | tf_op jit(solution)/shard_map/pallas_call | solution.py:26
  74.1 0.1 collective-permute-start.9
  74.2 1.3 %collective-permute-start.10 = (bf16[60,48,128]{2,1,0:T(8,128)(2,1)S(1)}, bf16[60,48,128]{2,1,0:T(8,128)(2,1)S(1)}, u32[]{:S(2)}, u32[]{:S(2)}) collective-permute-start(bf16[60,48,128]{2,1,0:T(8,128)(2,1)S(1)} %get-tuple-element.29), channel_id=1, source_target_pairs={{0,1},{1,0},{2,3},{3,2},{4,5},{5,4},{6,7},{7,6},{8,16},{9,17},{10,... | collective-permute-start | bytes 2211848 | tf_op jit(solution)/shard_map/ppermute | solution.py:379
  75.5 0.0 collective-permute-start.11
  75.5 3.1 %collective-permute-start.12 = (bf16[48,48,128]{2,1,0:T(8,128)(2,1)S(1)}, bf16[48,48,128]{2,1,0:T(8,128)(2,1)S(1)}, u32[]{:S(2)}, u32[]{:S(2)}) collective-permute-start(bf16[48,48,128]{2,1,0:T(8,128)(2,1)S(1)} %get-tuple-element.30.own_ref), channel_id=1, source_target_pairs={{0,7},{1,2},{2,1},{3,4},{4,3},{5,6},{6,5},{7,0},{8,15},{9,10},{10,... | collective-permute-start | bytes 1769480 | tf_op jit(solution)/shard_map/ppermute | solution.py:368
  78.6 0.0 collective-permute-done.11.even_ref
  78.6 7.6 %collective-permute-done.12.odd_ref = bf16[48,48,128]{2,1,0:T(8,128)(2,1)S(1)} collective-permute-done((bf16[48,48,128]{2,1,0:T(8,128)(2,1)S(1)}, bf16[48,48,128]{2,1,0:T(8,128)(2,1)S(1)}, u32[]{:S(2)}, u32[]{:S(2)}) %collective-permute-start.12) | collective-permute-done | bytes 589856 | tf_op jit(solution)/shard_map/ppermute | solution.py:368
  86.2 0.4 shard_map.129.after_ref.own_ref
  86.6 1.9 %collective-permute-start.15 = (bf16[48,48,128]{2,1,0:T(8,128)(2,1)S(1)}, bf16[48,48,128]{2,1,0:T(8,128)(2,1)S(1)}, u32[]{:S(2)}, u32[]{:S(2)}) collective-permute-start(bf16[48,48,128]{2,1,0:T(8,128)(2,1)S(1)} %shard_map.129.after_ref.own_ref), channel_id=1, source_target_pairs={{0,8},{8,0},{16,24},{24,16},{32,40},{40,32},{48,56},{56,48},{64,72... | collective-permute-start | bytes 1769480 | tf_op jit(solution)/shard_map/ppermute | solution.py:379
  88.5 1.4 %collective-permute-start.16 = (bf16[48,48,128]{2,1,0:T(8,128)(2,1)S(1)}, bf16[48,48,128]{2,1,0:T(8,128)(2,1)S(1)}, u32[]{:S(2)}, u32[]{:S(2)}) collective-permute-start(bf16[48,48,128]{2,1,0:T(8,128)(2,1)S(1)} %shard_map.129.after_ref.own_ref), channel_id=1, source_target_pairs={{0,1},{1,0},{2,3},{3,2},{4,5},{5,4},{6,7},{7,6},{8,16},{9,17},{10,... | collective-permute-start | bytes 1769480 | tf_op jit(solution)/shard_map/ppermute | solution.py:379
  89.9 1.9 %collective-permute-done.9.even_ref = bf16[60,48,128]{2,1,0:T(8,128)(2,1)S(1)} collective-permute-done((bf16[60,48,128]{2,1,0:T(8,128)(2,1)S(1)}, bf16[60,48,128]{2,1,0:T(8,128)(2,1)S(1)}, u32[]{:S(2)}, u32[]{:S(2)}) %collective-permute-start.9) | collective-permute-done | bytes 737312 | tf_op jit(solution)/shard_map/ppermute | solution.py:379
  91.8 1.1 collective-permute-done.10.odd_ref
  92.9 1.5 %shard_map.130 = (bf16[64,48,128]{2,1,0:T(8,128)(2,1)S(1)}, bf16[64,48,128]{2,1,0:T(8,128)(2,1)S(1)}, bf16[24,48,128]{2,1,0:T(8,128)(2,1)S(1)}) custom-call(f32[8,256]{1,0:T(8,128)S(1)} %shard_map.122.taps_ref, bf16[60,48,128]{2,1,0:T(8,128)(2,1)S(1)} %get-tuple-element.27.sent_ref, bf16[24,48,128]{2,1,0:T(8,128)(2,1)S(1)} %get-tuple-element.28.own_ref, ...), custom_call_target="tpu_custom_call" | custom-call | flops 20000000000 | bytes 4972544 | tf_op jit(solution)/shard_map/pallas_call | solution.py:26
  94.4 0.1 collective-permute-start.13
  94.5 5.5 %collective-permute-start.14 = (bf16[64,48,128]{2,1,0:T(8,128)(2,1)S(1)}, bf16[64,48,128]{2,1,0:T(8,128)(2,1)S(1)}, u32[]{:S(2)}, u32[]{:S(2)}) collective-permute-start(bf16[64,48,128]{2,1,0:T(8,128)(2,1)S(1)} %get-tuple-element.32), channel_id=1, source_target_pairs={{0,7},{1,2},{2,1},{3,4},{4,3},{5,6},{6,5},{7,0},{8,15},{9,10},{10,... | collective-permute-start | bytes 2359304 | tf_op jit(solution)/shard_map/ppermute | solution.py:368
  100.1 3.2 %collective-permute-done.15.even_ref = bf16[48,48,128]{2,1,0:T(8,128)(2,1)S(1)} collective-permute-done((bf16[48,48,128]{2,1,0:T(8,128)(2,1)S(1)}, bf16[48,48,128]{2,1,0:T(8,128)(2,1)S(1)}, u32[]{:S(2)}, u32[]{:S(2)}) %collective-permute-start.15) | collective-permute-done | bytes 589856 | tf_op jit(solution)/shard_map/ppermute | solution.py:379
  103.3 2.3 %collective-permute-done.16.odd_ref = bf16[48,48,128]{2,1,0:T(8,128)(2,1)S(1)} collective-permute-done((bf16[48,48,128]{2,1,0:T(8,128)(2,1)S(1)}, bf16[48,48,128]{2,1,0:T(8,128)(2,1)S(1)}, u32[]{:S(2)}, u32[]{:S(2)}) %collective-permute-start.16) | collective-permute-done | bytes 589856 | tf_op jit(solution)/shard_map/ppermute | solution.py:379
  105.7 0.0 copy-done.2
  105.7 1.7 %shard_map.131.begun_ref = bf16[2,48,48,128]{3,2,1,0:T(8,128)(2,1)} custom-call(f32[8,256]{1,0:T(8,128)S(1)} %shard_map.122.taps_ref, bf16[48,48,128]{2,1,0:T(8,128)(2,1)S(1)} %shard_map.129.after_ref.own_ref, bf16[48,48,128]{2,1,0:T(8,128)(2,1)S(1)} %collective-permute-done.15.even_ref, bf16[48,48,128]{2,1,0:T(8,128)(2,1)S(1)} %collective-permute-done.16.odd_ref, ...), custom_call_target="tpu_custom_call" | custom-call | flops 20000000000 | bytes 4136960 | tf_op jit(solution)/shard_map/pallas_call | solution.py:26
  107.4 0.0 collective-permute-done.13.even_ref
  107.4 2.3 %collective-permute-done.14.odd_ref = bf16[64,48,128]{2,1,0:T(8,128)(2,1)S(1)} collective-permute-done((bf16[64,48,128]{2,1,0:T(8,128)(2,1)S(1)}, bf16[64,48,128]{2,1,0:T(8,128)(2,1)S(1)}, u32[]{:S(2)}, u32[]{:S(2)}) %collective-permute-start.14) | collective-permute-done | bytes 786464 | tf_op jit(solution)/shard_map/ppermute | solution.py:368
  109.8 1.5 %shard_map.132 = (bf16[48,48,64]{2,1,0:T(8,128)(2,1)}, bf16[2,48,48,128]{3,2,1,0:T(8,128)(2,1)}) custom-call(f32[8,256]{1,0:T(8,128)S(1)} %shard_map.122.taps_ref, bf16[64,48,128]{2,1,0:T(8,128)(2,1)S(1)} %get-tuple-element.31.own_ref, bf16[64,48,128]{2,1,0:T(8,128)(2,1)S(1)} %collective-permute-done.13.even_ref, ...), custom_call_target="tpu_custom_call", output_to_operand_aliasing={{1}: (7, {})} | custom-call | flops 700000000 | bytes 6791168 | tf_op jit(solution)/shard_map/pallas_call | solution.py:26
  (5 shorter events, 0.0 us)
Async XLA Ops:
  0.6 1.3 %copy-start.1 = (bf16[2,48,48,128]{3,2,1,0:T(8,128)(2,1)S(1)}, bf16[2,48,48,128]{3,2,1,0:T(8,128)(2,1)}, u32[]{:S(2)}) copy-start(bf16[2,48,48,128]{3,2,1,0:T(8,128)(2,1)} %member_ref.5) | copy-start | bytes 3538948
  1.9 1.1 copy-start.3
  3.0 6.6 %copy-start.8 = (bf16[97]{0:T(256)(128)(2,1)S(1)}, bf16[97]{0:T(256)(128)(2,1)}, u32[]{:S(2)}) copy-start(bf16[97]{0:T(256)(128)(2,1)} %lx_ref.1) | copy-start | bytes 586
  3.0 6.6 %copy-start.9 = (bf16[97]{0:T(256)(128)(2,1)S(1)}, bf16[97]{0:T(256)(128)(2,1)}, u32[]{:S(2)}) copy-start(bf16[97]{0:T(256)(128)(2,1)} %ly_ref.1) | copy-start | bytes 586
  3.0 6.6 %copy-start.10 = (bf16[49]{0:T(256)(128)(2,1)S(1)}, bf16[49]{0:T(256)(128)(2,1)}, u32[]{:S(2)}) copy-start(bf16[49]{0:T(256)(128)(2,1)} %sx_ref.1) | copy-start | bytes 298
  3.0 6.6 %copy-start.11 = (bf16[49]{0:T(256)(128)(2,1)S(1)}, bf16[49]{0:T(256)(128)(2,1)}, u32[]{:S(2)}) copy-start(bf16[49]{0:T(256)(128)(2,1)} %sy_ref.1) | copy-start | bytes 298
  3.3 6.5 %collective-permute-start = (bf16[3072,128]{1,0:T(8,128)(2,1)S(1)}, bf16[3072,128]{1,0:T(8,128)(2,1)S(1)}, u32[]{:S(2)}, u32[]{:S(2)}) collective-permute-start(bf16[3072,128]{1,0:T(8,128)(2,1)S(1)} %get-tuple-element.18.sent_ref), channel_id=1, source_target_pairs={{0,1},{1,0},{2,3},{3,2},{4,5},{5,4},{6,7},{7,6},{8,9},{9,8},{10,11... | collective-permute-start | bytes 2359304 | tf_op jit(solution)/shard_map/ppermute | solution.py:368
  3.4 12.7 %collective-permute-start.1 = (bf16[3072,128]{1,0:T(8,128)(2,1)S(1)}, bf16[3072,128]{1,0:T(8,128)(2,1)S(1)}, u32[]{:S(2)}, u32[]{:S(2)}) collective-permute-start(bf16[3072,128]{1,0:T(8,128)(2,1)S(1)} %get-tuple-element.20), channel_id=1, source_target_pairs={{0,7},{1,2},{2,1},{3,4},{4,3},{5,6},{6,5},{7,0},{8,15},{9,10},{10,... | collective-permute-start | bytes 2359304 | tf_op jit(solution)/shard_map/ppermute | solution.py:368
  6.3 15.4 %collective-permute-start.4 = (bf16[48,48,128]{2,1,0:T(8,128)(2,1)S(1)}, bf16[48,48,128]{2,1,0:T(8,128)(2,1)S(1)}, u32[]{:S(2)}, u32[]{:S(2)}) collective-permute-start(bf16[48,48,128]{2,1,0:T(8,128)(2,1)S(1)} %get-tuple-element.24.own_ref), channel_id=1, source_target_pairs={{0,8},{8,0},{16,24},{24,16},{32,40},{40,32},{48,56},{56,48},{64,72... | collective-permute-start | bytes 1769480 | tf_op jit(solution)/shard_map/ppermute | solution.py:379
  7.9 17.2 %collective-permute-start.5 = (bf16[48,48,128]{2,1,0:T(8,128)(2,1)S(1)}, bf16[48,48,128]{2,1,0:T(8,128)(2,1)S(1)}, u32[]{:S(2)}, u32[]{:S(2)}) collective-permute-start(bf16[48,48,128]{2,1,0:T(8,128)(2,1)S(1)} %get-tuple-element.24.own_ref), channel_id=1, source_target_pairs={{0,1},{1,0},{2,3},{3,2},{4,5},{5,4},{6,7},{7,6},{8,16},{9,17},{10,... | collective-permute-start | bytes 1769480 | tf_op jit(solution)/shard_map/ppermute | solution.py:379
  16.8 21.1 %collective-permute-start.2 = (bf16[60,48,128]{2,1,0:T(8,128)(2,1)S(1)}, bf16[60,48,128]{2,1,0:T(8,128)(2,1)S(1)}, u32[]{:S(2)}, u32[]{:S(2)}) collective-permute-start(bf16[60,48,128]{2,1,0:T(8,128)(2,1)S(1)} %get-tuple-element.21.own_ref), channel_id=1, source_target_pairs={{0,8},{8,0},{16,24},{24,16},{32,40},{40,32},{48,56},{56,48},{64,72... | collective-permute-start | bytes 2211848 | tf_op jit(solution)/shard_map/ppermute | solution.py:379
  18.4 18.4 %copy-start = (bf16[2,48,48,128]{3,2,1,0:T(8,128)(2,1)S(1)}, bf16[2,48,48,128]{3,2,1,0:T(8,128)(2,1)}, u32[]{:S(2)}) copy-start(bf16[2,48,48,128]{3,2,1,0:T(8,128)(2,1)} %pert_ref.5) | copy-start | bytes 3538948
  18.4 18.4 %copy-start.6 = (bf16[128,128]{1,0:T(8,128)(2,1)S(1)}, bf16[128,128]{1,0:T(8,128)(2,1)}, u32[]{:S(2)}) copy-start(bf16[128,128]{1,0:T(8,128)(2,1)} %vert_ref.5) | copy-start | bytes 98308
  18.4 21.1 %collective-permute-start.3 = (bf16[60,48,128]{2,1,0:T(8,128)(2,1)S(1)}, bf16[60,48,128]{2,1,0:T(8,128)(2,1)S(1)}, u32[]{:S(2)}, u32[]{:S(2)}) collective-permute-start(bf16[60,48,128]{2,1,0:T(8,128)(2,1)S(1)} %get-tuple-element.22), channel_id=1, source_target_pairs={{0,1},{1,0},{2,3},{3,2},{4,5},{5,4},{6,7},{7,6},{8,16},{9,17},{10,... | collective-permute-start | bytes 2211848 | tf_op jit(solution)/shard_map/ppermute | solution.py:379
  26.1 13.5 %copy-start.7 = (bf16[128,128]{1,0:T(8,128)(2,1)S(1)}, bf16[128,128]{1,0:T(8,128)(2,1)}, u32[]{:S(2)}) copy-start(bf16[128,128]{1,0:T(8,128)(2,1)} %static_ref.5) | copy-start | bytes 98308
  26.1 2.1 %collective-permute-start.6 = (bf16[48,48,128]{2,1,0:T(8,128)(2,1)S(1)}, bf16[48,48,128]{2,1,0:T(8,128)(2,1)S(1)}, u32[]{:S(2)}, u32[]{:S(2)}) collective-permute-start(bf16[48,48,128]{2,1,0:T(8,128)(2,1)S(1)} %shard_map.125.own_ref), channel_id=1, source_target_pairs={{0,1},{1,0},{2,3},{3,2},{4,5},{5,4},{6,7},{7,6},{8,9},{9,8},{10,11... | collective-permute-start | bytes 1769480 | tf_op jit(solution)/shard_map/ppermute | solution.py:368
  26.2 10.6 %collective-permute-start.7 = (bf16[48,48,128]{2,1,0:T(8,128)(2,1)S(1)}, bf16[48,48,128]{2,1,0:T(8,128)(2,1)S(1)}, u32[]{:S(2)}, u32[]{:S(2)}) collective-permute-start(bf16[48,48,128]{2,1,0:T(8,128)(2,1)S(1)} %shard_map.125.own_ref), channel_id=1, source_target_pairs={{0,7},{1,2},{2,1},{3,4},{4,3},{5,6},{6,5},{7,0},{8,15},{9,10},{10,... | collective-permute-start | bytes 1769480 | tf_op jit(solution)/shard_map/ppermute | solution.py:368
  39.6 33.2 %copy-start.4 = (bf16[48,48,128]{2,1,0:T(8,128)(2,1)S(1)}, bf16[48,48,128]{2,1,0:T(8,128)(2,1)}, u32[]{:S(2)}) copy-start(bf16[48,48,128]{2,1,0:T(8,128)(2,1)} %dep_ref.1) | copy-start | bytes 1769476
  39.6 33.2 %copy-start.5 = (bf16[48,48,128]{2,1,0:T(8,128)(2,1)S(1)}, bf16[48,48,128]{2,1,0:T(8,128)(2,1)}, u32[]{:S(2)}) copy-start(bf16[48,48,128]{2,1,0:T(8,128)(2,1)} %weight_ref.1) | copy-start | bytes 1769476
  41.4 31.3 %collective-permute-start.8 = (bf16[48,48,128]{2,1,0:T(8,128)(2,1)S(1)}, bf16[48,48,128]{2,1,0:T(8,128)(2,1)S(1)}, u32[]{:S(2)}, u32[]{:S(2)}) collective-permute-start(bf16[48,48,128]{2,1,0:T(8,128)(2,1)S(1)} %get-tuple-element.26), channel_id=1, source_target_pairs={{0,128},{128,0},{1,129},{129,1},{2,130},{130,2},{3,131},{131,3},{4... | collective-permute-start | bytes 1769480 | tf_op jit(solution)/shard_map/ppermute | solution.py:430
  74.1 17.7 %collective-permute-start.9 = (bf16[60,48,128]{2,1,0:T(8,128)(2,1)S(1)}, bf16[60,48,128]{2,1,0:T(8,128)(2,1)S(1)}, u32[]{:S(2)}, u32[]{:S(2)}) collective-permute-start(bf16[60,48,128]{2,1,0:T(8,128)(2,1)S(1)} %get-tuple-element.27.sent_ref), channel_id=1, source_target_pairs={{0,8},{8,0},{16,24},{24,16},{32,40},{40,32},{48,56},{56,48},{64,72... | collective-permute-start | bytes 2211848 | tf_op jit(solution)/shard_map/ppermute | solution.py:379
  74.2 18.7 %collective-permute-start.10 = (bf16[60,48,128]{2,1,0:T(8,128)(2,1)S(1)}, bf16[60,48,128]{2,1,0:T(8,128)(2,1)S(1)}, u32[]{:S(2)}, u32[]{:S(2)}) collective-permute-start(bf16[60,48,128]{2,1,0:T(8,128)(2,1)S(1)} %get-tuple-element.29), channel_id=1, source_target_pairs={{0,1},{1,0},{2,3},{3,2},{4,5},{5,4},{6,7},{7,6},{8,16},{9,17},{10,... | collective-permute-start | bytes 2211848 | tf_op jit(solution)/shard_map/ppermute | solution.py:379
  75.5 3.1 %collective-permute-start.11 = (bf16[48,48,128]{2,1,0:T(8,128)(2,1)S(1)}, bf16[48,48,128]{2,1,0:T(8,128)(2,1)S(1)}, u32[]{:S(2)}, u32[]{:S(2)}) collective-permute-start(bf16[48,48,128]{2,1,0:T(8,128)(2,1)S(1)} %get-tuple-element.30.own_ref), channel_id=1, source_target_pairs={{0,1},{1,0},{2,3},{3,2},{4,5},{5,4},{6,7},{7,6},{8,9},{9,8},{10,11... | collective-permute-start | bytes 1769480 | tf_op jit(solution)/shard_map/ppermute | solution.py:368
  75.5 10.6 %collective-permute-start.12 = (bf16[48,48,128]{2,1,0:T(8,128)(2,1)S(1)}, bf16[48,48,128]{2,1,0:T(8,128)(2,1)S(1)}, u32[]{:S(2)}, u32[]{:S(2)}) collective-permute-start(bf16[48,48,128]{2,1,0:T(8,128)(2,1)S(1)} %get-tuple-element.30.own_ref), channel_id=1, source_target_pairs={{0,7},{1,2},{2,1},{3,4},{4,3},{5,6},{6,5},{7,0},{8,15},{9,10},{10,... | collective-permute-start | bytes 1769480 | tf_op jit(solution)/shard_map/ppermute | solution.py:368
  86.6 16.7 %collective-permute-start.15 = (bf16[48,48,128]{2,1,0:T(8,128)(2,1)S(1)}, bf16[48,48,128]{2,1,0:T(8,128)(2,1)S(1)}, u32[]{:S(2)}, u32[]{:S(2)}) collective-permute-start(bf16[48,48,128]{2,1,0:T(8,128)(2,1)S(1)} %shard_map.129.after_ref.own_ref), channel_id=1, source_target_pairs={{0,8},{8,0},{16,24},{24,16},{32,40},{40,32},{48,56},{56,48},{64,72... | collective-permute-start | bytes 1769480 | tf_op jit(solution)/shard_map/ppermute | solution.py:379
  88.5 17.2 %collective-permute-start.16 = (bf16[48,48,128]{2,1,0:T(8,128)(2,1)S(1)}, bf16[48,48,128]{2,1,0:T(8,128)(2,1)S(1)}, u32[]{:S(2)}, u32[]{:S(2)}) collective-permute-start(bf16[48,48,128]{2,1,0:T(8,128)(2,1)S(1)} %shard_map.129.after_ref.own_ref), channel_id=1, source_target_pairs={{0,1},{1,0},{2,3},{3,2},{4,5},{5,4},{6,7},{7,6},{8,16},{9,17},{10,... | collective-permute-start | bytes 1769480 | tf_op jit(solution)/shard_map/ppermute | solution.py:379
  92.9 12.8 %copy-start.2 = (bf16[2,48,48,128]{3,2,1,0:T(8,128)(2,1)S(1)}, bf16[2,48,48,128]{3,2,1,0:T(8,128)(2,1)}, u32[]{:S(2)}) copy-start(bf16[2,48,48,128]{3,2,1,0:T(8,128)(2,1)} %member_ref.5) | copy-start | bytes 3538948
  94.4 13.0 %collective-permute-start.13 = (bf16[64,48,128]{2,1,0:T(8,128)(2,1)S(1)}, bf16[64,48,128]{2,1,0:T(8,128)(2,1)S(1)}, u32[]{:S(2)}, u32[]{:S(2)}) collective-permute-start(bf16[64,48,128]{2,1,0:T(8,128)(2,1)S(1)} %get-tuple-element.31.own_ref), channel_id=1, source_target_pairs={{0,1},{1,0},{2,3},{3,2},{4,5},{5,4},{6,7},{7,6},{8,9},{9,8},{10,11... | collective-permute-start | bytes 2359304 | tf_op jit(solution)/shard_map/ppermute | solution.py:368
  94.5 15.2 %collective-permute-start.14 = (bf16[64,48,128]{2,1,0:T(8,128)(2,1)S(1)}, bf16[64,48,128]{2,1,0:T(8,128)(2,1)S(1)}, u32[]{:S(2)}, u32[]{:S(2)}) collective-permute-start(bf16[64,48,128]{2,1,0:T(8,128)(2,1)S(1)} %get-tuple-element.32), channel_id=1, source_target_pairs={{0,7},{1,2},{2,1},{3,4},{4,3},{5,6},{6,5},{7,0},{8,15},{9,10},{10,... | collective-permute-start | bytes 2359304 | tf_op jit(solution)/shard_map/ppermute | solution.py:368

commit v4 on v3

--- a/solution.py
+++ b/solution.py
@@ -231,7 +231,7 @@
         out_ref[at] = pert_ref[0, at].astype(F32) * local
         return carry
 
-    lax.fori_loop(0, 6, step, 0, unroll=2)
+    lax.fori_loop(0, 6, step, 0, unroll=6)
 
 
 def forward_b_kernel(
@@ -276,12 +276,12 @@
         own_ref[pl.ds(4 * i, 4)] = static.reshape(4, TILE, 128)
         return carry
 
-    lax.fori_loop(0, 6, step, 0, unroll=2)
+    lax.fori_loop(0, 6, step, 0, unroll=6)
     pack_x(own_ref[...], even_ref, odd_ref)
 
 
 def back_x_kernel(
-    rows, taps_ref, sent_ref, own_ref, even_ref, odd_ref, after_ref, to_even_ref, to_odd_ref, out_ref
+    rows, taps_ref, sent_ref, own_ref, even_ref, odd_ref, after_ref, to_even_ref, to_odd_ref, slab_ref, out_ref
 ):
     member = band_swapped(taps_ref[rows[0] : rows[0] + 1], "tx")
     static = band(taps_ref[rows[1] : rows[1] + 1], 24, 72)
@@ -289,7 +289,7 @@
         at = slice(c, c + 16)
         out = along_x(member, [even_ref[:TILE, at], sent_ref[:TILE, at], odd_ref[:TILE, at]])
         to_even_ref[:TILE, at] = out
-        to_odd_ref[:TILE, at] = out
+        to_odd_ref[:, at] = out
         left, right = sides(even_ref[TILE:, at], odd_ref[TILE:, at], "tx")
         out_ref[:, at] = along_x(static, [static_parts(left, own_ref[:, at], right)])
     packed = out_ref[...]
@@ -297,7 +297,7 @@
     left = packed[:, :SLAB].reshape(16, TILE, 128)
     odd, _ = place("ty")
     to_even_ref[TILE:] = pick(odd, left, right)
-    to_odd_ref[TILE:] = pick(odd, right, left)
+    slab_ref[...] = pick(odd, right, left)
 
 
 def back_y_kernel(row, taps_ref, own_ref, even_ref, odd_ref, out_ref):
@@ -321,7 +321,7 @@
 
 
 def last_a_kernel(
-    rows, taps_ref, own_ref, even_ref, odd_ref, s_ref, member_ref, control_ref, begun_ref,
+    rows, taps_ref, own_ref, even_ref, odd_ref, slab_ref, s_ref, member_ref, control_ref, begun_ref,
     static_out, member_out, static, member, sems
 ):
     copies = []
@@ -331,7 +331,7 @@
         copies[-1].start()
 
     matrix = band(taps_ref[rows[1] : rows[1] + 1], TILE, 112)
-    slabs = [r[TILE:].reshape(24, SLAB, 128) for r in (even_ref, odd_ref)]
+    slabs = [r.reshape(24, SLAB, 128) for r in (even_ref[TILE:], slab_ref[...])]
     left, right = sides(slabs[0], slabs[1], "ty")
     for x in range(0, 24, 2):
         lines = [jnp.concatenate([left[k], s_ref[k], right[k]], axis=0) for k in (x, x + 1)]
@@ -361,11 +361,11 @@
         copy.wait()
 
 
-def swaps_y(even, odd):
+def swaps_y(even, *odd):
     n = lax.axis_size("ty")
     first = [(i, i ^ 1) for i in range(n)]
     second = [(i, (i + 1) % n if i % 2 else (i - 1) % n) for i in range(n)]
-    return lax.ppermute(even, "ty", first), lax.ppermute(odd, "ty", second)
+    return (lax.ppermute(even, "ty", first),) + tuple(lax.ppermute(part, "ty", second) for part in odd)
 
 
 def swaps_x(even, odd):
@@ -437,11 +437,12 @@
     (b,) = call(functools.partial(back_y_kernel, 5), (shape(*tile),), (taps, b) + swaps_y(b, b), BRIEF)
     b_halo = swaps_x(b, b)
     args = (taps,) + a + (b,)
-    to_even, to_odd, s = call(
+    to_even, to_odd, slab, s = call(
         functools.partial(back_x_kernel, (4, 6)),
-        (shape(64, TILE, 128), shape(64, TILE, 128), shape(24, TILE, 128)), args, LONG, in_any=(len(args) - 1,),
-    )
-    a = (to_even,) + swaps_y(to_even, to_odd) + (s,)
+        (shape(64, TILE, 128), shape(*tile), shape(16, TILE, 128), shape(24, TILE, 128)), args, LONG,
+        in_any=(len(args) - 1,),
+    )
+    a = (to_even,) + swaps_y(to_even, to_odd, slab) + (s,)
     (begun,) = call(
         functools.partial(last_b_kernel, 4), (shape(2, *tile),), (taps, b) + b_halo + (member_control,), LONG,
         [pltpu.VMEM((3, TILE, 16, 128), BF), pltpu.SemaphoreType.DMA((3,))], out_any=(0,),

time: 112 us -> 112 us (level)
    ppermute x8 -> x9, waiting for transfers between devices: 26.3 us -> 26.7 us  [the longest x5 25.2 us: swaps_y(): lax.ppermute(part, 'ty', second)]
    ppermute x8 -> x9, starting transfers between devices: 12.3 us -> 12.5 us  [the longest x5 12.2 us: swaps_y(): lax.ppermute(part, 'ty', second)]
  transfers between devices with their start and end apart: 17 -> 18, of which waited for: 13 -> 13; matrix products, arithmetic and copies ran while one was open for 0% -> 0% of each run, Pallas kernels for 6% -> 5%
where the time goes in v4:
time: 112 us; the launch traced here: 111 us
  waiting for transfers between devices  67.1 us (60%)
  starting transfers between devices  30 us (27%)
  Pallas kernels  10.8 us (10%)
  local copies, waits for them, and re-layouts  2.37 us (2%)
    ppermute x5, waiting for transfers between devices, swaps_y(): lax.ppermute(part, 'ty', second)  25.2 us
    ppermute x1, waiting for transfers between devices, body(): came = lax.ppermute(sent, 'mem', [(i, size - 1 - i) for i in range(size)])  25 us
    ppermute x5, starting transfers between devices, swaps_y(): lax.ppermute(part, 'ty', second)  12.2 us
    pallas_call x11, Pallas kernels, call(): pl.pallas_call(kernel, out_shape=outs, in_specs=[ANY if i in in_any else...  10.8 us
    ppermute x4, waiting for transfers between devices, swaps_x(): lax.ppermute(odd, ('tx', 'ty'), second)  8.6 us
    ppermute x4, waiting for transfers between devices, swaps_x(): lax.ppermute(even, 'tx', first)  6.85 us
    ppermute x1, starting transfers between devices, body(): came = lax.ppermute(sent, 'mem', [(i, size - 1 - i) for i in range(size)])  6.38 us
    ppermute x4, starting transfers between devices, swaps_x(): lax.ppermute(odd, ('tx', 'ty'), second)  6.14 us
  transfers between devices with their start and end apart: 18, of which 13 were waited for; matrix products, arithmetic and copies ran while one was open for 0% of the time, Pallas kernels for 5%

profile of v4, /device:TPU:32, one launch (start us, length us, event | category | flops | bytes accessed | tf_op | source)
XLA Modules:
  0.0 111.2 jit_solution(3034376636440678789)
XLA Ops:
  0.6 0.0 copy-start.1
  0.6 1.3 %copy-done.1 = bf16[2,48,48,128]{3,2,1,0:T(8,128)(2,1)S(1)} copy-done((bf16[2,48,48,128]{3,2,1,0:T(8,128)(2,1)S(1)}, bf16[2,48,48,128]{3,2,1,0:T(8,128)(2,1)}, u32[]{:S(2)}) %copy-start.1) | copy-done | bytes 1179672
  1.9 0.0 copy-start.3
  1.9 1.1 copy-done.3
  3.0 0.0 copy-start.8
  3.0 0.0 copy-start.9
  3.0 0.3 shard_map.123
  3.3 0.1 collective-permute-start
  3.4 2.9 %collective-permute-start.1 = (bf16[3072,128]{1,0:T(8,128)(2,1)S(1)}, bf16[3072,128]{1,0:T(8,128)(2,1)S(1)}, u32[]{:S(2)}, u32[]{:S(2)}) collective-permute-start(bf16[3072,128]{1,0:T(8,128)(2,1)S(1)} %get-tuple-element.21), channel_id=1, source_target_pairs={{0,7},{1,2},{2,1},{3,4},{4,3},{5,6},{6,5},{7,0},{8,15},{9,10},{10,... | collective-permute-start | bytes 2359304 | tf_op jit(solution)/shard_map/ppermute | solution.py:368
  6.3 1.6 %collective-permute-start.4 = (bf16[48,48,128]{2,1,0:T(8,128)(2,1)S(1)}, bf16[48,48,128]{2,1,0:T(8,128)(2,1)S(1)}, u32[]{:S(2)}, u32[]{:S(2)}) collective-permute-start(bf16[48,48,128]{2,1,0:T(8,128)(2,1)S(1)} %get-tuple-element.25.own_ref), channel_id=1, source_target_pairs={{0,8},{8,0},{16,24},{24,16},{32,40},{40,32},{48,56},{56,48},{64,72... | collective-permute-start | bytes 1769480 | tf_op jit(solution)/shard_map/ppermute | solution.py:379
  7.9 1.7 %collective-permute-start.5 = (bf16[48,48,128]{2,1,0:T(8,128)(2,1)S(1)}, bf16[48,48,128]{2,1,0:T(8,128)(2,1)S(1)}, u32[]{:S(2)}, u32[]{:S(2)}) collective-permute-start(bf16[48,48,128]{2,1,0:T(8,128)(2,1)S(1)} %get-tuple-element.25.own_ref), channel_id=1, source_target_pairs={{0,1},{1,0},{2,3},{3,2},{4,5},{5,4},{6,7},{7,6},{8,16},{9,17},{10,... | collective-permute-start | bytes 1769480 | tf_op jit(solution)/shard_map/ppermute | solution.py:379
  9.6 0.0 copy-done.8
  9.6 0.0 copy-done.9
  9.6 0.0 copy-done.10
  9.6 0.0 copy-done.11
  9.6 0.2 shard_map.122.taps_ref
  9.8 0.0 collective-permute-done.even_ref
  9.8 6.4 %collective-permute-done.1.odd_ref = bf16[3072,128]{1,0:T(8,128)(2,1)S(1)} collective-permute-done((bf16[3072,128]{1,0:T(8,128)(2,1)S(1)}, bf16[3072,128]{1,0:T(8,128)(2,1)S(1)}, u32[]{:S(2)}, u32[]{:S(2)}) %collective-permute-start.1) | collective-permute-done | bytes 786464 | tf_op jit(solution)/shard_map/ppermute | solution.py:368
  16.1 0.6 shard_map.124
  16.8 1.7 %collective-permute-start.2 = (bf16[60,48,128]{2,1,0:T(8,128)(2,1)S(1)}, bf16[60,48,128]{2,1,0:T(8,128)(2,1)S(1)}, u32[]{:S(2)}, u32[]{:S(2)}) collective-permute-start(bf16[60,48,128]{2,1,0:T(8,128)(2,1)S(1)} %get-tuple-element.22.own_ref), channel_id=1, source_target_pairs={{0,8},{8,0},{16,24},{24,16},{32,40},{40,32},{48,56},{56,48},{64,72... | collective-permute-start | bytes 2211848 | tf_op jit(solution)/shard_map/ppermute | solution.py:379
  18.4 1.7 %collective-permute-start.3 = (bf16[60,48,128]{2,1,0:T(8,128)(2,1)S(1)}, bf16[60,48,128]{2,1,0:T(8,128)(2,1)S(1)}, u32[]{:S(2)}, u32[]{:S(2)}) collective-permute-start(bf16[60,48,128]{2,1,0:T(8,128)(2,1)S(1)} %get-tuple-element.23), channel_id=1, source_target_pairs={{0,1},{1,0},{2,3},{3,2},{4,5},{5,4},{6,7},{7,6},{8,16},{9,17},{10,... | collective-permute-start | bytes 2211848 | tf_op jit(solution)/shard_map/ppermute | solution.py:379
  20.2 1.5 %collective-permute-done.4.even_ref = bf16[48,48,128]{2,1,0:T(8,128)(2,1)S(1)} collective-permute-done((bf16[48,48,128]{2,1,0:T(8,128)(2,1)S(1)}, bf16[48,48,128]{2,1,0:T(8,128)(2,1)S(1)}, u32[]{:S(2)}, u32[]{:S(2)}) %collective-permute-start.4) | collective-permute-done | bytes 589856 | tf_op jit(solution)/shard_map/ppermute | solution.py:379
  21.7 3.4 %collective-permute-done.5.odd_ref = bf16[48,48,128]{2,1,0:T(8,128)(2,1)S(1)} collective-permute-done((bf16[48,48,128]{2,1,0:T(8,128)(2,1)S(1)}, bf16[48,48,128]{2,1,0:T(8,128)(2,1)S(1)}, u32[]{:S(2)}, u32[]{:S(2)}) %collective-permute-start.5) | collective-permute-done | bytes 589856 | tf_op jit(solution)/shard_map/ppermute | solution.py:379
  25.1 1.0 shard_map.125.own_ref
  26.1 0.0 copy-start.7
  26.1 0.1 collective-permute-start.6
  26.2 0.5 collective-permute-start.7
  26.7 1.5 %collective-permute-done.6.even_ref = bf16[48,48,128]{2,1,0:T(8,128)(2,1)S(1)} collective-permute-done((bf16[48,48,128]{2,1,0:T(8,128)(2,1)S(1)}, bf16[48,48,128]{2,1,0:T(8,128)(2,1)S(1)}, u32[]{:S(2)}, u32[]{:S(2)}) %collective-permute-start.6) | collective-permute-done | bytes 589856 | tf_op jit(solution)/shard_map/ppermute | solution.py:368
  28.2 8.6 %collective-permute-done.7.odd_ref = bf16[48,48,128]{2,1,0:T(8,128)(2,1)S(1)} collective-permute-done((bf16[48,48,128]{2,1,0:T(8,128)(2,1)S(1)}, bf16[48,48,128]{2,1,0:T(8,128)(2,1)S(1)}, u32[]{:S(2)}, u32[]{:S(2)}) %collective-permute-start.7) | collective-permute-done | bytes 589856 | tf_op jit(solution)/shard_map/ppermute | solution.py:368
  36.8 0.0 copy-done
  36.8 0.0 copy-done.6
  36.8 0.6 shard_map.126.first_ref
  37.4 0.0 collective-permute-done.2.even_ref
  37.5 2.1 %collective-permute-done.3.odd_ref = bf16[60,48,128]{2,1,0:T(8,128)(2,1)S(1)} collective-permute-done((bf16[60,48,128]{2,1,0:T(8,128)(2,1)S(1)}, bf16[60,48,128]{2,1,0:T(8,128)(2,1)S(1)}, u32[]{:S(2)}, u32[]{:S(2)}) %collective-permute-start.3) | collective-permute-done | bytes 737312 | tf_op jit(solution)/shard_map/ppermute | solution.py:379
  39.6 0.0 copy-done.7
  39.6 1.8 %shard_map.127 = (f32[48,48,128]{2,1,0:T(8,128)S(1)}, bf16[48,48,128]{2,1,0:T(8,128)(2,1)S(1)}) custom-call(f32[8,256]{1,0:T(8,128)S(1)} %shard_map.122.taps_ref, bf16[60,48,128]{2,1,0:T(8,128)(2,1)S(1)} %get-tuple-element.22.own_ref, bf16[60,48,128]{2,1,0:T(8,128)(2,1)S(1)} %collective-permute-done.2.even_ref, ...), custom_call_target="tpu_custom_call" | custom-call | flops 1000000000 | bytes 6709248 | tf_op jit(solution)/shard_map/pallas_call | solution.py:26
  41.4 6.4 %collective-permute-start.8 = (bf16[48,48,128]{2,1,0:T(8,128)(2,1)S(1)}, bf16[48,48,128]{2,1,0:T(8,128)(2,1)S(1)}, u32[]{:S(2)}, u32[]{:S(2)}) collective-permute-start(bf16[48,48,128]{2,1,0:T(8,128)(2,1)S(1)} %get-tuple-element.27), channel_id=1, source_target_pairs={{0,128},{128,0},{1,129},{129,1},{2,130},{130,2},{3,131},{131,3},{4... | collective-permute-start | bytes 1769480 | tf_op jit(solution)/shard_map/ppermute | solution.py:430
  47.8 25.0 %collective-permute-done.8.came_ref = bf16[48,48,128]{2,1,0:T(8,128)(2,1)S(1)} collective-permute-done((bf16[48,48,128]{2,1,0:T(8,128)(2,1)S(1)}, bf16[48,48,128]{2,1,0:T(8,128)(2,1)S(1)}, u32[]{:S(2)}, u32[]{:S(2)}) %collective-permute-start.8) | collective-permute-done | bytes 589856 | tf_op jit(solution)/shard_map/ppermute | solution.py:430
  72.8 0.0 copy-done.4
  72.8 0.0 copy-done.5
  72.8 1.0 shard_map.128
  73.7 0.1 collective-permute-start.9
  73.8 1.3 %collective-permute-start.10 = (bf16[60,48,128]{2,1,0:T(8,128)(2,1)S(1)}, bf16[60,48,128]{2,1,0:T(8,128)(2,1)S(1)}, u32[]{:S(2)}, u32[]{:S(2)}) collective-permute-start(bf16[60,48,128]{2,1,0:T(8,128)(2,1)S(1)} %get-tuple-element.30), channel_id=1, source_target_pairs={{0,1},{1,0},{2,3},{3,2},{4,5},{5,4},{6,7},{7,6},{8,16},{9,17},{10,... | collective-permute-start | bytes 2211848 | tf_op jit(solution)/shard_map/ppermute | solution.py:379
  75.1 0.0 collective-permute-start.11
  75.1 3.1 %collective-permute-start.12 = (bf16[48,48,128]{2,1,0:T(8,128)(2,1)S(1)}, bf16[48,48,128]{2,1,0:T(8,128)(2,1)S(1)}, u32[]{:S(2)}, u32[]{:S(2)}) collective-permute-start(bf16[48,48,128]{2,1,0:T(8,128)(2,1)S(1)} %get-tuple-element.31.own_ref), channel_id=1, source_target_pairs={{0,7},{1,2},{2,1},{3,4},{4,3},{5,6},{6,5},{7,0},{8,15},{9,10},{10,... | collective-permute-start | bytes 1769480 | tf_op jit(solution)/shard_map/ppermute | solution.py:368
  78.2 0.0 collective-permute-done.11.even_ref
  78.2 7.6 %collective-permute-done.12.odd_ref = bf16[48,48,128]{2,1,0:T(8,128)(2,1)S(1)} collective-permute-done((bf16[48,48,128]{2,1,0:T(8,128)(2,1)S(1)}, bf16[48,48,128]{2,1,0:T(8,128)(2,1)S(1)}, u32[]{:S(2)}, u32[]{:S(2)}) %collective-permute-start.12) | collective-permute-done | bytes 589856 | tf_op jit(solution)/shard_map/ppermute | solution.py:368
  85.8 0.4 shard_map.129.after_ref.own_ref
  86.2 1.7 %collective-permute-start.16 = (bf16[48,48,128]{2,1,0:T(8,128)(2,1)S(1)}, bf16[48,48,128]{2,1,0:T(8,128)(2,1)S(1)}, u32[]{:S(2)}, u32[]{:S(2)}) collective-permute-start(bf16[48,48,128]{2,1,0:T(8,128)(2,1)S(1)} %shard_map.129.after_ref.own_ref), channel_id=1, source_target_pairs={{0,8},{8,0},{16,24},{24,16},{32,40},{40,32},{48,56},{56,48},{64,72... | collective-permute-start | bytes 1769480 | tf_op jit(solution)/shard_map/ppermute | solution.py:379
  87.9 1.4 %collective-permute-start.17 = (bf16[48,48,128]{2,1,0:T(8,128)(2,1)S(1)}, bf16[48,48,128]{2,1,0:T(8,128)(2,1)S(1)}, u32[]{:S(2)}, u32[]{:S(2)}) collective-permute-start(bf16[48,48,128]{2,1,0:T(8,128)(2,1)S(1)} %shard_map.129.after_ref.own_ref), channel_id=1, source_target_pairs={{0,1},{1,0},{2,3},{3,2},{4,5},{5,4},{6,7},{7,6},{8,16},{9,17},{10,... | collective-permute-start | bytes 1769480 | tf_op jit(solution)/shard_map/ppermute | solution.py:379
  89.3 2.3 %collective-permute-done.9.even_ref = bf16[60,48,128]{2,1,0:T(8,128)(2,1)S(1)} collective-permute-done((bf16[60,48,128]{2,1,0:T(8,128)(2,1)S(1)}, bf16[60,48,128]{2,1,0:T(8,128)(2,1)S(1)}, u32[]{:S(2)}, u32[]{:S(2)}) %collective-permute-start.9) | collective-permute-done | bytes 737312 | tf_op jit(solution)/shard_map/ppermute | solution.py:379
  91.6 0.9 collective-permute-done.10.odd_ref
  92.5 1.5 %shard_map.130 = (bf16[64,48,128]{2,1,0:T(8,128)(2,1)S(1)}, bf16[48,48,128]{2,1,0:T(8,128)(2,1)S(1)}, bf16[16,48,128]{2,1,0:T(8,128)(2,1)S(1)}, bf16[24,48,128]{2,1,0:T(8,128)(2,1)S(1)}) custom-call(f32[8,256]{1,0:T(8,128)S(1)} %shard_map.122.taps_ref, bf16[60,48,128]{2,1,0:T(8,128)(2,1)S(1)} %get-tuple-element.28.sent_ref, ...), custom_call_target="tpu_custom_call" | custom-call | flops 20000000000 | bytes 4972544 | tf_op jit(solution)/shard_map/pallas_call | solution.py:26
  94.0 0.1 collective-permute-start.13
  94.1 5.7 %collective-permute-start.14 = (bf16[48,48,128]{2,1,0:T(8,128)(2,1)S(1)}, bf16[48,48,128]{2,1,0:T(8,128)(2,1)S(1)}, u32[]{:S(2)}, u32[]{:S(2)}) collective-permute-start(bf16[48,48,128]{2,1,0:T(8,128)(2,1)S(1)} %get-tuple-element.33), channel_id=1, source_target_pairs={{0,7},{1,2},{2,1},{3,4},{4,3},{5,6},{6,5},{7,0},{8,15},{9,10},{10,... | collective-permute-start | bytes 1769480 | tf_op jit(solution)/shard_map/ppermute | solution.py:368
  99.9 0.0 collective-permute-start.15
  99.9 3.0 %collective-permute-done.16.even_ref = bf16[48,48,128]{2,1,0:T(8,128)(2,1)S(1)} collective-permute-done((bf16[48,48,128]{2,1,0:T(8,128)(2,1)S(1)}, bf16[48,48,128]{2,1,0:T(8,128)(2,1)S(1)}, u32[]{:S(2)}, u32[]{:S(2)}) %collective-permute-start.16) | collective-permute-done | bytes 589856 | tf_op jit(solution)/shard_map/ppermute | solution.py:379
  102.9 2.2 %collective-permute-done.17.odd_ref = bf16[48,48,128]{2,1,0:T(8,128)(2,1)S(1)} collective-permute-done((bf16[48,48,128]{2,1,0:T(8,128)(2,1)S(1)}, bf16[48,48,128]{2,1,0:T(8,128)(2,1)S(1)}, u32[]{:S(2)}, u32[]{:S(2)}) %collective-permute-start.17) | collective-permute-done | bytes 589856 | tf_op jit(solution)/shard_map/ppermute | solution.py:379
  105.1 0.0 copy-done.2
  105.1 1.7 %shard_map.131.begun_ref = bf16[2,48,48,128]{3,2,1,0:T(8,128)(2,1)} custom-call(f32[8,256]{1,0:T(8,128)S(1)} %shard_map.122.taps_ref, bf16[48,48,128]{2,1,0:T(8,128)(2,1)S(1)} %shard_map.129.after_ref.own_ref, bf16[48,48,128]{2,1,0:T(8,128)(2,1)S(1)} %collective-permute-done.16.even_ref, bf16[48,48,128]{2,1,0:T(8,128)(2,1)S(1)} %collective-permute-done.17.odd_ref, ...), custom_call_target="tpu_custom_call" | custom-call | flops 20000000000 | bytes 4136960 | tf_op jit(solution)/shard_map/pallas_call | solution.py:26
  106.9 2.7 %collective-permute-done.15.slab_ref = bf16[16,48,128]{2,1,0:T(8,128)(2,1)S(1)} collective-permute-done((bf16[16,48,128]{2,1,0:T(8,128)(2,1)S(1)}, bf16[16,48,128]{2,1,0:T(8,128)(2,1)S(1)}, u32[]{:S(2)}, u32[]{:S(2)}) %collective-permute-start.15) | collective-permute-done | bytes 196640 | tf_op jit(solution)/shard_map/ppermute | solution.py:368
  109.5 0.0 collective-permute-done.14.odd_ref
  109.6 0.0 collective-permute-done.13.even_ref
  109.6 1.5 %shard_map.132 = (bf16[48,48,64]{2,1,0:T(8,128)(2,1)}, bf16[2,48,48,128]{3,2,1,0:T(8,128)(2,1)}) custom-call(f32[8,256]{1,0:T(8,128)S(1)} %shard_map.122.taps_ref, bf16[64,48,128]{2,1,0:T(8,128)(2,1)S(1)} %get-tuple-element.32.own_ref, bf16[64,48,128]{2,1,0:T(8,128)(2,1)S(1)} %collective-permute-done.13.even_ref, ...), custom_call_target="tpu_custom_call", output_to_operand_aliasing={{1}: (8, {})} | custom-call | flops 700000000 | bytes 6791168 | tf_op jit(solution)/shard_map/pallas_call | solution.py:26
  (7 shorter events, 0.0 us)
Async XLA Ops:
  0.6 1.3 %copy-start.1 = (bf16[2,48,48,128]{3,2,1,0:T(8,128)(2,1)S(1)}, bf16[2,48,48,128]{3,2,1,0:T(8,128)(2,1)}, u32[]{:S(2)}) copy-start(bf16[2,48,48,128]{3,2,1,0:T(8,128)(2,1)} %member_ref.5) | copy-start | bytes 3538948
  1.9 1.1 copy-start.3
  3.0 6.6 %copy-start.8 = (bf16[97]{0:T(256)(128)(2,1)S(1)}, bf16[97]{0:T(256)(128)(2,1)}, u32[]{:S(2)}) copy-start(bf16[97]{0:T(256)(128)(2,1)} %lx_ref.1) | copy-start | bytes 586
  3.0 6.6 %copy-start.9 = (bf16[97]{0:T(256)(128)(2,1)S(1)}, bf16[97]{0:T(256)(128)(2,1)}, u32[]{:S(2)}) copy-start(bf16[97]{0:T(256)(128)(2,1)} %ly_ref.1) | copy-start | bytes 586
  3.0 6.6 %copy-start.10 = (bf16[49]{0:T(256)(128)(2,1)S(1)}, bf16[49]{0:T(256)(128)(2,1)}, u32[]{:S(2)}) copy-start(bf16[49]{0:T(256)(128)(2,1)} %sx_ref.1) | copy-start | bytes 298
  3.0 6.6 %copy-start.11 = (bf16[49]{0:T(256)(128)(2,1)S(1)}, bf16[49]{0:T(256)(128)(2,1)}, u32[]{:S(2)}) copy-start(bf16[49]{0:T(256)(128)(2,1)} %sy_ref.1) | copy-start | bytes 298
  3.3 6.5 %collective-permute-start = (bf16[3072,128]{1,0:T(8,128)(2,1)S(1)}, bf16[3072,128]{1,0:T(8,128)(2,1)S(1)}, u32[]{:S(2)}, u32[]{:S(2)}) collective-permute-start(bf16[3072,128]{1,0:T(8,128)(2,1)S(1)} %get-tuple-element.19.sent_ref), channel_id=1, source_target_pairs={{0,1},{1,0},{2,3},{3,2},{4,5},{5,4},{6,7},{7,6},{8,9},{9,8},{10,11... | collective-permute-start | bytes 2359304 | tf_op jit(solution)/shard_map/ppermute | solution.py:368
  3.4 12.7 %collective-permute-start.1 = (bf16[3072,128]{1,0:T(8,128)(2,1)S(1)}, bf16[3072,128]{1,0:T(8,128)(2,1)S(1)}, u32[]{:S(2)}, u32[]{:S(2)}) collective-permute-start(bf16[3072,128]{1,0:T(8,128)(2,1)S(1)} %get-tuple-element.21), channel_id=1, source_target_pairs={{0,7},{1,2},{2,1},{3,4},{4,3},{5,6},{6,5},{7,0},{8,15},{9,10},{10,... | collective-permute-start | bytes 2359304 | tf_op jit(solution)/shard_map/ppermute | solution.py:368
  6.3 15.4 %collective-permute-start.4 = (bf16[48,48,128]{2,1,0:T(8,128)(2,1)S(1)}, bf16[48,48,128]{2,1,0:T(8,128)(2,1)S(1)}, u32[]{:S(2)}, u32[]{:S(2)}) collective-permute-start(bf16[48,48,128]{2,1,0:T(8,128)(2,1)S(1)} %get-tuple-element.25.own_ref), channel_id=1, source_target_pairs={{0,8},{8,0},{16,24},{24,16},{32,40},{40,32},{48,56},{56,48},{64,72... | collective-permute-start | bytes 1769480 | tf_op jit(solution)/shard_map/ppermute | solution.py:379
  7.9 17.2 %collective-permute-start.5 = (bf16[48,48,128]{2,1,0:T(8,128)(2,1)S(1)}, bf16[48,48,128]{2,1,0:T(8,128)(2,1)S(1)}, u32[]{:S(2)}, u32[]{:S(2)}) collective-permute-start(bf16[48,48,128]{2,1,0:T(8,128)(2,1)S(1)} %get-tuple-element.25.own_ref), channel_id=1, source_target_pairs={{0,1},{1,0},{2,3},{3,2},{4,5},{5,4},{6,7},{7,6},{8,16},{9,17},{10,... | collective-permute-start | bytes 1769480 | tf_op jit(solution)/shard_map/ppermute | solution.py:379
  16.8 20.7 %collective-permute-start.2 = (bf16[60,48,128]{2,1,0:T(8,128)(2,1)S(1)}, bf16[60,48,128]{2,1,0:T(8,128)(2,1)S(1)}, u32[]{:S(2)}, u32[]{:S(2)}) collective-permute-start(bf16[60,48,128]{2,1,0:T(8,128)(2,1)S(1)} %get-tuple-element.22.own_ref), channel_id=1, source_target_pairs={{0,8},{8,0},{16,24},{24,16},{32,40},{40,32},{48,56},{56,48},{64,72... | collective-permute-start | bytes 2211848 | tf_op jit(solution)/shard_map/ppermute | solution.py:379
  18.4 18.4 %copy-start = (bf16[2,48,48,128]{3,2,1,0:T(8,128)(2,1)S(1)}, bf16[2,48,48,128]{3,2,1,0:T(8,128)(2,1)}, u32[]{:S(2)}) copy-start(bf16[2,48,48,128]{3,2,1,0:T(8,128)(2,1)} %pert_ref.5) | copy-start | bytes 3538948
  18.4 18.4 %copy-start.6 = (bf16[128,128]{1,0:T(8,128)(2,1)S(1)}, bf16[128,128]{1,0:T(8,128)(2,1)}, u32[]{:S(2)}) copy-start(bf16[128,128]{1,0:T(8,128)(2,1)} %vert_ref.5) | copy-start | bytes 98308
  18.4 21.1 %collective-permute-start.3 = (bf16[60,48,128]{2,1,0:T(8,128)(2,1)S(1)}, bf16[60,48,128]{2,1,0:T(8,128)(2,1)S(1)}, u32[]{:S(2)}, u32[]{:S(2)}) collective-permute-start(bf16[60,48,128]{2,1,0:T(8,128)(2,1)S(1)} %get-tuple-element.23), channel_id=1, source_target_pairs={{0,1},{1,0},{2,3},{3,2},{4,5},{5,4},{6,7},{7,6},{8,16},{9,17},{10,... | collective-permute-start | bytes 2211848 | tf_op jit(solution)/shard_map/ppermute | solution.py:379
  26.1 13.5 %copy-start.7 = (bf16[128,128]{1,0:T(8,128)(2,1)S(1)}, bf16[128,128]{1,0:T(8,128)(2,1)}, u32[]{:S(2)}) copy-start(bf16[128,128]{1,0:T(8,128)(2,1)} %static_ref.5) | copy-start | bytes 98308
  26.1 2.1 %collective-permute-start.6 = (bf16[48,48,128]{2,1,0:T(8,128)(2,1)S(1)}, bf16[48,48,128]{2,1,0:T(8,128)(2,1)S(1)}, u32[]{:S(2)}, u32[]{:S(2)}) collective-permute-start(bf16[48,48,128]{2,1,0:T(8,128)(2,1)S(1)} %shard_map.125.own_ref), channel_id=1, source_target_pairs={{0,1},{1,0},{2,3},{3,2},{4,5},{5,4},{6,7},{7,6},{8,9},{9,8},{10,11... | collective-permute-start | bytes 1769480 | tf_op jit(solution)/shard_map/ppermute | solution.py:368
  26.2 10.6 %collective-permute-start.7 = (bf16[48,48,128]{2,1,0:T(8,128)(2,1)S(1)}, bf16[48,48,128]{2,1,0:T(8,128)(2,1)S(1)}, u32[]{:S(2)}, u32[]{:S(2)}) collective-permute-start(bf16[48,48,128]{2,1,0:T(8,128)(2,1)S(1)} %shard_map.125.own_ref), channel_id=1, source_target_pairs={{0,7},{1,2},{2,1},{3,4},{4,3},{5,6},{6,5},{7,0},{8,15},{9,10},{10,... | collective-permute-start | bytes 1769480 | tf_op jit(solution)/shard_map/ppermute | solution.py:368
  39.6 33.2 %copy-start.4 = (bf16[48,48,128]{2,1,0:T(8,128)(2,1)S(1)}, bf16[48,48,128]{2,1,0:T(8,128)(2,1)}, u32[]{:S(2)}) copy-start(bf16[48,48,128]{2,1,0:T(8,128)(2,1)} %dep_ref.1) | copy-start | bytes 1769476
  39.6 33.2 %copy-start.5 = (bf16[48,48,128]{2,1,0:T(8,128)(2,1)S(1)}, bf16[48,48,128]{2,1,0:T(8,128)(2,1)}, u32[]{:S(2)}) copy-start(bf16[48,48,128]{2,1,0:T(8,128)(2,1)} %weight_ref.1) | copy-start | bytes 1769476
  41.4 31.3 %collective-permute-start.8 = (bf16[48,48,128]{2,1,0:T(8,128)(2,1)S(1)}, bf16[48,48,128]{2,1,0:T(8,128)(2,1)S(1)}, u32[]{:S(2)}, u32[]{:S(2)}) collective-permute-start(bf16[48,48,128]{2,1,0:T(8,128)(2,1)S(1)} %get-tuple-element.27), channel_id=1, source_target_pairs={{0,128},{128,0},{1,129},{129,1},{2,130},{130,2},{3,131},{131,3},{4... | collective-permute-start | bytes 1769480 | tf_op jit(solution)/shard_map/ppermute | solution.py:430
  73.7 17.9 %collective-permute-start.9 = (bf16[60,48,128]{2,1,0:T(8,128)(2,1)S(1)}, bf16[60,48,128]{2,1,0:T(8,128)(2,1)S(1)}, u32[]{:S(2)}, u32[]{:S(2)}) collective-permute-start(bf16[60,48,128]{2,1,0:T(8,128)(2,1)S(1)} %get-tuple-element.28.sent_ref), channel_id=1, source_target_pairs={{0,8},{8,0},{16,24},{24,16},{32,40},{40,32},{48,56},{56,48},{64,72... | collective-permute-start | bytes 2211848 | tf_op jit(solution)/shard_map/ppermute | solution.py:379
  73.8 18.7 %collective-permute-start.10 = (bf16[60,48,128]{2,1,0:T(8,128)(2,1)S(1)}, bf16[60,48,128]{2,1,0:T(8,128)(2,1)S(1)}, u32[]{:S(2)}, u32[]{:S(2)}) collective-permute-start(bf16[60,48,128]{2,1,0:T(8,128)(2,1)S(1)} %get-tuple-element.30), channel_id=1, source_target_pairs={{0,1},{1,0},{2,3},{3,2},{4,5},{5,4},{6,7},{7,6},{8,16},{9,17},{10,... | collective-permute-start | bytes 2211848 | tf_op jit(solution)/shard_map/ppermute | solution.py:379
  75.1 3.1 %collective-permute-start.11 = (bf16[48,48,128]{2,1,0:T(8,128)(2,1)S(1)}, bf16[48,48,128]{2,1,0:T(8,128)(2,1)S(1)}, u32[]{:S(2)}, u32[]{:S(2)}) collective-permute-start(bf16[48,48,128]{2,1,0:T(8,128)(2,1)S(1)} %get-tuple-element.31.own_ref), channel_id=1, source_target_pairs={{0,1},{1,0},{2,3},{3,2},{4,5},{5,4},{6,7},{7,6},{8,9},{9,8},{10,11... | collective-permute-start | bytes 1769480 | tf_op jit(solution)/shard_map/ppermute | solution.py:368
  75.1 10.6 %collective-permute-start.12 = (bf16[48,48,128]{2,1,0:T(8,128)(2,1)S(1)}, bf16[48,48,128]{2,1,0:T(8,128)(2,1)S(1)}, u32[]{:S(2)}, u32[]{:S(2)}) collective-permute-start(bf16[48,48,128]{2,1,0:T(8,128)(2,1)S(1)} %get-tuple-element.31.own_ref), channel_id=1, source_target_pairs={{0,7},{1,2},{2,1},{3,4},{4,3},{5,6},{6,5},{7,0},{8,15},{9,10},{10,... | collective-permute-start | bytes 1769480 | tf_op jit(solution)/shard_map/ppermute | solution.py:368
  86.2 16.7 %collective-permute-start.16 = (bf16[48,48,128]{2,1,0:T(8,128)(2,1)S(1)}, bf16[48,48,128]{2,1,0:T(8,128)(2,1)S(1)}, u32[]{:S(2)}, u32[]{:S(2)}) collective-permute-start(bf16[48,48,128]{2,1,0:T(8,128)(2,1)S(1)} %shard_map.129.after_ref.own_ref), channel_id=1, source_target_pairs={{0,8},{8,0},{16,24},{24,16},{32,40},{40,32},{48,56},{56,48},{64,72... | collective-permute-start | bytes 1769480 | tf_op jit(solution)/shard_map/ppermute | solution.py:379
  87.9 17.2 %collective-permute-start.17 = (bf16[48,48,128]{2,1,0:T(8,128)(2,1)S(1)}, bf16[48,48,128]{2,1,0:T(8,128)(2,1)S(1)}, u32[]{:S(2)}, u32[]{:S(2)}) collective-permute-start(bf16[48,48,128]{2,1,0:T(8,128)(2,1)S(1)} %shard_map.129.after_ref.own_ref), channel_id=1, source_target_pairs={{0,1},{1,0},{2,3},{3,2},{4,5},{5,4},{6,7},{7,6},{8,16},{9,17},{10,... | collective-permute-start | bytes 1769480 | tf_op jit(solution)/shard_map/ppermute | solution.py:379
  92.5 12.6 %copy-start.2 = (bf16[2,48,48,128]{3,2,1,0:T(8,128)(2,1)S(1)}, bf16[2,48,48,128]{3,2,1,0:T(8,128)(2,1)}, u32[]{:S(2)}) copy-start(bf16[2,48,48,128]{3,2,1,0:T(8,128)(2,1)} %member_ref.5) | copy-start | bytes 3538948
  94.0 15.5 %collective-permute-start.13 = (bf16[64,48,128]{2,1,0:T(8,128)(2,1)S(1)}, bf16[64,48,128]{2,1,0:T(8,128)(2,1)S(1)}, u32[]{:S(2)}, u32[]{:S(2)}) collective-permute-start(bf16[64,48,128]{2,1,0:T(8,128)(2,1)S(1)} %get-tuple-element.32.own_ref), channel_id=1, source_target_pairs={{0,1},{1,0},{2,3},{3,2},{4,5},{5,4},{6,7},{7,6},{8,9},{9,8},{10,11... | collective-permute-start | bytes 2359304 | tf_op jit(solution)/shard_map/ppermute | solution.py:368
  94.1 15.4 %collective-permute-start.14 = (bf16[48,48,128]{2,1,0:T(8,128)(2,1)S(1)}, bf16[48,48,128]{2,1,0:T(8,128)(2,1)S(1)}, u32[]{:S(2)}, u32[]{:S(2)}) collective-permute-start(bf16[48,48,128]{2,1,0:T(8,128)(2,1)S(1)} %get-tuple-element.33), channel_id=1, source_target_pairs={{0,7},{1,2},{2,1},{3,4},{4,3},{5,6},{6,5},{7,0},{8,15},{9,10},{10,... | collective-permute-start | bytes 1769480 | tf_op jit(solution)/shard_map/ppermute | solution.py:368
  99.9 9.7 %collective-permute-start.15 = (bf16[16,48,128]{2,1,0:T(8,128)(2,1)S(1)}, bf16[16,48,128]{2,1,0:T(8,128)(2,1)S(1)}, u32[]{:S(2)}, u32[]{:S(2)}) collective-permute-start(bf16[16,48,128]{2,1,0:T(8,128)(2,1)S(1)} %get-tuple-element.34), channel_id=1, source_target_pairs={{0,7},{1,2},{2,1},{3,4},{4,3},{5,6},{6,5},{7,0},{8,15},{9,10},{10,... | collective-permute-start | bytes 589832 | tf_op jit(solution)/shard_map/ppermute | solution.py:368

commit v5 on v4

--- a/solution.py
+++ b/solution.py
@@ -196,10 +196,10 @@
     along_y(matrix, line, TILE, store)
 
 
-def second_x(rows, taps_ref, own_ref, even_ref, odd_ref, s_ref, block):
+def second_x(cols, rows, taps_ref, own_ref, even_ref, odd_ref, s_ref, block):
     matrix = band_swapped(taps_ref[rows[0] : rows[0] + 1], "tx")
     matrix_s = band(taps_ref[rows[1] : rows[1] + 1], 24, 72)
-    for c in range(0, TILE, 16):
+    for c in range(cols[0], cols[1], 16):
         at = slice(c, c + 16)
         b = along_x(matrix, [even_ref[:TILE, at], own_ref[:TILE, at], odd_ref[:TILE, at]])
         left, right = sides(even_ref[TILE:, at], odd_ref[TILE:, at], "tx")
@@ -235,8 +235,8 @@
 
 
 def forward_b_kernel(
-    rows, taps_ref, own_ref, even_ref, odd_ref, s_ref, first_ref, pert_ref, vert_ref, static_ref,
-    kept_ref, sent_ref
+    cols, rows, taps_ref, own_ref, even_ref, odd_ref, s_ref, first_ref, pert_ref, vert_ref, static_ref,
+    after_ref, kept_ref, sent_ref
 ):
     vert = vert_ref[...]
     static_mat = static_block(static_ref)
@@ -246,14 +246,15 @@
         total += pert_ref[1, :, at].astype(F32) * dot_t(b.reshape(768, 128), vert).reshape(TILE, 16, 128)
         static = dot_t(s.reshape(384, 128), static_mat)
         total += jnp.concatenate([static[:, :128], static[:, 128:]], axis=0).reshape(TILE, 16, 128)
-        kept_ref[:, at] = total
-        sent_ref[:, at] = total.astype(BF)
-
-    second_x(rows, taps_ref, own_ref, even_ref, odd_ref, s_ref, block)
+        to = slice(at.start - cols[0], at.stop - cols[0])
+        kept_ref[:, to] = total
+        sent_ref[:, to] = total.astype(BF)
+
+    second_x(cols, rows, taps_ref, own_ref, even_ref, odd_ref, s_ref, block)
 
 
 def residual_kernel(
-    kept_ref, came_ref, dep_ref, weight_ref, pert_ref, vert_ref, static_ref, even_ref, odd_ref, own_ref, b_ref
+    kept0, came0, kept1, came1, dep_ref, weight_ref, pert_ref, vert_ref, static_ref, even_ref, odd_ref, own_ref, b_ref
 ):
     vert = vert_ref[...]
     static_mat = static_block(static_ref)
@@ -262,7 +263,8 @@
         res = []
         for x in (4 * i, 24 + 4 * i):
             at = pl.ds(x, 4)
-            total = kept_ref[at] + came_ref[at].astype(F32)
+            parts = [kept[at] + came[at].astype(F32) for kept, came in ((kept0, came0), (kept1, came1))]
+            total = jnp.concatenate(parts, axis=1)
             r = (weight_ref[at].astype(F32) * (total - dep_ref[at].astype(F32))).astype(BF)
             r32 = r.astype(F32)
             res.append(r.reshape(192, 128))
@@ -422,16 +424,20 @@
         functools.partial(forward_a_kernel, 1), (shape(*tile, dtype=F32),),
         (taps,) + a + (perturbations, local_vertical), 800_000_000, [pltpu.VMEM(tile, BF)],
     )
-    kept, sent = call(
-        functools.partial(forward_b_kernel, (0, 2)), (shape(*tile, dtype=F32), shape(*tile)),
-        (taps,) + b + (first, perturbations, local_vertical, static_vertical), 1_000_000_000,
-    )
     size = lax.axis_size("mem")
-    came = lax.ppermute(sent, "mem", [(i, size - 1 - i) for i in range(size)])
+    parts, sent = (), first
+    for cols, cost in (((0, 32), 700_000_000), ((32, TILE), LONG)):
+        wide = (TILE, cols[1] - cols[0], 128)
+        args = (taps,) + b + (first, perturbations, local_vertical, static_vertical, sent)
+        kept, sent = call(
+            functools.partial(forward_b_kernel, cols, (0, 2)), (shape(*wide, dtype=F32), shape(*wide)),
+            args, cost, in_any=(len(args) - 1,),
+        )
+        parts += (kept, lax.ppermute(sent, "mem", [(i, size - 1 - i) for i in range(size)]))
 
     to_even, to_odd, own, b = call(
         residual_kernel, (shape(60, TILE, 128), shape(60, TILE, 128), shape(24, TILE, 128), shape(*tile)),
-        (kept, came, departures, obs_weight, perturbations, local_vertical, static_vertical), 400_000_000,
+        parts + (departures, obs_weight, perturbations, local_vertical, static_vertical), 400_000_000,
     )
     a = (to_even, own) + swaps_x(to_even, to_odd)
     (b,) = call(functools.partial(back_y_kernel, 5), (shape(*tile),), (taps, b) + swaps_y(b, b), BRIEF)

time: 112 us -> 112 us (level)
    ppermute x1 -> x2, waiting for transfers between devices: 25 us -> 24.1 us  [body(): lax.ppermute(sent, 'mem', [(i, size - 1 - i) for i in range(size)])]
    pallas_call x11 -> x12, Pallas kernels: 10.8 us -> 10.9 us  [call(): pl.pallas_call(kernel, out_shape=outs, in_specs=[ANY if i in in_any else...]
    ppermute x1 -> x2, starting transfers between devices: 6.38 us -> 6.48 us  [body(): lax.ppermute(sent, 'mem', [(i, size - 1 - i) for i in range(size)])]
  transfers between devices with their start and end apart: 18 -> 19, of which waited for: 13 -> 13; matrix products, arithmetic and copies ran while one was open for 0% -> 0% of each run, Pallas kernels for 5% -> 6%
where the time goes in v5:
time: 112 us; the launch traced here: 111 us
  waiting for transfers between devices  66.3 us (59%)
  starting transfers between devices  30.2 us (27%)
  Pallas kernels  10.9 us (10%)
  local copies, waits for them, and re-layouts  2.37 us (2%)
    ppermute x5, waiting for transfers between devices, swaps_y(): lax.ppermute(part, 'ty', second)  25.2 us
    ppermute x2, waiting for transfers between devices, body(): lax.ppermute(sent, 'mem', [(i, size - 1 - i) for i in range(size)])  24.1 us
    ppermute x5, starting transfers between devices, swaps_y(): lax.ppermute(part, 'ty', second)  12.2 us
    pallas_call x12, Pallas kernels, call(): pl.pallas_call(kernel, out_shape=outs, in_specs=[ANY if i in in_any else...  10.9 us
    ppermute x4, waiting for transfers between devices, swaps_x(): lax.ppermute(odd, ('tx', 'ty'), second)  8.59 us
    ppermute x4, waiting for transfers between devices, swaps_x(): lax.ppermute(even, 'tx', first)  6.87 us
    ppermute x2, starting transfers between devices, body(): lax.ppermute(sent, 'mem', [(i, size - 1 - i) for i in range(size)])  6.48 us
    ppermute x4, starting transfers between devices, swaps_x(): lax.ppermute(odd, ('tx', 'ty'), second)  6.15 us
  transfers between devices with their start and end apart: 19, of which 13 were waited for; matrix products, arithmetic and copies ran while one was open for 0% of the time, Pallas kernels for 6%

profile of v5, /device:TPU:32, one launch (start us, length us, event | category | flops | bytes accessed | tf_op | source)
XLA Modules:
  0.0 110.7 jit_solution(6827728432789836462)
XLA Ops:
  0.6 0.0 copy-start.1
  0.6 1.3 %copy-done.1 = bf16[2,48,48,128]{3,2,1,0:T(8,128)(2,1)S(1)} copy-done((bf16[2,48,48,128]{3,2,1,0:T(8,128)(2,1)S(1)}, bf16[2,48,48,128]{3,2,1,0:T(8,128)(2,1)}, u32[]{:S(2)}) %copy-start.1) | copy-done | bytes 1179672
  1.9 1.1 copy-done.3
  3.0 0.3 shard_map.123
  3.3 0.1 collective-permute-start
  3.4 2.9 %collective-permute-start.1 = (bf16[3072,128]{1,0:T(8,128)(2,1)S(1)}, bf16[3072,128]{1,0:T(8,128)(2,1)S(1)}, u32[]{:S(2)}, u32[]{:S(2)}) collective-permute-start(bf16[3072,128]{1,0:T(8,128)(2,1)S(1)} %get-tuple-element.23), channel_id=1, source_target_pairs={{0,7},{1,2},{2,1},{3,4},{4,3},{5,6},{6,5},{7,0},{8,15},{9,10},{10,... | collective-permute-start | bytes 2359304 | tf_op jit(solution)/shard_map/ppermute | solution.py:370
  6.3 1.6 %collective-permute-start.4 = (bf16[48,48,128]{2,1,0:T(8,128)(2,1)S(1)}, bf16[48,48,128]{2,1,0:T(8,128)(2,1)S(1)}, u32[]{:S(2)}, u32[]{:S(2)}) collective-permute-start(bf16[48,48,128]{2,1,0:T(8,128)(2,1)S(1)} %get-tuple-element.27.own_ref), channel_id=1, source_target_pairs={{0,8},{8,0},{16,24},{24,16},{32,40},{40,32},{48,56},{56,48},{64,72... | collective-permute-start | bytes 1769480 | tf_op jit(solution)/shard_map/ppermute | solution.py:381
  7.9 1.7 %collective-permute-start.5 = (bf16[48,48,128]{2,1,0:T(8,128)(2,1)S(1)}, bf16[48,48,128]{2,1,0:T(8,128)(2,1)S(1)}, u32[]{:S(2)}, u32[]{:S(2)}) collective-permute-start(bf16[48,48,128]{2,1,0:T(8,128)(2,1)S(1)} %get-tuple-element.27.own_ref), channel_id=1, source_target_pairs={{0,1},{1,0},{2,3},{3,2},{4,5},{5,4},{6,7},{7,6},{8,16},{9,17},{10,... | collective-permute-start | bytes 1769480 | tf_op jit(solution)/shard_map/ppermute | solution.py:381
  9.6 0.0 copy-done.8
  9.6 0.0 copy-done.9
  9.6 0.0 copy-done.10
  9.6 0.0 copy-done.11
  9.6 0.2 shard_map.122.taps_ref
  9.8 0.0 collective-permute-done.even_ref
  9.8 6.4 %collective-permute-done.1.odd_ref = bf16[3072,128]{1,0:T(8,128)(2,1)S(1)} collective-permute-done((bf16[3072,128]{1,0:T(8,128)(2,1)S(1)}, bf16[3072,128]{1,0:T(8,128)(2,1)S(1)}, u32[]{:S(2)}, u32[]{:S(2)}) %collective-permute-start.1) | collective-permute-done | bytes 786464 | tf_op jit(solution)/shard_map/ppermute | solution.py:370
  16.1 0.6 shard_map.124
  16.8 1.7 %collective-permute-start.2 = (bf16[60,48,128]{2,1,0:T(8,128)(2,1)S(1)}, bf16[60,48,128]{2,1,0:T(8,128)(2,1)S(1)}, u32[]{:S(2)}, u32[]{:S(2)}) collective-permute-start(bf16[60,48,128]{2,1,0:T(8,128)(2,1)S(1)} %get-tuple-element.24.own_ref), channel_id=1, source_target_pairs={{0,8},{8,0},{16,24},{24,16},{32,40},{40,32},{48,56},{56,48},{64,72... | collective-permute-start | bytes 2211848 | tf_op jit(solution)/shard_map/ppermute | solution.py:381
  18.5 1.7 %collective-permute-start.3 = (bf16[60,48,128]{2,1,0:T(8,128)(2,1)S(1)}, bf16[60,48,128]{2,1,0:T(8,128)(2,1)S(1)}, u32[]{:S(2)}, u32[]{:S(2)}) collective-permute-start(bf16[60,48,128]{2,1,0:T(8,128)(2,1)S(1)} %get-tuple-element.25), channel_id=1, source_target_pairs={{0,1},{1,0},{2,3},{3,2},{4,5},{5,4},{6,7},{7,6},{8,16},{9,17},{10,... | collective-permute-start | bytes 2211848 | tf_op jit(solution)/shard_map/ppermute | solution.py:381
  20.2 1.5 %collective-permute-done.4.even_ref = bf16[48,48,128]{2,1,0:T(8,128)(2,1)S(1)} collective-permute-done((bf16[48,48,128]{2,1,0:T(8,128)(2,1)S(1)}, bf16[48,48,128]{2,1,0:T(8,128)(2,1)S(1)}, u32[]{:S(2)}, u32[]{:S(2)}) %collective-permute-start.4) | collective-permute-done | bytes 589856 | tf_op jit(solution)/shard_map/ppermute | solution.py:381
  21.7 3.4 %collective-permute-done.5.odd_ref = bf16[48,48,128]{2,1,0:T(8,128)(2,1)S(1)} collective-permute-done((bf16[48,48,128]{2,1,0:T(8,128)(2,1)S(1)}, bf16[48,48,128]{2,1,0:T(8,128)(2,1)S(1)}, u32[]{:S(2)}, u32[]{:S(2)}) %collective-permute-start.5) | collective-permute-done | bytes 589856 | tf_op jit(solution)/shard_map/ppermute | solution.py:381
  25.1 1.0 shard_map.125.own_ref
  26.1 0.0 copy-start.7
  26.1 0.1 collective-permute-start.6
  26.2 0.5 collective-permute-start.7
  26.7 1.5 %collective-permute-done.6.even_ref = bf16[48,48,128]{2,1,0:T(8,128)(2,1)S(1)} collective-permute-done((bf16[48,48,128]{2,1,0:T(8,128)(2,1)S(1)}, bf16[48,48,128]{2,1,0:T(8,128)(2,1)S(1)}, u32[]{:S(2)}, u32[]{:S(2)}) %collective-permute-start.6) | collective-permute-done | bytes 589856 | tf_op jit(solution)/shard_map/ppermute | solution.py:370
  28.2 8.6 %collective-permute-done.7.odd_ref = bf16[48,48,128]{2,1,0:T(8,128)(2,1)S(1)} collective-permute-done((bf16[48,48,128]{2,1,0:T(8,128)(2,1)S(1)}, bf16[48,48,128]{2,1,0:T(8,128)(2,1)S(1)}, u32[]{:S(2)}, u32[]{:S(2)}) %collective-permute-start.7) | collective-permute-done | bytes 589856 | tf_op jit(solution)/shard_map/ppermute | solution.py:370
  36.8 0.0 copy-done
  36.8 0.0 copy-done.6
  36.8 0.6 shard_map.126.first_ref.after_ref
  37.4 0.0 collective-permute-done.2.even_ref
  37.4 2.1 %collective-permute-done.3.odd_ref = bf16[60,48,128]{2,1,0:T(8,128)(2,1)S(1)} collective-permute-done((bf16[60,48,128]{2,1,0:T(8,128)(2,1)S(1)}, bf16[60,48,128]{2,1,0:T(8,128)(2,1)S(1)}, u32[]{:S(2)}, u32[]{:S(2)}) %collective-permute-start.3) | collective-permute-done | bytes 737312 | tf_op jit(solution)/shard_map/ppermute | solution.py:381
  39.6 0.0 copy-done.7
  39.6 1.3 %shard_map.127 = (f32[48,32,128]{2,1,0:T(8,128)S(1)}, bf16[48,32,128]{2,1,0:T(8,128)(2,1)S(1)}) custom-call(f32[8,256]{1,0:T(8,128)S(1)} %shard_map.122.taps_ref, bf16[60,48,128]{2,1,0:T(8,128)(2,1)S(1)} %get-tuple-element.24.own_ref, bf16[60,48,128]{2,1,0:T(8,128)(2,1)S(1)} %collective-permute-done.2.even_ref, ...), custom_call_target="tpu_custom_call" | custom-call | flops 700000000 | bytes 7299072 | tf_op jit(solution)/shard_map/pallas_call | solution.py:26
  40.8 0.0 copy-start.4
  40.9 0.0 copy-start.5
  40.9 6.4 %collective-permute-start.8 = (bf16[48,32,128]{2,1,0:T(8,128)(2,1)S(1)}, bf16[48,32,128]{2,1,0:T(8,128)(2,1)S(1)}, u32[]{:S(2)}, u32[]{:S(2)}) collective-permute-start(bf16[48,32,128]{2,1,0:T(8,128)(2,1)S(1)} %get-tuple-element.29.after_ref), channel_id=1, source_target_pairs={{0,128},{128,0},{1,129},{129,1},{2,130},{130,2},{3,131},{131,3},{4... | collective-permute-start | bytes 1179656 | tf_op jit(solution)/shard_map/ppermute | solution.py:436
  47.2 0.7 shard_map.128
  48.0 0.1 collective-permute-start.9
  48.1 24.1 %collective-permute-done.9.came1 = bf16[48,16,128]{2,1,0:T(8,128)(2,1)S(1)} collective-permute-done((bf16[48,16,128]{2,1,0:T(8,128)(2,1)S(1)}, bf16[48,16,128]{2,1,0:T(8,128)(2,1)S(1)}, u32[]{:S(2)}, u32[]{:S(2)}) %collective-permute-start.9) | collective-permute-done | bytes 196640 | tf_op jit(solution)/shard_map/ppermute | solution.py:436
  72.2 0.0 collective-permute-done.8.came0
  72.2 0.0 copy-done.5
  72.2 0.9 shard_map.129
  73.2 0.1 collective-permute-start.10
  73.3 1.3 %collective-permute-start.11 = (bf16[60,48,128]{2,1,0:T(8,128)(2,1)S(1)}, bf16[60,48,128]{2,1,0:T(8,128)(2,1)S(1)}, u32[]{:S(2)}, u32[]{:S(2)}) collective-permute-start(bf16[60,48,128]{2,1,0:T(8,128)(2,1)S(1)} %get-tuple-element.34), channel_id=1, source_target_pairs={{0,1},{1,0},{2,3},{3,2},{4,5},{5,4},{6,7},{7,6},{8,16},{9,17},{10,... | collective-permute-start | bytes 2211848 | tf_op jit(solution)/shard_map/ppermute | solution.py:381
  74.6 0.0 collective-permute-start.12
  74.6 3.1 %collective-permute-start.13 = (bf16[48,48,128]{2,1,0:T(8,128)(2,1)S(1)}, bf16[48,48,128]{2,1,0:T(8,128)(2,1)S(1)}, u32[]{:S(2)}, u32[]{:S(2)}) collective-permute-start(bf16[48,48,128]{2,1,0:T(8,128)(2,1)S(1)} %get-tuple-element.35.own_ref), channel_id=1, source_target_pairs={{0,7},{1,2},{2,1},{3,4},{4,3},{5,6},{6,5},{7,0},{8,15},{9,10},{10,... | collective-permute-start | bytes 1769480 | tf_op jit(solution)/shard_map/ppermute | solution.py:370
  77.6 0.0 collective-permute-done.12.even_ref
  77.6 7.6 %collective-permute-done.13.odd_ref = bf16[48,48,128]{2,1,0:T(8,128)(2,1)S(1)} collective-permute-done((bf16[48,48,128]{2,1,0:T(8,128)(2,1)S(1)}, bf16[48,48,128]{2,1,0:T(8,128)(2,1)S(1)}, u32[]{:S(2)}, u32[]{:S(2)}) %collective-permute-start.13) | collective-permute-done | bytes 589856 | tf_op jit(solution)/shard_map/ppermute | solution.py:370
  85.2 0.4 shard_map.130.after_ref.own_ref
  85.6 1.7 %collective-permute-start.17 = (bf16[48,48,128]{2,1,0:T(8,128)(2,1)S(1)}, bf16[48,48,128]{2,1,0:T(8,128)(2,1)S(1)}, u32[]{:S(2)}, u32[]{:S(2)}) collective-permute-start(bf16[48,48,128]{2,1,0:T(8,128)(2,1)S(1)} %shard_map.130.after_ref.own_ref), channel_id=1, source_target_pairs={{0,8},{8,0},{16,24},{24,16},{32,40},{40,32},{48,56},{56,48},{64,72... | collective-permute-start | bytes 1769480 | tf_op jit(solution)/shard_map/ppermute | solution.py:381
  87.3 1.4 %collective-permute-start.18 = (bf16[48,48,128]{2,1,0:T(8,128)(2,1)S(1)}, bf16[48,48,128]{2,1,0:T(8,128)(2,1)S(1)}, u32[]{:S(2)}, u32[]{:S(2)}) collective-permute-start(bf16[48,48,128]{2,1,0:T(8,128)(2,1)S(1)} %shard_map.130.after_ref.own_ref), channel_id=1, source_target_pairs={{0,1},{1,0},{2,3},{3,2},{4,5},{5,4},{6,7},{7,6},{8,16},{9,17},{10,... | collective-permute-start | bytes 1769480 | tf_op jit(solution)/shard_map/ppermute | solution.py:381
  88.8 2.3 %collective-permute-done.10.even_ref = bf16[60,48,128]{2,1,0:T(8,128)(2,1)S(1)} collective-permute-done((bf16[60,48,128]{2,1,0:T(8,128)(2,1)S(1)}, bf16[60,48,128]{2,1,0:T(8,128)(2,1)S(1)}, u32[]{:S(2)}, u32[]{:S(2)}) %collective-permute-start.10) | collective-permute-done | bytes 737312 | tf_op jit(solution)/shard_map/ppermute | solution.py:381
  91.1 0.9 collective-permute-done.11.odd_ref
  91.9 1.5 %shard_map.131 = (bf16[64,48,128]{2,1,0:T(8,128)(2,1)S(1)}, bf16[48,48,128]{2,1,0:T(8,128)(2,1)S(1)}, bf16[16,48,128]{2,1,0:T(8,128)(2,1)S(1)}, bf16[24,48,128]{2,1,0:T(8,128)(2,1)S(1)}) custom-call(f32[8,256]{1,0:T(8,128)S(1)} %shard_map.122.taps_ref, bf16[60,48,128]{2,1,0:T(8,128)(2,1)S(1)} %get-tuple-element.32.sent_ref, ...), custom_call_target="tpu_custom_call" | custom-call | flops 20000000000 | bytes 4972544 | tf_op jit(solution)/shard_map/pallas_call | solution.py:26
  93.5 0.1 collective-permute-start.14
  93.6 5.7 %collective-permute-start.15 = (bf16[48,48,128]{2,1,0:T(8,128)(2,1)S(1)}, bf16[48,48,128]{2,1,0:T(8,128)(2,1)S(1)}, u32[]{:S(2)}, u32[]{:S(2)}) collective-permute-start(bf16[48,48,128]{2,1,0:T(8,128)(2,1)S(1)} %get-tuple-element.37), channel_id=1, source_target_pairs={{0,7},{1,2},{2,1},{3,4},{4,3},{5,6},{6,5},{7,0},{8,15},{9,10},{10,... | collective-permute-start | bytes 1769480 | tf_op jit(solution)/shard_map/ppermute | solution.py:370
  99.3 0.0 collective-permute-start.16
  99.4 3.0 %collective-permute-done.17.even_ref = bf16[48,48,128]{2,1,0:T(8,128)(2,1)S(1)} collective-permute-done((bf16[48,48,128]{2,1,0:T(8,128)(2,1)S(1)}, bf16[48,48,128]{2,1,0:T(8,128)(2,1)S(1)}, u32[]{:S(2)}, u32[]{:S(2)}) %collective-permute-start.17) | collective-permute-done | bytes 589856 | tf_op jit(solution)/shard_map/ppermute | solution.py:381
  102.4 2.2 %collective-permute-done.18.odd_ref = bf16[48,48,128]{2,1,0:T(8,128)(2,1)S(1)} collective-permute-done((bf16[48,48,128]{2,1,0:T(8,128)(2,1)S(1)}, bf16[48,48,128]{2,1,0:T(8,128)(2,1)S(1)}, u32[]{:S(2)}, u32[]{:S(2)}) %collective-permute-start.18) | collective-permute-done | bytes 589856 | tf_op jit(solution)/shard_map/ppermute | solution.py:381
  104.6 1.7 %shard_map.132.begun_ref = bf16[2,48,48,128]{3,2,1,0:T(8,128)(2,1)} custom-call(f32[8,256]{1,0:T(8,128)S(1)} %shard_map.122.taps_ref, bf16[48,48,128]{2,1,0:T(8,128)(2,1)S(1)} %shard_map.130.after_ref.own_ref, bf16[48,48,128]{2,1,0:T(8,128)(2,1)S(1)} %collective-permute-done.17.even_ref, bf16[48,48,128]{2,1,0:T(8,128)(2,1)S(1)} %collective-permute-done.18.odd_ref, ...), custom_call_target="tpu_custom_call" | custom-call | flops 20000000000 | bytes 4136960 | tf_op jit(solution)/shard_map/pallas_call | solution.py:26
  106.3 2.7 %collective-permute-done.16.slab_ref = bf16[16,48,128]{2,1,0:T(8,128)(2,1)S(1)} collective-permute-done((bf16[16,48,128]{2,1,0:T(8,128)(2,1)S(1)}, bf16[16,48,128]{2,1,0:T(8,128)(2,1)S(1)}, u32[]{:S(2)}, u32[]{:S(2)}) %collective-permute-start.16) | collective-permute-done | bytes 196640 | tf_op jit(solution)/shard_map/ppermute | solution.py:370
  109.0 0.0 collective-permute-done.15.odd_ref
  109.0 0.0 collective-permute-done.14.even_ref
  109.0 1.5 %shard_map.133 = (bf16[48,48,64]{2,1,0:T(8,128)(2,1)}, bf16[2,48,48,128]{3,2,1,0:T(8,128)(2,1)}) custom-call(f32[8,256]{1,0:T(8,128)S(1)} %shard_map.122.taps_ref, bf16[64,48,128]{2,1,0:T(8,128)(2,1)S(1)} %get-tuple-element.36.own_ref, bf16[64,48,128]{2,1,0:T(8,128)(2,1)S(1)} %collective-permute-done.14.even_ref, ...), custom_call_target="tpu_custom_call", output_to_operand_aliasing={{1}: (8, {})} | custom-call | flops 700000000 | bytes 6791168 | tf_op jit(solution)/shard_map/pallas_call | solution.py:26
  (10 shorter events, 0.0 us)
Async XLA Ops:
  0.6 1.3 %copy-start.1 = (bf16[2,48,48,128]{3,2,1,0:T(8,128)(2,1)S(1)}, bf16[2,48,48,128]{3,2,1,0:T(8,128)(2,1)}, u32[]{:S(2)}) copy-start(bf16[2,48,48,128]{3,2,1,0:T(8,128)(2,1)} %member_ref.5) | copy-start | bytes 3538948
  1.9 1.1 copy-start.3
  3.0 6.6 %copy-start.8 = (bf16[97]{0:T(256)(128)(2,1)S(1)}, bf16[97]{0:T(256)(128)(2,1)}, u32[]{:S(2)}) copy-start(bf16[97]{0:T(256)(128)(2,1)} %lx_ref.1) | copy-start | bytes 586
  3.0 6.6 %copy-start.9 = (bf16[97]{0:T(256)(128)(2,1)S(1)}, bf16[97]{0:T(256)(128)(2,1)}, u32[]{:S(2)}) copy-start(bf16[97]{0:T(256)(128)(2,1)} %ly_ref.1) | copy-start | bytes 586
  3.0 6.6 %copy-start.10 = (bf16[49]{0:T(256)(128)(2,1)S(1)}, bf16[49]{0:T(256)(128)(2,1)}, u32[]{:S(2)}) copy-start(bf16[49]{0:T(256)(128)(2,1)} %sx_ref.1) | copy-start | bytes 298
  3.0 6.6 %copy-start.11 = (bf16[49]{0:T(256)(128)(2,1)S(1)}, bf16[49]{0:T(256)(128)(2,1)}, u32[]{:S(2)}) copy-start(bf16[49]{0:T(256)(128)(2,1)} %sy_ref.1) | copy-start | bytes 298
  3.3 6.5 %collective-permute-start = (bf16[3072,128]{1,0:T(8,128)(2,1)S(1)}, bf16[3072,128]{1,0:T(8,128)(2,1)S(1)}, u32[]{:S(2)}, u32[]{:S(2)}) collective-permute-start(bf16[3072,128]{1,0:T(8,128)(2,1)S(1)} %get-tuple-element.21.sent_ref), channel_id=1, source_target_pairs={{0,1},{1,0},{2,3},{3,2},{4,5},{5,4},{6,7},{7,6},{8,9},{9,8},{10,11... | collective-permute-start | bytes 2359304 | tf_op jit(solution)/shard_map/ppermute | solution.py:370
  3.4 12.7 %collective-permute-start.1 = (bf16[3072,128]{1,0:T(8,128)(2,1)S(1)}, bf16[3072,128]{1,0:T(8,128)(2,1)S(1)}, u32[]{:S(2)}, u32[]{:S(2)}) collective-permute-start(bf16[3072,128]{1,0:T(8,128)(2,1)S(1)} %get-tuple-element.23), channel_id=1, source_target_pairs={{0,7},{1,2},{2,1},{3,4},{4,3},{5,6},{6,5},{7,0},{8,15},{9,10},{10,... | collective-permute-start | bytes 2359304 | tf_op jit(solution)/shard_map/ppermute | solution.py:370
  6.3 15.4 %collective-permute-start.4 = (bf16[48,48,128]{2,1,0:T(8,128)(2,1)S(1)}, bf16[48,48,128]{2,1,0:T(8,128)(2,1)S(1)}, u32[]{:S(2)}, u32[]{:S(2)}) collective-permute-start(bf16[48,48,128]{2,1,0:T(8,128)(2,1)S(1)} %get-tuple-element.27.own_ref), channel_id=1, source_target_pairs={{0,8},{8,0},{16,24},{24,16},{32,40},{40,32},{48,56},{56,48},{64,72... | collective-permute-start | bytes 1769480 | tf_op jit(solution)/shard_map/ppermute | solution.py:381
  7.9 17.2 %collective-permute-start.5 = (bf16[48,48,128]{2,1,0:T(8,128)(2,1)S(1)}, bf16[48,48,128]{2,1,0:T(8,128)(2,1)S(1)}, u32[]{:S(2)}, u32[]{:S(2)}) collective-permute-start(bf16[48,48,128]{2,1,0:T(8,128)(2,1)S(1)} %get-tuple-element.27.own_ref), channel_id=1, source_target_pairs={{0,1},{1,0},{2,3},{3,2},{4,5},{5,4},{6,7},{7,6},{8,16},{9,17},{10,... | collective-permute-start | bytes 1769480 | tf_op jit(solution)/shard_map/ppermute | solution.py:381
  16.8 20.6 %collective-permute-start.2 = (bf16[60,48,128]{2,1,0:T(8,128)(2,1)S(1)}, bf16[60,48,128]{2,1,0:T(8,128)(2,1)S(1)}, u32[]{:S(2)}, u32[]{:S(2)}) collective-permute-start(bf16[60,48,128]{2,1,0:T(8,128)(2,1)S(1)} %get-tuple-element.24.own_ref), channel_id=1, source_target_pairs={{0,8},{8,0},{16,24},{24,16},{32,40},{40,32},{48,56},{56,48},{64,72... | collective-permute-start | bytes 2211848 | tf_op jit(solution)/shard_map/ppermute | solution.py:381
  18.4 18.4 %copy-start = (bf16[2,48,48,128]{3,2,1,0:T(8,128)(2,1)S(1)}, bf16[2,48,48,128]{3,2,1,0:T(8,128)(2,1)}, u32[]{:S(2)}) copy-start(bf16[2,48,48,128]{3,2,1,0:T(8,128)(2,1)} %pert_ref.7) | copy-start | bytes 3538948
  18.4 18.4 %copy-start.6 = (bf16[128,128]{1,0:T(8,128)(2,1)S(1)}, bf16[128,128]{1,0:T(8,128)(2,1)}, u32[]{:S(2)}) copy-start(bf16[128,128]{1,0:T(8,128)(2,1)} %vert_ref.7) | copy-start | bytes 98308
  18.5 21.1 %collective-permute-start.3 = (bf16[60,48,128]{2,1,0:T(8,128)(2,1)S(1)}, bf16[60,48,128]{2,1,0:T(8,128)(2,1)S(1)}, u32[]{:S(2)}, u32[]{:S(2)}) collective-permute-start(bf16[60,48,128]{2,1,0:T(8,128)(2,1)S(1)} %get-tuple-element.25), channel_id=1, source_target_pairs={{0,1},{1,0},{2,3},{3,2},{4,5},{5,4},{6,7},{7,6},{8,16},{9,17},{10,... | collective-permute-start | bytes 2211848 | tf_op jit(solution)/shard_map/ppermute | solution.py:381
  26.1 13.5 %copy-start.7 = (bf16[128,128]{1,0:T(8,128)(2,1)S(1)}, bf16[128,128]{1,0:T(8,128)(2,1)}, u32[]{:S(2)}) copy-start(bf16[128,128]{1,0:T(8,128)(2,1)} %static_ref.7) | copy-start | bytes 98308
  26.1 2.1 %collective-permute-start.6 = (bf16[48,48,128]{2,1,0:T(8,128)(2,1)S(1)}, bf16[48,48,128]{2,1,0:T(8,128)(2,1)S(1)}, u32[]{:S(2)}, u32[]{:S(2)}) collective-permute-start(bf16[48,48,128]{2,1,0:T(8,128)(2,1)S(1)} %shard_map.125.own_ref), channel_id=1, source_target_pairs={{0,1},{1,0},{2,3},{3,2},{4,5},{5,4},{6,7},{7,6},{8,9},{9,8},{10,11... | collective-permute-start | bytes 1769480 | tf_op jit(solution)/shard_map/ppermute | solution.py:370
  26.2 10.6 %collective-permute-start.7 = (bf16[48,48,128]{2,1,0:T(8,128)(2,1)S(1)}, bf16[48,48,128]{2,1,0:T(8,128)(2,1)S(1)}, u32[]{:S(2)}, u32[]{:S(2)}) collective-permute-start(bf16[48,48,128]{2,1,0:T(8,128)(2,1)S(1)} %shard_map.125.own_ref), channel_id=1, source_target_pairs={{0,7},{1,2},{2,1},{3,4},{4,3},{5,6},{6,5},{7,0},{8,15},{9,10},{10,... | collective-permute-start | bytes 1769480 | tf_op jit(solution)/shard_map/ppermute | solution.py:370
  40.8 31.4 %copy-start.4 = (bf16[48,48,128]{2,1,0:T(8,128)(2,1)S(1)}, bf16[48,48,128]{2,1,0:T(8,128)(2,1)}, u32[]{:S(2)}) copy-start(bf16[48,48,128]{2,1,0:T(8,128)(2,1)} %dep_ref.1) | copy-start | bytes 1769476
  40.9 31.4 %copy-start.5 = (bf16[48,48,128]{2,1,0:T(8,128)(2,1)S(1)}, bf16[48,48,128]{2,1,0:T(8,128)(2,1)}, u32[]{:S(2)}) copy-start(bf16[48,48,128]{2,1,0:T(8,128)(2,1)} %weight_ref.1) | copy-start | bytes 1769476
  40.9 31.3 %collective-permute-start.8 = (bf16[48,32,128]{2,1,0:T(8,128)(2,1)S(1)}, bf16[48,32,128]{2,1,0:T(8,128)(2,1)S(1)}, u32[]{:S(2)}, u32[]{:S(2)}) collective-permute-start(bf16[48,32,128]{2,1,0:T(8,128)(2,1)S(1)} %get-tuple-element.29.after_ref), channel_id=1, source_target_pairs={{0,128},{128,0},{1,129},{129,1},{2,130},{130,2},{3,131},{131,3},{4... | collective-permute-start | bytes 1179656 | tf_op jit(solution)/shard_map/ppermute | solution.py:436
  48.0 24.2 %collective-permute-start.9 = (bf16[48,16,128]{2,1,0:T(8,128)(2,1)S(1)}, bf16[48,16,128]{2,1,0:T(8,128)(2,1)S(1)}, u32[]{:S(2)}, u32[]{:S(2)}) collective-permute-start(bf16[48,16,128]{2,1,0:T(8,128)(2,1)S(1)} %get-tuple-element.31), channel_id=1, source_target_pairs={{0,128},{128,0},{1,129},{129,1},{2,130},{130,2},{3,131},{131,3},{4... | collective-permute-start | bytes 589832 | tf_op jit(solution)/shard_map/ppermute | solution.py:436
  73.2 17.9 %collective-permute-start.10 = (bf16[60,48,128]{2,1,0:T(8,128)(2,1)S(1)}, bf16[60,48,128]{2,1,0:T(8,128)(2,1)S(1)}, u32[]{:S(2)}, u32[]{:S(2)}) collective-permute-start(bf16[60,48,128]{2,1,0:T(8,128)(2,1)S(1)} %get-tuple-element.32.sent_ref), channel_id=1, source_target_pairs={{0,8},{8,0},{16,24},{24,16},{32,40},{40,32},{48,56},{56,48},{64,72... | collective-permute-start | bytes 2211848 | tf_op jit(solution)/shard_map/ppermute | solution.py:381
  73.3 18.7 %collective-permute-start.11 = (bf16[60,48,128]{2,1,0:T(8,128)(2,1)S(1)}, bf16[60,48,128]{2,1,0:T(8,128)(2,1)S(1)}, u32[]{:S(2)}, u32[]{:S(2)}) collective-permute-start(bf16[60,48,128]{2,1,0:T(8,128)(2,1)S(1)} %get-tuple-element.34), channel_id=1, source_target_pairs={{0,1},{1,0},{2,3},{3,2},{4,5},{5,4},{6,7},{7,6},{8,16},{9,17},{10,... | collective-permute-start | bytes 2211848 | tf_op jit(solution)/shard_map/ppermute | solution.py:381
  74.6 3.1 %collective-permute-start.12 = (bf16[48,48,128]{2,1,0:T(8,128)(2,1)S(1)}, bf16[48,48,128]{2,1,0:T(8,128)(2,1)S(1)}, u32[]{:S(2)}, u32[]{:S(2)}) collective-permute-start(bf16[48,48,128]{2,1,0:T(8,128)(2,1)S(1)} %get-tuple-element.35.own_ref), channel_id=1, source_target_pairs={{0,1},{1,0},{2,3},{3,2},{4,5},{5,4},{6,7},{7,6},{8,9},{9,8},{10,11... | collective-permute-start | bytes 1769480 | tf_op jit(solution)/shard_map/ppermute | solution.py:370
  74.6 10.6 %collective-permute-start.13 = (bf16[48,48,128]{2,1,0:T(8,128)(2,1)S(1)}, bf16[48,48,128]{2,1,0:T(8,128)(2,1)S(1)}, u32[]{:S(2)}, u32[]{:S(2)}) collective-permute-start(bf16[48,48,128]{2,1,0:T(8,128)(2,1)S(1)} %get-tuple-element.35.own_ref), channel_id=1, source_target_pairs={{0,7},{1,2},{2,1},{3,4},{4,3},{5,6},{6,5},{7,0},{8,15},{9,10},{10,... | collective-permute-start | bytes 1769480 | tf_op jit(solution)/shard_map/ppermute | solution.py:370
  85.6 16.7 %collective-permute-start.17 = (bf16[48,48,128]{2,1,0:T(8,128)(2,1)S(1)}, bf16[48,48,128]{2,1,0:T(8,128)(2,1)S(1)}, u32[]{:S(2)}, u32[]{:S(2)}) collective-permute-start(bf16[48,48,128]{2,1,0:T(8,128)(2,1)S(1)} %shard_map.130.after_ref.own_ref), channel_id=1, source_target_pairs={{0,8},{8,0},{16,24},{24,16},{32,40},{40,32},{48,56},{56,48},{64,72... | collective-permute-start | bytes 1769480 | tf_op jit(solution)/shard_map/ppermute | solution.py:381
  87.3 17.2 %collective-permute-start.18 = (bf16[48,48,128]{2,1,0:T(8,128)(2,1)S(1)}, bf16[48,48,128]{2,1,0:T(8,128)(2,1)S(1)}, u32[]{:S(2)}, u32[]{:S(2)}) collective-permute-start(bf16[48,48,128]{2,1,0:T(8,128)(2,1)S(1)} %shard_map.130.after_ref.own_ref), channel_id=1, source_target_pairs={{0,1},{1,0},{2,3},{3,2},{4,5},{5,4},{6,7},{7,6},{8,16},{9,17},{10,... | collective-permute-start | bytes 1769480 | tf_op jit(solution)/shard_map/ppermute | solution.py:381
  91.9 12.6 %copy-start.2 = (bf16[2,48,48,128]{3,2,1,0:T(8,128)(2,1)S(1)}, bf16[2,48,48,128]{3,2,1,0:T(8,128)(2,1)}, u32[]{:S(2)}) copy-start(bf16[2,48,48,128]{3,2,1,0:T(8,128)(2,1)} %member_ref.5) | copy-start | bytes 3538948
  93.5 15.5 %collective-permute-start.14 = (bf16[64,48,128]{2,1,0:T(8,128)(2,1)S(1)}, bf16[64,48,128]{2,1,0:T(8,128)(2,1)S(1)}, u32[]{:S(2)}, u32[]{:S(2)}) collective-permute-start(bf16[64,48,128]{2,1,0:T(8,128)(2,1)S(1)} %get-tuple-element.36.own_ref), channel_id=1, source_target_pairs={{0,1},{1,0},{2,3},{3,2},{4,5},{5,4},{6,7},{7,6},{8,9},{9,8},{10,11... | collective-permute-start | bytes 2359304 | tf_op jit(solution)/shard_map/ppermute | solution.py:370
  93.6 15.4 %collective-permute-start.15 = (bf16[48,48,128]{2,1,0:T(8,128)(2,1)S(1)}, bf16[48,48,128]{2,1,0:T(8,128)(2,1)S(1)}, u32[]{:S(2)}, u32[]{:S(2)}) collective-permute-start(bf16[48,48,128]{2,1,0:T(8,128)(2,1)S(1)} %get-tuple-element.37), channel_id=1, source_target_pairs={{0,7},{1,2},{2,1},{3,4},{4,3},{5,6},{6,5},{7,0},{8,15},{9,10},{10,... | collective-permute-start | bytes 1769480 | tf_op jit(solution)/shard_map/ppermute | solution.py:370
  99.3 9.7 %collective-permute-start.16 = (bf16[16,48,128]{2,1,0:T(8,128)(2,1)S(1)}, bf16[16,48,128]{2,1,0:T(8,128)(2,1)S(1)}, u32[]{:S(2)}, u32[]{:S(2)}) collective-permute-start(bf16[16,48,128]{2,1,0:T(8,128)(2,1)S(1)} %get-tuple-element.38), channel_id=1, source_target_pairs={{0,7},{1,2},{2,1},{3,4},{4,3},{5,6},{6,5},{7,0},{8,15},{9,10},{10,... | collective-permute-start | bytes 589832 | tf_op jit(solution)/shard_map/ppermute | solution.py:370

commit v6 on v5

--- a/solution.py
+++ b/solution.py
@@ -254,7 +254,7 @@
 
 
 def residual_kernel(
-    kept0, came0, kept1, came1, dep_ref, weight_ref, pert_ref, vert_ref, static_ref, even_ref, odd_ref, own_ref, b_ref
+    kept0, came0, kept1, came1, kept2, came2, dep_ref, weight_ref, pert_ref, vert_ref, static_ref, even_ref, odd_ref, own_ref, b_ref
 ):
     vert = vert_ref[...]
     static_mat = static_block(static_ref)
@@ -263,7 +263,8 @@
         res = []
         for x in (4 * i, 24 + 4 * i):
             at = pl.ds(x, 4)
-            parts = [kept[at] + came[at].astype(F32) for kept, came in ((kept0, came0), (kept1, came1))]
+            pairs = ((kept0, came0), (kept1, came1), (kept2, came2))
+            parts = [kept[at] + came[at].astype(F32) for kept, came in pairs]
             total = jnp.concatenate(parts, axis=1)
             r = (weight_ref[at].astype(F32) * (total - dep_ref[at].astype(F32))).astype(BF)
             r32 = r.astype(F32)
@@ -426,7 +427,7 @@
     )
     size = lax.axis_size("mem")
     parts, sent = (), first
-    for cols, cost in (((0, 32), 700_000_000), ((32, TILE), LONG)):
+    for cols, cost in (((0, 16), 700_000_000), ((16, 32), LONG), ((32, TILE), LONG)):
         wide = (TILE, cols[1] - cols[0], 128)
         args = (taps,) + b + (first, perturbations, local_vertical, static_vertical, sent)
         kept, sent = call(

time: 112 us -> 111 us (level)
  waiting for transfers between devices: 66.3 us -> 61.7 us
  starting transfers between devices: 30.2 us -> 34.3 us
    ppermute x2 -> x3, waiting for transfers between devices: 24.1 us -> 17.3 us  [body(): lax.ppermute(sent, 'mem', [(i, size - 1 - i) for i in range(size)])]
    ppermute x2 -> x3, starting transfers between devices: 6.48 us -> 12.5 us  [body(): lax.ppermute(sent, 'mem', [(i, size - 1 - i) for i in range(size)])]
    ppermute x4, waiting for transfers between devices: 6.87 us -> 8.94 us  [swaps_x(): lax.ppermute(even, 'tx', first)]
    pallas_call x12 -> x13, Pallas kernels: 10.9 us -> 11.1 us  [call(): pl.pallas_call(kernel, out_shape=outs, in_specs=[ANY if i in in_any else...]
  transfers between devices with their start and end apart: 19 -> 20, of which waited for: 13 -> 15; matrix products, arithmetic and copies ran while one was open for 0% -> 0% of each run, Pallas kernels for 6% -> 7%
where the time goes in v6:
time: 111 us; the launch traced here: 110 us
  waiting for transfers between devices  61.7 us (56%)
  starting transfers between devices  34.3 us (31%)
  Pallas kernels  11.1 us (10%)
  local copies, waits for them, and re-layouts  2.37 us (2%)
    ppermute x5, waiting for transfers between devices, swaps_y(): lax.ppermute(part, 'ty', second)  24.4 us
    ppermute x3, waiting for transfers between devices, body(): lax.ppermute(sent, 'mem', [(i, size - 1 - i) for i in range(size)])  17.3 us
    ppermute x3, starting transfers between devices, body(): lax.ppermute(sent, 'mem', [(i, size - 1 - i) for i in range(size)])  12.5 us
    ppermute x5, starting transfers between devices, swaps_y(): lax.ppermute(part, 'ty', second)  11.3 us
    pallas_call x13, Pallas kernels, call(): pl.pallas_call(kernel, out_shape=outs, in_specs=[ANY if i in in_any else...  11.1 us
    ppermute x4, waiting for transfers between devices, swaps_x(): lax.ppermute(odd, ('tx', 'ty'), second)  9.56 us
    ppermute x4, waiting for transfers between devices, swaps_x(): lax.ppermute(even, 'tx', first)  8.94 us
    ppermute x4, starting transfers between devices, swaps_x(): lax.ppermute(odd, ('tx', 'ty'), second)  5.33 us
  transfers between devices with their start and end apart: 20, of which 15 were waited for; matrix products, arithmetic and copies ran while one was open for 0% of the time, Pallas kernels for 7%

profile of v6, /device:TPU:32, one launch (start us, length us, event | category | flops | bytes accessed | tf_op | source)
XLA Modules:
  0.0 110.5 jit_solution(138797217901045487)
XLA Ops:
  0.6 0.0 copy-start.1
  0.6 1.3 %copy-done.1 = bf16[2,48,48,128]{3,2,1,0:T(8,128)(2,1)S(1)} copy-done((bf16[2,48,48,128]{3,2,1,0:T(8,128)(2,1)S(1)}, bf16[2,48,48,128]{3,2,1,0:T(8,128)(2,1)}, u32[]{:S(2)}) %copy-start.1) | copy-done | bytes 1179672
  1.9 1.1 copy-done.3
  3.0 0.3 shard_map.123
  3.3 0.1 collective-permute-start
  3.4 2.9 %collective-permute-start.1 = (bf16[3072,128]{1,0:T(8,128)(2,1)S(1)}, bf16[3072,128]{1,0:T(8,128)(2,1)S(1)}, u32[]{:S(2)}, u32[]{:S(2)}) collective-permute-start(bf16[3072,128]{1,0:T(8,128)(2,1)S(1)} %get-tuple-element.25), channel_id=1, source_target_pairs={{0,7},{1,2},{2,1},{3,4},{4,3},{5,6},{6,5},{7,0},{8,15},{9,10},{10,... | collective-permute-start | bytes 2359304 | tf_op jit(solution)/shard_map/ppermute | solution.py:371
  6.3 1.6 %collective-permute-start.4 = (bf16[48,48,128]{2,1,0:T(8,128)(2,1)S(1)}, bf16[48,48,128]{2,1,0:T(8,128)(2,1)S(1)}, u32[]{:S(2)}, u32[]{:S(2)}) collective-permute-start(bf16[48,48,128]{2,1,0:T(8,128)(2,1)S(1)} %get-tuple-element.29.own_ref), channel_id=1, source_target_pairs={{0,8},{8,0},{16,24},{24,16},{32,40},{40,32},{48,56},{56,48},{64,72... | collective-permute-start | bytes 1769480 | tf_op jit(solution)/shard_map/ppermute | solution.py:382
  7.9 1.7 %collective-permute-start.5 = (bf16[48,48,128]{2,1,0:T(8,128)(2,1)S(1)}, bf16[48,48,128]{2,1,0:T(8,128)(2,1)S(1)}, u32[]{:S(2)}, u32[]{:S(2)}) collective-permute-start(bf16[48,48,128]{2,1,0:T(8,128)(2,1)S(1)} %get-tuple-element.29.own_ref), channel_id=1, source_target_pairs={{0,1},{1,0},{2,3},{3,2},{4,5},{5,4},{6,7},{7,6},{8,16},{9,17},{10,... | collective-permute-start | bytes 1769480 | tf_op jit(solution)/shard_map/ppermute | solution.py:382
  9.6 0.0 copy-done.8
  9.6 0.2 shard_map.122.taps_ref
  9.8 0.0 collective-permute-done.even_ref
  9.8 6.4 %collective-permute-done.1.odd_ref = bf16[3072,128]{1,0:T(8,128)(2,1)S(1)} collective-permute-done((bf16[3072,128]{1,0:T(8,128)(2,1)S(1)}, bf16[3072,128]{1,0:T(8,128)(2,1)S(1)}, u32[]{:S(2)}, u32[]{:S(2)}) %collective-permute-start.1) | collective-permute-done | bytes 786464 | tf_op jit(solution)/shard_map/ppermute | solution.py:371
  16.1 0.6 shard_map.124
  16.8 1.7 %collective-permute-start.2 = (bf16[60,48,128]{2,1,0:T(8,128)(2,1)S(1)}, bf16[60,48,128]{2,1,0:T(8,128)(2,1)S(1)}, u32[]{:S(2)}, u32[]{:S(2)}) collective-permute-start(bf16[60,48,128]{2,1,0:T(8,128)(2,1)S(1)} %get-tuple-element.26.own_ref), channel_id=1, source_target_pairs={{0,8},{8,0},{16,24},{24,16},{32,40},{40,32},{48,56},{56,48},{64,72... | collective-permute-start | bytes 2211848 | tf_op jit(solution)/shard_map/ppermute | solution.py:382
  18.5 1.7 %collective-permute-start.3 = (bf16[60,48,128]{2,1,0:T(8,128)(2,1)S(1)}, bf16[60,48,128]{2,1,0:T(8,128)(2,1)S(1)}, u32[]{:S(2)}, u32[]{:S(2)}) collective-permute-start(bf16[60,48,128]{2,1,0:T(8,128)(2,1)S(1)} %get-tuple-element.27), channel_id=1, source_target_pairs={{0,1},{1,0},{2,3},{3,2},{4,5},{5,4},{6,7},{7,6},{8,16},{9,17},{10,... | collective-permute-start | bytes 2211848 | tf_op jit(solution)/shard_map/ppermute | solution.py:382
  20.2 1.5 %collective-permute-done.4.even_ref = bf16[48,48,128]{2,1,0:T(8,128)(2,1)S(1)} collective-permute-done((bf16[48,48,128]{2,1,0:T(8,128)(2,1)S(1)}, bf16[48,48,128]{2,1,0:T(8,128)(2,1)S(1)}, u32[]{:S(2)}, u32[]{:S(2)}) %collective-permute-start.4) | collective-permute-done | bytes 589856 | tf_op jit(solution)/shard_map/ppermute | solution.py:382
  21.7 3.4 %collective-permute-done.5.odd_ref = bf16[48,48,128]{2,1,0:T(8,128)(2,1)S(1)} collective-permute-done((bf16[48,48,128]{2,1,0:T(8,128)(2,1)S(1)}, bf16[48,48,128]{2,1,0:T(8,128)(2,1)S(1)}, u32[]{:S(2)}, u32[]{:S(2)}) %collective-permute-start.5) | collective-permute-done | bytes 589856 | tf_op jit(solution)/shard_map/ppermute | solution.py:382
  25.1 1.0 shard_map.125.own_ref
  26.1 0.0 copy-start.7
  26.1 0.1 collective-permute-start.6
  26.2 0.5 collective-permute-start.7
  26.7 1.5 %collective-permute-done.6.even_ref = bf16[48,48,128]{2,1,0:T(8,128)(2,1)S(1)} collective-permute-done((bf16[48,48,128]{2,1,0:T(8,128)(2,1)S(1)}, bf16[48,48,128]{2,1,0:T(8,128)(2,1)S(1)}, u32[]{:S(2)}, u32[]{:S(2)}) %collective-permute-start.6) | collective-permute-done | bytes 589856 | tf_op jit(solution)/shard_map/ppermute | solution.py:371
  28.2 8.6 %collective-permute-done.7.odd_ref = bf16[48,48,128]{2,1,0:T(8,128)(2,1)S(1)} collective-permute-done((bf16[48,48,128]{2,1,0:T(8,128)(2,1)S(1)}, bf16[48,48,128]{2,1,0:T(8,128)(2,1)S(1)}, u32[]{:S(2)}, u32[]{:S(2)}) %collective-permute-start.7) | collective-permute-done | bytes 589856 | tf_op jit(solution)/shard_map/ppermute | solution.py:371
  36.8 0.0 copy-done.6
  36.8 0.6 shard_map.126.first_ref.after_ref
  37.4 0.0 collective-permute-done.2.even_ref
  37.4 2.1 %collective-permute-done.3.odd_ref = bf16[60,48,128]{2,1,0:T(8,128)(2,1)S(1)} collective-permute-done((bf16[60,48,128]{2,1,0:T(8,128)(2,1)S(1)}, bf16[60,48,128]{2,1,0:T(8,128)(2,1)S(1)}, u32[]{:S(2)}, u32[]{:S(2)}) %collective-permute-start.3) | collective-permute-done | bytes 737312 | tf_op jit(solution)/shard_map/ppermute | solution.py:382
  39.6 0.0 copy-done.7
  39.6 0.7 shard_map.127
  40.3 6.4 %collective-permute-start.8 = (bf16[48,16,128]{2,1,0:T(8,128)(2,1)S(1)}, bf16[48,16,128]{2,1,0:T(8,128)(2,1)S(1)}, u32[]{:S(2)}, u32[]{:S(2)}) collective-permute-start(bf16[48,16,128]{2,1,0:T(8,128)(2,1)S(1)} %get-tuple-element.31.after_ref), channel_id=1, source_target_pairs={{0,128},{128,0},{1,129},{129,1},{2,130},{130,2},{3,131},{131,3},{4... | collective-permute-start | bytes 589832 | tf_op jit(solution)/shard_map/ppermute | solution.py:437
  46.7 0.7 shard_map.128
  47.4 0.0 copy-start.4
  47.5 0.0 copy-start.5
  47.5 0.1 collective-permute-start.9
  47.6 0.7 shard_map.129
  48.3 6.0 %collective-permute-start.10 = (bf16[48,16,128]{2,1,0:T(8,128)(2,1)S(1)}, bf16[48,16,128]{2,1,0:T(8,128)(2,1)S(1)}, u32[]{:S(2)}, u32[]{:S(2)}) collective-permute-start(bf16[48,16,128]{2,1,0:T(8,128)(2,1)S(1)} %get-tuple-element.35), channel_id=1, source_target_pairs={{0,128},{128,0},{1,129},{129,1},{2,130},{130,2},{3,131},{131,3},{4... | collective-permute-start | bytes 589832 | tf_op jit(solution)/shard_map/ppermute | solution.py:437
  54.3 3.6 %collective-permute-done.8.came0 = bf16[48,16,128]{2,1,0:T(8,128)(2,1)S(1)} collective-permute-done((bf16[48,16,128]{2,1,0:T(8,128)(2,1)S(1)}, bf16[48,16,128]{2,1,0:T(8,128)(2,1)S(1)}, u32[]{:S(2)}, u32[]{:S(2)}) %collective-permute-start.8) | collective-permute-done | bytes 196640 | tf_op jit(solution)/shard_map/ppermute | solution.py:437
  57.9 10.4 %collective-permute-done.9.came1 = bf16[48,16,128]{2,1,0:T(8,128)(2,1)S(1)} collective-permute-done((bf16[48,16,128]{2,1,0:T(8,128)(2,1)S(1)}, bf16[48,16,128]{2,1,0:T(8,128)(2,1)S(1)}, u32[]{:S(2)}, u32[]{:S(2)}) %collective-permute-start.9) | collective-permute-done | bytes 196640 | tf_op jit(solution)/shard_map/ppermute | solution.py:437
  68.3 3.3 %collective-permute-done.10.came2 = bf16[48,16,128]{2,1,0:T(8,128)(2,1)S(1)} collective-permute-done((bf16[48,16,128]{2,1,0:T(8,128)(2,1)S(1)}, bf16[48,16,128]{2,1,0:T(8,128)(2,1)S(1)}, u32[]{:S(2)}, u32[]{:S(2)}) %collective-permute-start.10) | collective-permute-done | bytes 196640 | tf_op jit(solution)/shard_map/ppermute | solution.py:437
  71.7 0.0 copy-done.4
  71.7 0.9 shard_map.130
  72.6 0.1 collective-permute-start.11
  72.7 0.3 collective-permute-start.12
  73.0 0.1 collective-permute-start.13
  73.1 4.2 %collective-permute-start.14 = (bf16[48,48,128]{2,1,0:T(8,128)(2,1)S(1)}, bf16[48,48,128]{2,1,0:T(8,128)(2,1)S(1)}, u32[]{:S(2)}, u32[]{:S(2)}) collective-permute-start(bf16[48,48,128]{2,1,0:T(8,128)(2,1)S(1)} %get-tuple-element.39.own_ref), channel_id=1, source_target_pairs={{0,7},{1,2},{2,1},{3,4},{4,3},{5,6},{6,5},{7,0},{8,15},{9,10},{10,... | collective-permute-start | bytes 1769480 | tf_op jit(solution)/shard_map/ppermute | solution.py:371
  77.3 0.0 collective-permute-done.13.even_ref
  77.3 7.6 %collective-permute-done.14.odd_ref = bf16[48,48,128]{2,1,0:T(8,128)(2,1)S(1)} collective-permute-done((bf16[48,48,128]{2,1,0:T(8,128)(2,1)S(1)}, bf16[48,48,128]{2,1,0:T(8,128)(2,1)S(1)}, u32[]{:S(2)}, u32[]{:S(2)}) %collective-permute-start.14) | collective-permute-done | bytes 589856 | tf_op jit(solution)/shard_map/ppermute | solution.py:371
  84.9 0.4 shard_map.131.after_ref.own_ref
  85.3 1.5 %collective-permute-start.18 = (bf16[48,48,128]{2,1,0:T(8,128)(2,1)S(1)}, bf16[48,48,128]{2,1,0:T(8,128)(2,1)S(1)}, u32[]{:S(2)}, u32[]{:S(2)}) collective-permute-start(bf16[48,48,128]{2,1,0:T(8,128)(2,1)S(1)} %shard_map.131.after_ref.own_ref), channel_id=1, source_target_pairs={{0,8},{8,0},{16,24},{24,16},{32,40},{40,32},{48,56},{56,48},{64,72... | collective-permute-start | bytes 1769480 | tf_op jit(solution)/shard_map/ppermute | solution.py:382
  86.8 1.6 %collective-permute-start.19 = (bf16[48,48,128]{2,1,0:T(8,128)(2,1)S(1)}, bf16[48,48,128]{2,1,0:T(8,128)(2,1)S(1)}, u32[]{:S(2)}, u32[]{:S(2)}) collective-permute-start(bf16[48,48,128]{2,1,0:T(8,128)(2,1)S(1)} %shard_map.131.after_ref.own_ref), channel_id=1, source_target_pairs={{0,1},{1,0},{2,3},{3,2},{4,5},{5,4},{6,7},{7,6},{8,16},{9,17},{10,... | collective-permute-start | bytes 1769480 | tf_op jit(solution)/shard_map/ppermute | solution.py:382
  88.4 3.7 %collective-permute-done.11.even_ref = bf16[60,48,128]{2,1,0:T(8,128)(2,1)S(1)} collective-permute-done((bf16[60,48,128]{2,1,0:T(8,128)(2,1)S(1)}, bf16[60,48,128]{2,1,0:T(8,128)(2,1)S(1)}, u32[]{:S(2)}, u32[]{:S(2)}) %collective-permute-start.11) | collective-permute-done | bytes 737312 | tf_op jit(solution)/shard_map/ppermute | solution.py:382
  92.1 1.6 %collective-permute-done.12.odd_ref = bf16[60,48,128]{2,1,0:T(8,128)(2,1)S(1)} collective-permute-done((bf16[60,48,128]{2,1,0:T(8,128)(2,1)S(1)}, bf16[60,48,128]{2,1,0:T(8,128)(2,1)S(1)}, u32[]{:S(2)}, u32[]{:S(2)}) %collective-permute-start.12) | collective-permute-done | bytes 737312 | tf_op jit(solution)/shard_map/ppermute | solution.py:382
  93.8 1.5 %shard_map.132 = (bf16[64,48,128]{2,1,0:T(8,128)(2,1)S(1)}, bf16[48,48,128]{2,1,0:T(8,128)(2,1)S(1)}, bf16[16,48,128]{2,1,0:T(8,128)(2,1)S(1)}, bf16[24,48,128]{2,1,0:T(8,128)(2,1)S(1)}) custom-call(f32[8,256]{1,0:T(8,128)S(1)} %shard_map.122.taps_ref, bf16[60,48,128]{2,1,0:T(8,128)(2,1)S(1)} %get-tuple-element.36.sent_ref, ...), custom_call_target="tpu_custom_call" | custom-call | flops 20000000000 | bytes 4972544 | tf_op jit(solution)/shard_map/pallas_call | solution.py:26
  95.3 0.1 collective-permute-start.15
  95.4 3.7 %collective-permute-start.16 = (bf16[48,48,128]{2,1,0:T(8,128)(2,1)S(1)}, bf16[48,48,128]{2,1,0:T(8,128)(2,1)S(1)}, u32[]{:S(2)}, u32[]{:S(2)}) collective-permute-start(bf16[48,48,128]{2,1,0:T(8,128)(2,1)S(1)} %get-tuple-element.41), channel_id=1, source_target_pairs={{0,7},{1,2},{2,1},{3,4},{4,3},{5,6},{6,5},{7,0},{8,15},{9,10},{10,... | collective-permute-start | bytes 1769480 | tf_op jit(solution)/shard_map/ppermute | solution.py:371
  99.1 0.0 collective-permute-start.17
  99.2 3.7 %collective-permute-done.18.even_ref = bf16[48,48,128]{2,1,0:T(8,128)(2,1)S(1)} collective-permute-done((bf16[48,48,128]{2,1,0:T(8,128)(2,1)S(1)}, bf16[48,48,128]{2,1,0:T(8,128)(2,1)S(1)}, u32[]{:S(2)}, u32[]{:S(2)}) %collective-permute-start.18) | collective-permute-done | bytes 589856 | tf_op jit(solution)/shard_map/ppermute | solution.py:382
  102.8 2.4 %collective-permute-done.19.odd_ref = bf16[48,48,128]{2,1,0:T(8,128)(2,1)S(1)} collective-permute-done((bf16[48,48,128]{2,1,0:T(8,128)(2,1)S(1)}, bf16[48,48,128]{2,1,0:T(8,128)(2,1)S(1)}, u32[]{:S(2)}, u32[]{:S(2)}) %collective-permute-start.19) | collective-permute-done | bytes 589856 | tf_op jit(solution)/shard_map/ppermute | solution.py:382
  105.2 0.0 copy-done.2
  105.2 1.7 %shard_map.133.begun_ref = bf16[2,48,48,128]{3,2,1,0:T(8,128)(2,1)} custom-call(f32[8,256]{1,0:T(8,128)S(1)} %shard_map.122.taps_ref, bf16[48,48,128]{2,1,0:T(8,128)(2,1)S(1)} %shard_map.131.after_ref.own_ref, bf16[48,48,128]{2,1,0:T(8,128)(2,1)S(1)} %collective-permute-done.18.even_ref, bf16[48,48,128]{2,1,0:T(8,128)(2,1)S(1)} %collective-permute-done.19.odd_ref, ...), custom_call_target="tpu_custom_call" | custom-call | flops 20000000000 | bytes 4136960 | tf_op jit(solution)/shard_map/pallas_call | solution.py:26
  107.0 1.8 %collective-permute-done.17.slab_ref = bf16[16,48,128]{2,1,0:T(8,128)(2,1)S(1)} collective-permute-done((bf16[16,48,128]{2,1,0:T(8,128)(2,1)S(1)}, bf16[16,48,128]{2,1,0:T(8,128)(2,1)S(1)}, u32[]{:S(2)}, u32[]{:S(2)}) %collective-permute-start.17) | collective-permute-done | bytes 196640 | tf_op jit(solution)/shard_map/ppermute | solution.py:371
  108.8 0.0 collective-permute-done.16.odd_ref
  108.8 0.0 collective-permute-done.15.even_ref
  108.8 1.5 %shard_map.134 = (bf16[48,48,64]{2,1,0:T(8,128)(2,1)}, bf16[2,48,48,128]{3,2,1,0:T(8,128)(2,1)}) custom-call(f32[8,256]{1,0:T(8,128)S(1)} %shard_map.122.taps_ref, bf16[64,48,128]{2,1,0:T(8,128)(2,1)S(1)} %get-tuple-element.40.own_ref, bf16[64,48,128]{2,1,0:T(8,128)(2,1)S(1)} %collective-permute-done.15.even_ref, ...), custom_call_target="tpu_custom_call", output_to_operand_aliasing={{1}: (8, {})} | custom-call | flops 700000000 | bytes 6791168 | tf_op jit(solution)/shard_map/pallas_call | solution.py:26
  (13 shorter events, 0.0 us)
Async XLA Ops:
  0.6 1.3 %copy-start.1 = (bf16[2,48,48,128]{3,2,1,0:T(8,128)(2,1)S(1)}, bf16[2,48,48,128]{3,2,1,0:T(8,128)(2,1)}, u32[]{:S(2)}) copy-start(bf16[2,48,48,128]{3,2,1,0:T(8,128)(2,1)} %member_ref.5) | copy-start | bytes 3538948
  1.9 1.1 copy-start.3
  3.0 6.6 %copy-start.8 = (bf16[97]{0:T(256)(128)(2,1)S(1)}, bf16[97]{0:T(256)(128)(2,1)}, u32[]{:S(2)}) copy-start(bf16[97]{0:T(256)(128)(2,1)} %lx_ref.1) | copy-start | bytes 586
  3.0 6.6 %copy-start.9 = (bf16[97]{0:T(256)(128)(2,1)S(1)}, bf16[97]{0:T(256)(128)(2,1)}, u32[]{:S(2)}) copy-start(bf16[97]{0:T(256)(128)(2,1)} %ly_ref.1) | copy-start | bytes 586
  3.0 6.6 %copy-start.10 = (bf16[49]{0:T(256)(128)(2,1)S(1)}, bf16[49]{0:T(256)(128)(2,1)}, u32[]{:S(2)}) copy-start(bf16[49]{0:T(256)(128)(2,1)} %sx_ref.1) | copy-start | bytes 298
  3.0 6.6 %copy-start.11 = (bf16[49]{0:T(256)(128)(2,1)S(1)}, bf16[49]{0:T(256)(128)(2,1)}, u32[]{:S(2)}) copy-start(bf16[49]{0:T(256)(128)(2,1)} %sy_ref.1) | copy-start | bytes 298
  3.3 6.5 %collective-permute-start = (bf16[3072,128]{1,0:T(8,128)(2,1)S(1)}, bf16[3072,128]{1,0:T(8,128)(2,1)S(1)}, u32[]{:S(2)}, u32[]{:S(2)}) collective-permute-start(bf16[3072,128]{1,0:T(8,128)(2,1)S(1)} %get-tuple-element.23.sent_ref), channel_id=1, source_target_pairs={{0,1},{1,0},{2,3},{3,2},{4,5},{5,4},{6,7},{7,6},{8,9},{9,8},{10,11... | collective-permute-start | bytes 2359304 | tf_op jit(solution)/shard_map/ppermute | solution.py:371
  3.4 12.7 %collective-permute-start.1 = (bf16[3072,128]{1,0:T(8,128)(2,1)S(1)}, bf16[3072,128]{1,0:T(8,128)(2,1)S(1)}, u32[]{:S(2)}, u32[]{:S(2)}) collective-permute-start(bf16[3072,128]{1,0:T(8,128)(2,1)S(1)} %get-tuple-element.25), channel_id=1, source_target_pairs={{0,7},{1,2},{2,1},{3,4},{4,3},{5,6},{6,5},{7,0},{8,15},{9,10},{10,... | collective-permute-start | bytes 2359304 | tf_op jit(solution)/shard_map/ppermute | solution.py:371
  6.3 15.4 %collective-permute-start.4 = (bf16[48,48,128]{2,1,0:T(8,128)(2,1)S(1)}, bf16[48,48,128]{2,1,0:T(8,128)(2,1)S(1)}, u32[]{:S(2)}, u32[]{:S(2)}) collective-permute-start(bf16[48,48,128]{2,1,0:T(8,128)(2,1)S(1)} %get-tuple-element.29.own_ref), channel_id=1, source_target_pairs={{0,8},{8,0},{16,24},{24,16},{32,40},{40,32},{48,56},{56,48},{64,72... | collective-permute-start | bytes 1769480 | tf_op jit(solution)/shard_map/ppermute | solution.py:382
  7.9 17.2 %collective-permute-start.5 = (bf16[48,48,128]{2,1,0:T(8,128)(2,1)S(1)}, bf16[48,48,128]{2,1,0:T(8,128)(2,1)S(1)}, u32[]{:S(2)}, u32[]{:S(2)}) collective-permute-start(bf16[48,48,128]{2,1,0:T(8,128)(2,1)S(1)} %get-tuple-element.29.own_ref), channel_id=1, source_target_pairs={{0,1},{1,0},{2,3},{3,2},{4,5},{5,4},{6,7},{7,6},{8,16},{9,17},{10,... | collective-permute-start | bytes 1769480 | tf_op jit(solution)/shard_map/ppermute | solution.py:382
  16.8 20.6 %collective-permute-start.2 = (bf16[60,48,128]{2,1,0:T(8,128)(2,1)S(1)}, bf16[60,48,128]{2,1,0:T(8,128)(2,1)S(1)}, u32[]{:S(2)}, u32[]{:S(2)}) collective-permute-start(bf16[60,48,128]{2,1,0:T(8,128)(2,1)S(1)} %get-tuple-element.26.own_ref), channel_id=1, source_target_pairs={{0,8},{8,0},{16,24},{24,16},{32,40},{40,32},{48,56},{56,48},{64,72... | collective-permute-start | bytes 2211848 | tf_op jit(solution)/shard_map/ppermute | solution.py:382
  18.4 18.4 %copy-start = (bf16[2,48,48,128]{3,2,1,0:T(8,128)(2,1)S(1)}, bf16[2,48,48,128]{3,2,1,0:T(8,128)(2,1)}, u32[]{:S(2)}) copy-start(bf16[2,48,48,128]{3,2,1,0:T(8,128)(2,1)} %pert_ref.9) | copy-start | bytes 3538948
  18.4 18.4 %copy-start.6 = (bf16[128,128]{1,0:T(8,128)(2,1)S(1)}, bf16[128,128]{1,0:T(8,128)(2,1)}, u32[]{:S(2)}) copy-start(bf16[128,128]{1,0:T(8,128)(2,1)} %vert_ref.9) | copy-start | bytes 98308
  18.5 21.1 %collective-permute-start.3 = (bf16[60,48,128]{2,1,0:T(8,128)(2,1)S(1)}, bf16[60,48,128]{2,1,0:T(8,128)(2,1)S(1)}, u32[]{:S(2)}, u32[]{:S(2)}) collective-permute-start(bf16[60,48,128]{2,1,0:T(8,128)(2,1)S(1)} %get-tuple-element.27), channel_id=1, source_target_pairs={{0,1},{1,0},{2,3},{3,2},{4,5},{5,4},{6,7},{7,6},{8,16},{9,17},{10,... | collective-permute-start | bytes 2211848 | tf_op jit(solution)/shard_map/ppermute | solution.py:382
  26.1 13.5 %copy-start.7 = (bf16[128,128]{1,0:T(8,128)(2,1)S(1)}, bf16[128,128]{1,0:T(8,128)(2,1)}, u32[]{:S(2)}) copy-start(bf16[128,128]{1,0:T(8,128)(2,1)} %static_ref.9) | copy-start | bytes 98308
  26.1 2.1 %collective-permute-start.6 = (bf16[48,48,128]{2,1,0:T(8,128)(2,1)S(1)}, bf16[48,48,128]{2,1,0:T(8,128)(2,1)S(1)}, u32[]{:S(2)}, u32[]{:S(2)}) collective-permute-start(bf16[48,48,128]{2,1,0:T(8,128)(2,1)S(1)} %shard_map.125.own_ref), channel_id=1, source_target_pairs={{0,1},{1,0},{2,3},{3,2},{4,5},{5,4},{6,7},{7,6},{8,9},{9,8},{10,11... | collective-permute-start | bytes 1769480 | tf_op jit(solution)/shard_map/ppermute | solution.py:371
  26.2 10.6 %collective-permute-start.7 = (bf16[48,48,128]{2,1,0:T(8,128)(2,1)S(1)}, bf16[48,48,128]{2,1,0:T(8,128)(2,1)S(1)}, u32[]{:S(2)}, u32[]{:S(2)}) collective-permute-start(bf16[48,48,128]{2,1,0:T(8,128)(2,1)S(1)} %shard_map.125.own_ref), channel_id=1, source_target_pairs={{0,7},{1,2},{2,1},{3,4},{4,3},{5,6},{6,5},{7,0},{8,15},{9,10},{10,... | collective-permute-start | bytes 1769480 | tf_op jit(solution)/shard_map/ppermute | solution.py:371
  40.3 17.6 %collective-permute-start.8 = (bf16[48,16,128]{2,1,0:T(8,128)(2,1)S(1)}, bf16[48,16,128]{2,1,0:T(8,128)(2,1)S(1)}, u32[]{:S(2)}, u32[]{:S(2)}) collective-permute-start(bf16[48,16,128]{2,1,0:T(8,128)(2,1)S(1)} %get-tuple-element.31.after_ref), channel_id=1, source_target_pairs={{0,128},{128,0},{1,129},{129,1},{2,130},{130,2},{3,131},{131,3},{4... | collective-permute-start | bytes 589832 | tf_op jit(solution)/shard_map/ppermute | solution.py:437
  47.4 24.2 %copy-start.4 = (bf16[48,48,128]{2,1,0:T(8,128)(2,1)S(1)}, bf16[48,48,128]{2,1,0:T(8,128)(2,1)}, u32[]{:S(2)}) copy-start(bf16[48,48,128]{2,1,0:T(8,128)(2,1)} %dep_ref.1) | copy-start | bytes 1769476
  47.5 24.2 %copy-start.5 = (bf16[48,48,128]{2,1,0:T(8,128)(2,1)S(1)}, bf16[48,48,128]{2,1,0:T(8,128)(2,1)}, u32[]{:S(2)}) copy-start(bf16[48,48,128]{2,1,0:T(8,128)(2,1)} %weight_ref.1) | copy-start | bytes 1769476
  47.5 20.9 %collective-permute-start.9 = (bf16[48,16,128]{2,1,0:T(8,128)(2,1)S(1)}, bf16[48,16,128]{2,1,0:T(8,128)(2,1)S(1)}, u32[]{:S(2)}, u32[]{:S(2)}) collective-permute-start(bf16[48,16,128]{2,1,0:T(8,128)(2,1)S(1)} %get-tuple-element.33.after_ref), channel_id=1, source_target_pairs={{0,128},{128,0},{1,129},{129,1},{2,130},{130,2},{3,131},{131,3},{4... | collective-permute-start | bytes 589832 | tf_op jit(solution)/shard_map/ppermute | solution.py:437
  48.3 23.3 %collective-permute-start.10 = (bf16[48,16,128]{2,1,0:T(8,128)(2,1)S(1)}, bf16[48,16,128]{2,1,0:T(8,128)(2,1)S(1)}, u32[]{:S(2)}, u32[]{:S(2)}) collective-permute-start(bf16[48,16,128]{2,1,0:T(8,128)(2,1)S(1)} %get-tuple-element.35), channel_id=1, source_target_pairs={{0,128},{128,0},{1,129},{129,1},{2,130},{130,2},{3,131},{131,3},{4... | collective-permute-start | bytes 589832 | tf_op jit(solution)/shard_map/ppermute | solution.py:437
  72.6 19.5 %collective-permute-start.11 = (bf16[60,48,128]{2,1,0:T(8,128)(2,1)S(1)}, bf16[60,48,128]{2,1,0:T(8,128)(2,1)S(1)}, u32[]{:S(2)}, u32[]{:S(2)}) collective-permute-start(bf16[60,48,128]{2,1,0:T(8,128)(2,1)S(1)} %get-tuple-element.36.sent_ref), channel_id=1, source_target_pairs={{0,8},{8,0},{16,24},{24,16},{32,40},{40,32},{48,56},{56,48},{64,72... | collective-permute-start | bytes 2211848 | tf_op jit(solution)/shard_map/ppermute | solution.py:382
  72.7 21.1 %collective-permute-start.12 = (bf16[60,48,128]{2,1,0:T(8,128)(2,1)S(1)}, bf16[60,48,128]{2,1,0:T(8,128)(2,1)S(1)}, u32[]{:S(2)}, u32[]{:S(2)}) collective-permute-start(bf16[60,48,128]{2,1,0:T(8,128)(2,1)S(1)} %get-tuple-element.38), channel_id=1, source_target_pairs={{0,1},{1,0},{2,3},{3,2},{4,5},{5,4},{6,7},{7,6},{8,16},{9,17},{10,... | collective-permute-start | bytes 2211848 | tf_op jit(solution)/shard_map/ppermute | solution.py:382
  73.0 4.3 %collective-permute-start.13 = (bf16[48,48,128]{2,1,0:T(8,128)(2,1)S(1)}, bf16[48,48,128]{2,1,0:T(8,128)(2,1)S(1)}, u32[]{:S(2)}, u32[]{:S(2)}) collective-permute-start(bf16[48,48,128]{2,1,0:T(8,128)(2,1)S(1)} %get-tuple-element.39.own_ref), channel_id=1, source_target_pairs={{0,1},{1,0},{2,3},{3,2},{4,5},{5,4},{6,7},{7,6},{8,9},{9,8},{10,11... | collective-permute-start | bytes 1769480 | tf_op jit(solution)/shard_map/ppermute | solution.py:371
  73.1 11.8 %collective-permute-start.14 = (bf16[48,48,128]{2,1,0:T(8,128)(2,1)S(1)}, bf16[48,48,128]{2,1,0:T(8,128)(2,1)S(1)}, u32[]{:S(2)}, u32[]{:S(2)}) collective-permute-start(bf16[48,48,128]{2,1,0:T(8,128)(2,1)S(1)} %get-tuple-element.39.own_ref), channel_id=1, source_target_pairs={{0,7},{1,2},{2,1},{3,4},{4,3},{5,6},{6,5},{7,0},{8,15},{9,10},{10,... | collective-permute-start | bytes 1769480 | tf_op jit(solution)/shard_map/ppermute | solution.py:371
  85.3 17.5 %collective-permute-start.18 = (bf16[48,48,128]{2,1,0:T(8,128)(2,1)S(1)}, bf16[48,48,128]{2,1,0:T(8,128)(2,1)S(1)}, u32[]{:S(2)}, u32[]{:S(2)}) collective-permute-start(bf16[48,48,128]{2,1,0:T(8,128)(2,1)S(1)} %shard_map.131.after_ref.own_ref), channel_id=1, source_target_pairs={{0,8},{8,0},{16,24},{24,16},{32,40},{40,32},{48,56},{56,48},{64,72... | collective-permute-start | bytes 1769480 | tf_op jit(solution)/shard_map/ppermute | solution.py:382
  86.8 18.4 %collective-permute-start.19 = (bf16[48,48,128]{2,1,0:T(8,128)(2,1)S(1)}, bf16[48,48,128]{2,1,0:T(8,128)(2,1)S(1)}, u32[]{:S(2)}, u32[]{:S(2)}) collective-permute-start(bf16[48,48,128]{2,1,0:T(8,128)(2,1)S(1)} %shard_map.131.after_ref.own_ref), channel_id=1, source_target_pairs={{0,1},{1,0},{2,3},{3,2},{4,5},{5,4},{6,7},{7,6},{8,16},{9,17},{10,... | collective-permute-start | bytes 1769480 | tf_op jit(solution)/shard_map/ppermute | solution.py:382
  93.8 11.5 %copy-start.2 = (bf16[2,48,48,128]{3,2,1,0:T(8,128)(2,1)S(1)}, bf16[2,48,48,128]{3,2,1,0:T(8,128)(2,1)}, u32[]{:S(2)}) copy-start(bf16[2,48,48,128]{3,2,1,0:T(8,128)(2,1)} %member_ref.5) | copy-start | bytes 3538948
  95.3 13.5 %collective-permute-start.15 = (bf16[64,48,128]{2,1,0:T(8,128)(2,1)S(1)}, bf16[64,48,128]{2,1,0:T(8,128)(2,1)S(1)}, u32[]{:S(2)}, u32[]{:S(2)}) collective-permute-start(bf16[64,48,128]{2,1,0:T(8,128)(2,1)S(1)} %get-tuple-element.40.own_ref), channel_id=1, source_target_pairs={{0,1},{1,0},{2,3},{3,2},{4,5},{5,4},{6,7},{7,6},{8,9},{9,8},{10,11... | collective-permute-start | bytes 2359304 | tf_op jit(solution)/shard_map/ppermute | solution.py:371
  95.4 13.4 %collective-permute-start.16 = (bf16[48,48,128]{2,1,0:T(8,128)(2,1)S(1)}, bf16[48,48,128]{2,1,0:T(8,128)(2,1)S(1)}, u32[]{:S(2)}, u32[]{:S(2)}) collective-permute-start(bf16[48,48,128]{2,1,0:T(8,128)(2,1)S(1)} %get-tuple-element.41), channel_id=1, source_target_pairs={{0,7},{1,2},{2,1},{3,4},{4,3},{5,6},{6,5},{7,0},{8,15},{9,10},{10,... | collective-permute-start | bytes 1769480 | tf_op jit(solution)/shard_map/ppermute | solution.py:371
  99.1 9.7 %collective-permute-start.17 = (bf16[16,48,128]{2,1,0:T(8,128)(2,1)S(1)}, bf16[16,48,128]{2,1,0:T(8,128)(2,1)S(1)}, u32[]{:S(2)}, u32[]{:S(2)}) collective-permute-start(bf16[16,48,128]{2,1,0:T(8,128)(2,1)S(1)} %get-tuple-element.42), channel_id=1, source_target_pairs={{0,7},{1,2},{2,1},{3,4},{4,3},{5,6},{6,5},{7,0},{8,15},{9,10},{10,... | collective-permute-start | bytes 589832 | tf_op jit(solution)/shard_map/ppermute | solution.py:371

commit v7 on v6

--- a/solution.py
+++ b/solution.py
@@ -153,7 +153,7 @@
     pack_slabs(packed, even_ref, odd_ref)
 
 
-def first_y_kernel(row_m, row_s, taps_ref, sent_ref, own_ref, even_ref, odd_ref, to_even_ref, to_odd_ref, out_ref):
+def first_y_kernel(row_m, row_s, taps_ref, sent_ref, own_ref, odd_ref, even_ref, to_even_ref, to_odd_ref, out_ref):
     member = band_swapped(taps_ref[row_m : row_m + 1], "ty")
     static = band(taps_ref[row_s : row_s + 1], TILE, 112)
 
@@ -384,7 +384,7 @@
 
 def first_filters(taps, a, to_even, to_odd, own):
     a_halo = swaps_x(a, a)
-    b_halo = swaps_y(to_even, to_odd)
+    b_halo = swaps_y(to_even, to_odd)[::-1]
     tile = (TILE, TILE, 128)
     b_to_even, b_to_odd, s = call(
         functools.partial(first_y_kernel, 1, 3),

time: 111 us -> 112 us (level)
  waiting for transfers between devices: 61.7 us -> 65.9 us
  starting transfers between devices: 34.3 us -> 31.1 us
    ppermute x5, starting transfers between devices: 11.3 us -> 7.19 us  [swaps_y(): lax.ppermute(part, 'ty', second)]
    ppermute x4, starting transfers between devices: 4.81 us -> 6.3 us  [swaps_x(): lax.ppermute(even, 'tx', first)]
  transfers between devices with their start and end apart: 20 -> 20, of which waited for: 15 -> 16; matrix products, arithmetic and copies ran while one was open for 0% -> 0% of each run, Pallas kernels for 7% -> 7%
where the time goes in v7:
time: 112 us; the launch traced here: 111 us
  waiting for transfers between devices  65.9 us (59%)
  starting transfers between devices  31.1 us (28%)
  Pallas kernels  11.1 us (10%)
  local copies, waits for them, and re-layouts  2.37 us (2%)
    ppermute x5, waiting for transfers between devices, swaps_y(): lax.ppermute(part, 'ty', second)  25.4 us
    ppermute x3, waiting for transfers between devices, body(): lax.ppermute(sent, 'mem', [(i, size - 1 - i) for i in range(size)])  18 us
    ppermute x3, starting transfers between devices, body(): lax.ppermute(sent, 'mem', [(i, size - 1 - i) for i in range(size)])  12.5 us
    pallas_call x13, Pallas kernels, call(): pl.pallas_call(kernel, out_shape=outs, in_specs=[ANY if i in in_any else...  11.1 us
    ppermute x4, waiting for transfers between devices, swaps_x(): lax.ppermute(odd, ('tx', 'ty'), second)  10.5 us
    ppermute x4, waiting for transfers between devices, swaps_x(): lax.ppermute(even, 'tx', first)  9.79 us
    ppermute x5, starting transfers between devices, swaps_y(): lax.ppermute(part, 'ty', second)  7.19 us
    ppermute x4, starting transfers between devices, swaps_x(): lax.ppermute(even, 'tx', first)  6.3 us
  transfers between devices with their start and end apart: 20, of which 16 were waited for; matrix products, arithmetic and copies ran while one was open for 0% of the time, Pallas kernels for 7%

profile of v7, /device:TPU:32, one launch (start us, length us, event | category | flops | bytes accessed | tf_op | source)
XLA Modules:
  0.0 111.5 jit_solution(12380966173050980923)
XLA Ops:
  0.6 0.0 copy-start.1
  0.6 1.3 %copy-done.1 = bf16[2,48,48,128]{3,2,1,0:T(8,128)(2,1)S(1)} copy-done((bf16[2,48,48,128]{3,2,1,0:T(8,128)(2,1)S(1)}, bf16[2,48,48,128]{3,2,1,0:T(8,128)(2,1)}, u32[]{:S(2)}) %copy-start.1) | copy-done | bytes 1179672
  1.9 1.1 copy-done.3
  3.0 0.3 shard_map.123
  3.3 2.3 %collective-permute-start = (bf16[3072,128]{1,0:T(8,128)(2,1)S(1)}, bf16[3072,128]{1,0:T(8,128)(2,1)S(1)}, u32[]{:S(2)}, u32[]{:S(2)}) collective-permute-start(bf16[3072,128]{1,0:T(8,128)(2,1)S(1)} %get-tuple-element.25), channel_id=1, source_target_pairs={{0,7},{1,2},{2,1},{3,4},{4,3},{5,6},{6,5},{7,0},{8,15},{9,10},{10,... | collective-permute-start | bytes 2359304 | tf_op jit(solution)/shard_map/ppermute | solution.py:371
  5.6 0.0 collective-permute-start.1
  5.6 1.6 %collective-permute-start.4 = (bf16[48,48,128]{2,1,0:T(8,128)(2,1)S(1)}, bf16[48,48,128]{2,1,0:T(8,128)(2,1)S(1)}, u32[]{:S(2)}, u32[]{:S(2)}) collective-permute-start(bf16[48,48,128]{2,1,0:T(8,128)(2,1)S(1)} %get-tuple-element.29.own_ref), channel_id=1, source_target_pairs={{0,8},{8,0},{16,24},{24,16},{32,40},{40,32},{48,56},{56,48},{64,72... | collective-permute-start | bytes 1769480 | tf_op jit(solution)/shard_map/ppermute | solution.py:382
  7.2 1.7 %collective-permute-start.5 = (bf16[48,48,128]{2,1,0:T(8,128)(2,1)S(1)}, bf16[48,48,128]{2,1,0:T(8,128)(2,1)S(1)}, u32[]{:S(2)}, u32[]{:S(2)}) collective-permute-start(bf16[48,48,128]{2,1,0:T(8,128)(2,1)S(1)} %get-tuple-element.29.own_ref), channel_id=1, source_target_pairs={{0,1},{1,0},{2,3},{3,2},{4,5},{5,4},{6,7},{7,6},{8,16},{9,17},{10,... | collective-permute-start | bytes 1769480 | tf_op jit(solution)/shard_map/ppermute | solution.py:382
  8.9 0.0 copy-done.8
  8.9 0.0 copy-done.9
  8.9 0.2 shard_map.122.taps_ref
  9.1 6.9 %collective-permute-done.odd_ref = bf16[3072,128]{1,0:T(8,128)(2,1)S(1)} collective-permute-done((bf16[3072,128]{1,0:T(8,128)(2,1)S(1)}, bf16[3072,128]{1,0:T(8,128)(2,1)S(1)}, u32[]{:S(2)}, u32[]{:S(2)}) %collective-permute-start) | collective-permute-done | bytes 786464 | tf_op jit(solution)/shard_map/ppermute | solution.py:371
  16.0 0.0 collective-permute-done.1.even_ref
  16.1 0.6 shard_map.124
  16.7 1.7 %collective-permute-start.2 = (bf16[60,48,128]{2,1,0:T(8,128)(2,1)S(1)}, bf16[60,48,128]{2,1,0:T(8,128)(2,1)S(1)}, u32[]{:S(2)}, u32[]{:S(2)}) collective-permute-start(bf16[60,48,128]{2,1,0:T(8,128)(2,1)S(1)} %get-tuple-element.26.own_ref), channel_id=1, source_target_pairs={{0,8},{8,0},{16,24},{24,16},{32,40},{40,32},{48,56},{56,48},{64,72... | collective-permute-start | bytes 2211848 | tf_op jit(solution)/shard_map/ppermute | solution.py:382
  18.4 1.7 %collective-permute-start.3 = (bf16[60,48,128]{2,1,0:T(8,128)(2,1)S(1)}, bf16[60,48,128]{2,1,0:T(8,128)(2,1)S(1)}, u32[]{:S(2)}, u32[]{:S(2)}) collective-permute-start(bf16[60,48,128]{2,1,0:T(8,128)(2,1)S(1)} %get-tuple-element.27), channel_id=1, source_target_pairs={{0,1},{1,0},{2,3},{3,2},{4,5},{5,4},{6,7},{7,6},{8,16},{9,17},{10,... | collective-permute-start | bytes 2211848 | tf_op jit(solution)/shard_map/ppermute | solution.py:382
  20.1 1.7 %collective-permute-done.4.even_ref = bf16[48,48,128]{2,1,0:T(8,128)(2,1)S(1)} collective-permute-done((bf16[48,48,128]{2,1,0:T(8,128)(2,1)S(1)}, bf16[48,48,128]{2,1,0:T(8,128)(2,1)S(1)}, u32[]{:S(2)}, u32[]{:S(2)}) %collective-permute-start.4) | collective-permute-done | bytes 589856 | tf_op jit(solution)/shard_map/ppermute | solution.py:382
  21.7 3.7 %collective-permute-done.5.odd_ref = bf16[48,48,128]{2,1,0:T(8,128)(2,1)S(1)} collective-permute-done((bf16[48,48,128]{2,1,0:T(8,128)(2,1)S(1)}, bf16[48,48,128]{2,1,0:T(8,128)(2,1)S(1)}, u32[]{:S(2)}, u32[]{:S(2)}) %collective-permute-start.5) | collective-permute-done | bytes 589856 | tf_op jit(solution)/shard_map/ppermute | solution.py:382
  25.5 1.0 shard_map.125.own_ref
  26.4 0.0 copy-start.7
  26.5 0.1 collective-permute-start.6
  26.6 0.4 collective-permute-start.7
  26.9 1.6 %collective-permute-done.6.even_ref = bf16[48,48,128]{2,1,0:T(8,128)(2,1)S(1)} collective-permute-done((bf16[48,48,128]{2,1,0:T(8,128)(2,1)S(1)}, bf16[48,48,128]{2,1,0:T(8,128)(2,1)S(1)}, u32[]{:S(2)}, u32[]{:S(2)}) %collective-permute-start.6) | collective-permute-done | bytes 589856 | tf_op jit(solution)/shard_map/ppermute | solution.py:371
  28.6 8.6 %collective-permute-done.7.odd_ref = bf16[48,48,128]{2,1,0:T(8,128)(2,1)S(1)} collective-permute-done((bf16[48,48,128]{2,1,0:T(8,128)(2,1)S(1)}, bf16[48,48,128]{2,1,0:T(8,128)(2,1)S(1)}, u32[]{:S(2)}, u32[]{:S(2)}) %collective-permute-start.7) | collective-permute-done | bytes 589856 | tf_op jit(solution)/shard_map/ppermute | solution.py:371
  37.2 0.0 copy-done
  37.2 0.6 shard_map.126.first_ref.after_ref
  37.8 0.0 collective-permute-done.2.even_ref
  37.8 2.8 %collective-permute-done.3.odd_ref = bf16[60,48,128]{2,1,0:T(8,128)(2,1)S(1)} collective-permute-done((bf16[60,48,128]{2,1,0:T(8,128)(2,1)S(1)}, bf16[60,48,128]{2,1,0:T(8,128)(2,1)S(1)}, u32[]{:S(2)}, u32[]{:S(2)}) %collective-permute-start.3) | collective-permute-done | bytes 737312 | tf_op jit(solution)/shard_map/ppermute | solution.py:382
  40.6 0.7 shard_map.127
  41.3 6.4 %collective-permute-start.8 = (bf16[48,16,128]{2,1,0:T(8,128)(2,1)S(1)}, bf16[48,16,128]{2,1,0:T(8,128)(2,1)S(1)}, u32[]{:S(2)}, u32[]{:S(2)}) collective-permute-start(bf16[48,16,128]{2,1,0:T(8,128)(2,1)S(1)} %get-tuple-element.31.after_ref), channel_id=1, source_target_pairs={{0,128},{128,0},{1,129},{129,1},{2,130},{130,2},{3,131},{131,3},{4... | collective-permute-start | bytes 589832 | tf_op jit(solution)/shard_map/ppermute | solution.py:437
  47.7 0.7 shard_map.128
  48.4 0.0 copy-start.4
  48.5 0.0 copy-start.5
  48.5 0.1 collective-permute-start.9
  48.6 0.7 shard_map.129
  49.3 6.0 %collective-permute-start.10 = (bf16[48,16,128]{2,1,0:T(8,128)(2,1)S(1)}, bf16[48,16,128]{2,1,0:T(8,128)(2,1)S(1)}, u32[]{:S(2)}, u32[]{:S(2)}) collective-permute-start(bf16[48,16,128]{2,1,0:T(8,128)(2,1)S(1)} %get-tuple-element.35), channel_id=1, source_target_pairs={{0,128},{128,0},{1,129},{129,1},{2,130},{130,2},{3,131},{131,3},{4... | collective-permute-start | bytes 589832 | tf_op jit(solution)/shard_map/ppermute | solution.py:437
  55.3 4.3 %collective-permute-done.8.came0 = bf16[48,16,128]{2,1,0:T(8,128)(2,1)S(1)} collective-permute-done((bf16[48,16,128]{2,1,0:T(8,128)(2,1)S(1)}, bf16[48,16,128]{2,1,0:T(8,128)(2,1)S(1)}, u32[]{:S(2)}, u32[]{:S(2)}) %collective-permute-start.8) | collective-permute-done | bytes 196640 | tf_op jit(solution)/shard_map/ppermute | solution.py:437
  59.6 10.4 %collective-permute-done.9.came1 = bf16[48,16,128]{2,1,0:T(8,128)(2,1)S(1)} collective-permute-done((bf16[48,16,128]{2,1,0:T(8,128)(2,1)S(1)}, bf16[48,16,128]{2,1,0:T(8,128)(2,1)S(1)}, u32[]{:S(2)}, u32[]{:S(2)}) %collective-permute-start.9) | collective-permute-done | bytes 196640 | tf_op jit(solution)/shard_map/ppermute | solution.py:437
  70.0 3.3 %collective-permute-done.10.came2 = bf16[48,16,128]{2,1,0:T(8,128)(2,1)S(1)} collective-permute-done((bf16[48,16,128]{2,1,0:T(8,128)(2,1)S(1)}, bf16[48,16,128]{2,1,0:T(8,128)(2,1)S(1)}, u32[]{:S(2)}, u32[]{:S(2)}) %collective-permute-start.10) | collective-permute-done | bytes 196640 | tf_op jit(solution)/shard_map/ppermute | solution.py:437
  73.3 0.0 copy-done.5
  73.3 0.9 shard_map.130
  74.3 0.1 collective-permute-start.11
  74.4 0.3 collective-permute-start.12
  74.6 0.1 collective-permute-start.13
  74.7 1.5 %collective-permute-start.14 = (bf16[48,48,128]{2,1,0:T(8,128)(2,1)S(1)}, bf16[48,48,128]{2,1,0:T(8,128)(2,1)S(1)}, u32[]{:S(2)}, u32[]{:S(2)}) collective-permute-start(bf16[48,48,128]{2,1,0:T(8,128)(2,1)S(1)} %get-tuple-element.39.own_ref), channel_id=1, source_target_pairs={{0,7},{1,2},{2,1},{3,4},{4,3},{5,6},{6,5},{7,0},{8,15},{9,10},{10,... | collective-permute-start | bytes 1769480 | tf_op jit(solution)/shard_map/ppermute | solution.py:371
  76.2 0.5 collective-permute-done.13.even_ref
  76.7 8.6 %collective-permute-done.14.odd_ref = bf16[48,48,128]{2,1,0:T(8,128)(2,1)S(1)} collective-permute-done((bf16[48,48,128]{2,1,0:T(8,128)(2,1)S(1)}, bf16[48,48,128]{2,1,0:T(8,128)(2,1)S(1)}, u32[]{:S(2)}, u32[]{:S(2)}) %collective-permute-start.14) | collective-permute-done | bytes 589856 | tf_op jit(solution)/shard_map/ppermute | solution.py:371
  85.3 0.4 shard_map.131.after_ref.own_ref
  85.8 3.0 %collective-permute-start.18 = (bf16[48,48,128]{2,1,0:T(8,128)(2,1)S(1)}, bf16[48,48,128]{2,1,0:T(8,128)(2,1)S(1)}, u32[]{:S(2)}, u32[]{:S(2)}) collective-permute-start(bf16[48,48,128]{2,1,0:T(8,128)(2,1)S(1)} %shard_map.131.after_ref.own_ref), channel_id=1, source_target_pairs={{0,8},{8,0},{16,24},{24,16},{32,40},{40,32},{48,56},{56,48},{64,72... | collective-permute-start | bytes 1769480 | tf_op jit(solution)/shard_map/ppermute | solution.py:382
  88.7 1.1 %collective-permute-start.19 = (bf16[48,48,128]{2,1,0:T(8,128)(2,1)S(1)}, bf16[48,48,128]{2,1,0:T(8,128)(2,1)S(1)}, u32[]{:S(2)}, u32[]{:S(2)}) collective-permute-start(bf16[48,48,128]{2,1,0:T(8,128)(2,1)S(1)} %shard_map.131.after_ref.own_ref), channel_id=1, source_target_pairs={{0,1},{1,0},{2,3},{3,2},{4,5},{5,4},{6,7},{7,6},{8,16},{9,17},{10,... | collective-permute-start | bytes 1769480 | tf_op jit(solution)/shard_map/ppermute | solution.py:382
  89.9 3.9 %collective-permute-done.11.even_ref = bf16[60,48,128]{2,1,0:T(8,128)(2,1)S(1)} collective-permute-done((bf16[60,48,128]{2,1,0:T(8,128)(2,1)S(1)}, bf16[60,48,128]{2,1,0:T(8,128)(2,1)S(1)}, u32[]{:S(2)}, u32[]{:S(2)}) %collective-permute-start.11) | collective-permute-done | bytes 737312 | tf_op jit(solution)/shard_map/ppermute | solution.py:382
  93.8 1.7 %collective-permute-done.12.odd_ref = bf16[60,48,128]{2,1,0:T(8,128)(2,1)S(1)} collective-permute-done((bf16[60,48,128]{2,1,0:T(8,128)(2,1)S(1)}, bf16[60,48,128]{2,1,0:T(8,128)(2,1)S(1)}, u32[]{:S(2)}, u32[]{:S(2)}) %collective-permute-start.12) | collective-permute-done | bytes 737312 | tf_op jit(solution)/shard_map/ppermute | solution.py:382
  95.4 1.5 %shard_map.132 = (bf16[64,48,128]{2,1,0:T(8,128)(2,1)S(1)}, bf16[48,48,128]{2,1,0:T(8,128)(2,1)S(1)}, bf16[16,48,128]{2,1,0:T(8,128)(2,1)S(1)}, bf16[24,48,128]{2,1,0:T(8,128)(2,1)S(1)}) custom-call(f32[8,256]{1,0:T(8,128)S(1)} %shard_map.122.taps_ref, bf16[60,48,128]{2,1,0:T(8,128)(2,1)S(1)} %get-tuple-element.36.sent_ref, ...), custom_call_target="tpu_custom_call" | custom-call | flops 20000000000 | bytes 4972544 | tf_op jit(solution)/shard_map/pallas_call | solution.py:26
  97.0 0.1 collective-permute-start.15
  97.1 1.6 %collective-permute-start.16 = (bf16[48,48,128]{2,1,0:T(8,128)(2,1)S(1)}, bf16[48,48,128]{2,1,0:T(8,128)(2,1)S(1)}, u32[]{:S(2)}, u32[]{:S(2)}) collective-permute-start(bf16[48,48,128]{2,1,0:T(8,128)(2,1)S(1)} %get-tuple-element.41), channel_id=1, source_target_pairs={{0,7},{1,2},{2,1},{3,4},{4,3},{5,6},{6,5},{7,0},{8,15},{9,10},{10,... | collective-permute-start | bytes 1769480 | tf_op jit(solution)/shard_map/ppermute | solution.py:371
  98.7 1.5 %collective-permute-start.17 = (bf16[16,48,128]{2,1,0:T(8,128)(2,1)S(1)}, bf16[16,48,128]{2,1,0:T(8,128)(2,1)S(1)}, u32[]{:S(2)}, u32[]{:S(2)}) collective-permute-start(bf16[16,48,128]{2,1,0:T(8,128)(2,1)S(1)} %get-tuple-element.42), channel_id=1, source_target_pairs={{0,7},{1,2},{2,1},{3,4},{4,3},{5,6},{6,5},{7,0},{8,15},{9,10},{10,... | collective-permute-start | bytes 589832 | tf_op jit(solution)/shard_map/ppermute | solution.py:371
  100.1 4.3 %collective-permute-done.18.even_ref = bf16[48,48,128]{2,1,0:T(8,128)(2,1)S(1)} collective-permute-done((bf16[48,48,128]{2,1,0:T(8,128)(2,1)S(1)}, bf16[48,48,128]{2,1,0:T(8,128)(2,1)S(1)}, u32[]{:S(2)}, u32[]{:S(2)}) %collective-permute-start.18) | collective-permute-done | bytes 589856 | tf_op jit(solution)/shard_map/ppermute | solution.py:382
  104.4 2.4 %collective-permute-done.19.odd_ref = bf16[48,48,128]{2,1,0:T(8,128)(2,1)S(1)} collective-permute-done((bf16[48,48,128]{2,1,0:T(8,128)(2,1)S(1)}, bf16[48,48,128]{2,1,0:T(8,128)(2,1)S(1)}, u32[]{:S(2)}, u32[]{:S(2)}) %collective-permute-start.19) | collective-permute-done | bytes 589856 | tf_op jit(solution)/shard_map/ppermute | solution.py:382
  106.8 0.0 copy-done.2
  106.8 1.7 %shard_map.133.begun_ref = bf16[2,48,48,128]{3,2,1,0:T(8,128)(2,1)} custom-call(f32[8,256]{1,0:T(8,128)S(1)} %shard_map.122.taps_ref, bf16[48,48,128]{2,1,0:T(8,128)(2,1)S(1)} %shard_map.131.after_ref.own_ref, bf16[48,48,128]{2,1,0:T(8,128)(2,1)S(1)} %collective-permute-done.18.even_ref, bf16[48,48,128]{2,1,0:T(8,128)(2,1)S(1)} %collective-permute-done.19.odd_ref, ...), custom_call_target="tpu_custom_call" | custom-call | flops 20000000000 | bytes 4136960 | tf_op jit(solution)/shard_map/pallas_call | solution.py:26
  108.5 1.3 %collective-permute-done.17.slab_ref = bf16[16,48,128]{2,1,0:T(8,128)(2,1)S(1)} collective-permute-done((bf16[16,48,128]{2,1,0:T(8,128)(2,1)S(1)}, bf16[16,48,128]{2,1,0:T(8,128)(2,1)S(1)}, u32[]{:S(2)}, u32[]{:S(2)}) %collective-permute-start.17) | collective-permute-done | bytes 196640 | tf_op jit(solution)/shard_map/ppermute | solution.py:371
  109.8 0.0 collective-permute-done.16.odd_ref
  109.8 0.0 collective-permute-done.15.even_ref
  109.8 1.5 %shard_map.134 = (bf16[48,48,64]{2,1,0:T(8,128)(2,1)}, bf16[2,48,48,128]{3,2,1,0:T(8,128)(2,1)}) custom-call(f32[8,256]{1,0:T(8,128)S(1)} %shard_map.122.taps_ref, bf16[64,48,128]{2,1,0:T(8,128)(2,1)S(1)} %get-tuple-element.40.own_ref, bf16[64,48,128]{2,1,0:T(8,128)(2,1)S(1)} %collective-permute-done.15.even_ref, ...), custom_call_target="tpu_custom_call", output_to_operand_aliasing={{1}: (8, {})} | custom-call | flops 700000000 | bytes 6791168 | tf_op jit(solution)/shard_map/pallas_call | solution.py:26
  (13 shorter events, 0.0 us)
Async XLA Ops:
  0.6 1.3 %copy-start.1 = (bf16[2,48,48,128]{3,2,1,0:T(8,128)(2,1)S(1)}, bf16[2,48,48,128]{3,2,1,0:T(8,128)(2,1)}, u32[]{:S(2)}) copy-start(bf16[2,48,48,128]{3,2,1,0:T(8,128)(2,1)} %member_ref.5) | copy-start | bytes 3538948
  1.9 1.1 copy-start.3
  3.0 6.0 %copy-start.8 = (bf16[97]{0:T(256)(128)(2,1)S(1)}, bf16[97]{0:T(256)(128)(2,1)}, u32[]{:S(2)}) copy-start(bf16[97]{0:T(256)(128)(2,1)} %lx_ref.1) | copy-start | bytes 586
  3.0 6.0 %copy-start.9 = (bf16[97]{0:T(256)(128)(2,1)S(1)}, bf16[97]{0:T(256)(128)(2,1)}, u32[]{:S(2)}) copy-start(bf16[97]{0:T(256)(128)(2,1)} %ly_ref.1) | copy-start | bytes 586
  3.0 6.0 %copy-start.10 = (bf16[49]{0:T(256)(128)(2,1)S(1)}, bf16[49]{0:T(256)(128)(2,1)}, u32[]{:S(2)}) copy-start(bf16[49]{0:T(256)(128)(2,1)} %sx_ref.1) | copy-start | bytes 298
  3.0 6.0 %copy-start.11 = (bf16[49]{0:T(256)(128)(2,1)S(1)}, bf16[49]{0:T(256)(128)(2,1)}, u32[]{:S(2)}) copy-start(bf16[49]{0:T(256)(128)(2,1)} %sy_ref.1) | copy-start | bytes 298
  3.3 12.7 %collective-permute-start = (bf16[3072,128]{1,0:T(8,128)(2,1)S(1)}, bf16[3072,128]{1,0:T(8,128)(2,1)S(1)}, u32[]{:S(2)}, u32[]{:S(2)}) collective-permute-start(bf16[3072,128]{1,0:T(8,128)(2,1)S(1)} %get-tuple-element.25), channel_id=1, source_target_pairs={{0,7},{1,2},{2,1},{3,4},{4,3},{5,6},{6,5},{7,0},{8,15},{9,10},{10,... | collective-permute-start | bytes 2359304 | tf_op jit(solution)/shard_map/ppermute | solution.py:371
  5.6 10.4 %collective-permute-start.1 = (bf16[3072,128]{1,0:T(8,128)(2,1)S(1)}, bf16[3072,128]{1,0:T(8,128)(2,1)S(1)}, u32[]{:S(2)}, u32[]{:S(2)}) collective-permute-start(bf16[3072,128]{1,0:T(8,128)(2,1)S(1)} %get-tuple-element.23.sent_ref), channel_id=1, source_target_pairs={{0,1},{1,0},{2,3},{3,2},{4,5},{5,4},{6,7},{7,6},{8,9},{9,8},{10,11... | collective-permute-start | bytes 2359304 | tf_op jit(solution)/shard_map/ppermute | solution.py:371
  5.6 16.1 %collective-permute-start.4 = (bf16[48,48,128]{2,1,0:T(8,128)(2,1)S(1)}, bf16[48,48,128]{2,1,0:T(8,128)(2,1)S(1)}, u32[]{:S(2)}, u32[]{:S(2)}) collective-permute-start(bf16[48,48,128]{2,1,0:T(8,128)(2,1)S(1)} %get-tuple-element.29.own_ref), channel_id=1, source_target_pairs={{0,8},{8,0},{16,24},{24,16},{32,40},{40,32},{48,56},{56,48},{64,72... | collective-permute-start | bytes 1769480 | tf_op jit(solution)/shard_map/ppermute | solution.py:382
  7.2 18.3 %collective-permute-start.5 = (bf16[48,48,128]{2,1,0:T(8,128)(2,1)S(1)}, bf16[48,48,128]{2,1,0:T(8,128)(2,1)S(1)}, u32[]{:S(2)}, u32[]{:S(2)}) collective-permute-start(bf16[48,48,128]{2,1,0:T(8,128)(2,1)S(1)} %get-tuple-element.29.own_ref), channel_id=1, source_target_pairs={{0,1},{1,0},{2,3},{3,2},{4,5},{5,4},{6,7},{7,6},{8,16},{9,17},{10,... | collective-permute-start | bytes 1769480 | tf_op jit(solution)/shard_map/ppermute | solution.py:382
  16.7 21.1 %collective-permute-start.2 = (bf16[60,48,128]{2,1,0:T(8,128)(2,1)S(1)}, bf16[60,48,128]{2,1,0:T(8,128)(2,1)S(1)}, u32[]{:S(2)}, u32[]{:S(2)}) collective-permute-start(bf16[60,48,128]{2,1,0:T(8,128)(2,1)S(1)} %get-tuple-element.26.own_ref), channel_id=1, source_target_pairs={{0,8},{8,0},{16,24},{24,16},{32,40},{40,32},{48,56},{56,48},{64,72... | collective-permute-start | bytes 2211848 | tf_op jit(solution)/shard_map/ppermute | solution.py:382
  18.3 18.8 %copy-start = (bf16[2,48,48,128]{3,2,1,0:T(8,128)(2,1)S(1)}, bf16[2,48,48,128]{3,2,1,0:T(8,128)(2,1)}, u32[]{:S(2)}) copy-start(bf16[2,48,48,128]{3,2,1,0:T(8,128)(2,1)} %pert_ref.9) | copy-start | bytes 3538948
  18.4 18.8 %copy-start.6 = (bf16[128,128]{1,0:T(8,128)(2,1)S(1)}, bf16[128,128]{1,0:T(8,128)(2,1)}, u32[]{:S(2)}) copy-start(bf16[128,128]{1,0:T(8,128)(2,1)} %vert_ref.9) | copy-start | bytes 98308
  18.4 22.2 %collective-permute-start.3 = (bf16[60,48,128]{2,1,0:T(8,128)(2,1)S(1)}, bf16[60,48,128]{2,1,0:T(8,128)(2,1)S(1)}, u32[]{:S(2)}, u32[]{:S(2)}) collective-permute-start(bf16[60,48,128]{2,1,0:T(8,128)(2,1)S(1)} %get-tuple-element.27), channel_id=1, source_target_pairs={{0,1},{1,0},{2,3},{3,2},{4,5},{5,4},{6,7},{7,6},{8,16},{9,17},{10,... | collective-permute-start | bytes 2211848 | tf_op jit(solution)/shard_map/ppermute | solution.py:382
  26.4 14.1 %copy-start.7 = (bf16[128,128]{1,0:T(8,128)(2,1)S(1)}, bf16[128,128]{1,0:T(8,128)(2,1)}, u32[]{:S(2)}) copy-start(bf16[128,128]{1,0:T(8,128)(2,1)} %static_ref.9) | copy-start | bytes 98308
  26.5 2.1 %collective-permute-start.6 = (bf16[48,48,128]{2,1,0:T(8,128)(2,1)S(1)}, bf16[48,48,128]{2,1,0:T(8,128)(2,1)S(1)}, u32[]{:S(2)}, u32[]{:S(2)}) collective-permute-start(bf16[48,48,128]{2,1,0:T(8,128)(2,1)S(1)} %shard_map.125.own_ref), channel_id=1, source_target_pairs={{0,1},{1,0},{2,3},{3,2},{4,5},{5,4},{6,7},{7,6},{8,9},{9,8},{10,11... | collective-permute-start | bytes 1769480 | tf_op jit(solution)/shard_map/ppermute | solution.py:371
  26.6 10.6 %collective-permute-start.7 = (bf16[48,48,128]{2,1,0:T(8,128)(2,1)S(1)}, bf16[48,48,128]{2,1,0:T(8,128)(2,1)S(1)}, u32[]{:S(2)}, u32[]{:S(2)}) collective-permute-start(bf16[48,48,128]{2,1,0:T(8,128)(2,1)S(1)} %shard_map.125.own_ref), channel_id=1, source_target_pairs={{0,7},{1,2},{2,1},{3,4},{4,3},{5,6},{6,5},{7,0},{8,15},{9,10},{10,... | collective-permute-start | bytes 1769480 | tf_op jit(solution)/shard_map/ppermute | solution.py:371
  41.3 18.3 %collective-permute-start.8 = (bf16[48,16,128]{2,1,0:T(8,128)(2,1)S(1)}, bf16[48,16,128]{2,1,0:T(8,128)(2,1)S(1)}, u32[]{:S(2)}, u32[]{:S(2)}) collective-permute-start(bf16[48,16,128]{2,1,0:T(8,128)(2,1)S(1)} %get-tuple-element.31.after_ref), channel_id=1, source_target_pairs={{0,128},{128,0},{1,129},{129,1},{2,130},{130,2},{3,131},{131,3},{4... | collective-permute-start | bytes 589832 | tf_op jit(solution)/shard_map/ppermute | solution.py:437
  48.4 24.9 %copy-start.4 = (bf16[48,48,128]{2,1,0:T(8,128)(2,1)S(1)}, bf16[48,48,128]{2,1,0:T(8,128)(2,1)}, u32[]{:S(2)}) copy-start(bf16[48,48,128]{2,1,0:T(8,128)(2,1)} %dep_ref.1) | copy-start | bytes 1769476
  48.5 24.8 %copy-start.5 = (bf16[48,48,128]{2,1,0:T(8,128)(2,1)S(1)}, bf16[48,48,128]{2,1,0:T(8,128)(2,1)}, u32[]{:S(2)}) copy-start(bf16[48,48,128]{2,1,0:T(8,128)(2,1)} %weight_ref.1) | copy-start | bytes 1769476
  48.5 21.5 %collective-permute-start.9 = (bf16[48,16,128]{2,1,0:T(8,128)(2,1)S(1)}, bf16[48,16,128]{2,1,0:T(8,128)(2,1)S(1)}, u32[]{:S(2)}, u32[]{:S(2)}) collective-permute-start(bf16[48,16,128]{2,1,0:T(8,128)(2,1)S(1)} %get-tuple-element.33.after_ref), channel_id=1, source_target_pairs={{0,128},{128,0},{1,129},{129,1},{2,130},{130,2},{3,131},{131,3},{4... | collective-permute-start | bytes 589832 | tf_op jit(solution)/shard_map/ppermute | solution.py:437
  49.3 24.0 %collective-permute-start.10 = (bf16[48,16,128]{2,1,0:T(8,128)(2,1)S(1)}, bf16[48,16,128]{2,1,0:T(8,128)(2,1)S(1)}, u32[]{:S(2)}, u32[]{:S(2)}) collective-permute-start(bf16[48,16,128]{2,1,0:T(8,128)(2,1)S(1)} %get-tuple-element.35), channel_id=1, source_target_pairs={{0,128},{128,0},{1,129},{129,1},{2,130},{130,2},{3,131},{131,3},{4... | collective-permute-start | bytes 589832 | tf_op jit(solution)/shard_map/ppermute | solution.py:437
  74.3 19.5 %collective-permute-start.11 = (bf16[60,48,128]{2,1,0:T(8,128)(2,1)S(1)}, bf16[60,48,128]{2,1,0:T(8,128)(2,1)S(1)}, u32[]{:S(2)}, u32[]{:S(2)}) collective-permute-start(bf16[60,48,128]{2,1,0:T(8,128)(2,1)S(1)} %get-tuple-element.36.sent_ref), channel_id=1, source_target_pairs={{0,8},{8,0},{16,24},{24,16},{32,40},{40,32},{48,56},{56,48},{64,72... | collective-permute-start | bytes 2211848 | tf_op jit(solution)/shard_map/ppermute | solution.py:382
  74.4 21.1 %collective-permute-start.12 = (bf16[60,48,128]{2,1,0:T(8,128)(2,1)S(1)}, bf16[60,48,128]{2,1,0:T(8,128)(2,1)S(1)}, u32[]{:S(2)}, u32[]{:S(2)}) collective-permute-start(bf16[60,48,128]{2,1,0:T(8,128)(2,1)S(1)} %get-tuple-element.38), channel_id=1, source_target_pairs={{0,1},{1,0},{2,3},{3,2},{4,5},{5,4},{6,7},{7,6},{8,16},{9,17},{10,... | collective-permute-start | bytes 2211848 | tf_op jit(solution)/shard_map/ppermute | solution.py:382
  74.6 2.1 %collective-permute-start.13 = (bf16[48,48,128]{2,1,0:T(8,128)(2,1)S(1)}, bf16[48,48,128]{2,1,0:T(8,128)(2,1)S(1)}, u32[]{:S(2)}, u32[]{:S(2)}) collective-permute-start(bf16[48,48,128]{2,1,0:T(8,128)(2,1)S(1)} %get-tuple-element.39.own_ref), channel_id=1, source_target_pairs={{0,1},{1,0},{2,3},{3,2},{4,5},{5,4},{6,7},{7,6},{8,9},{9,8},{10,11... | collective-permute-start | bytes 1769480 | tf_op jit(solution)/shard_map/ppermute | solution.py:371
  74.7 10.6 %collective-permute-start.14 = (bf16[48,48,128]{2,1,0:T(8,128)(2,1)S(1)}, bf16[48,48,128]{2,1,0:T(8,128)(2,1)S(1)}, u32[]{:S(2)}, u32[]{:S(2)}) collective-permute-start(bf16[48,48,128]{2,1,0:T(8,128)(2,1)S(1)} %get-tuple-element.39.own_ref), channel_id=1, source_target_pairs={{0,7},{1,2},{2,1},{3,4},{4,3},{5,6},{6,5},{7,0},{8,15},{9,10},{10,... | collective-permute-start | bytes 1769480 | tf_op jit(solution)/shard_map/ppermute | solution.py:371
  85.8 18.6 %collective-permute-start.18 = (bf16[48,48,128]{2,1,0:T(8,128)(2,1)S(1)}, bf16[48,48,128]{2,1,0:T(8,128)(2,1)S(1)}, u32[]{:S(2)}, u32[]{:S(2)}) collective-permute-start(bf16[48,48,128]{2,1,0:T(8,128)(2,1)S(1)} %shard_map.131.after_ref.own_ref), channel_id=1, source_target_pairs={{0,8},{8,0},{16,24},{24,16},{32,40},{40,32},{48,56},{56,48},{64,72... | collective-permute-start | bytes 1769480 | tf_op jit(solution)/shard_map/ppermute | solution.py:382
  88.7 18.0 %collective-permute-start.19 = (bf16[48,48,128]{2,1,0:T(8,128)(2,1)S(1)}, bf16[48,48,128]{2,1,0:T(8,128)(2,1)S(1)}, u32[]{:S(2)}, u32[]{:S(2)}) collective-permute-start(bf16[48,48,128]{2,1,0:T(8,128)(2,1)S(1)} %shard_map.131.after_ref.own_ref), channel_id=1, source_target_pairs={{0,1},{1,0},{2,3},{3,2},{4,5},{5,4},{6,7},{7,6},{8,16},{9,17},{10,... | collective-permute-start | bytes 1769480 | tf_op jit(solution)/shard_map/ppermute | solution.py:382
  95.4 11.3 %copy-start.2 = (bf16[2,48,48,128]{3,2,1,0:T(8,128)(2,1)S(1)}, bf16[2,48,48,128]{3,2,1,0:T(8,128)(2,1)}, u32[]{:S(2)}) copy-start(bf16[2,48,48,128]{3,2,1,0:T(8,128)(2,1)} %member_ref.5) | copy-start | bytes 3538948
  97.0 12.8 %collective-permute-start.15 = (bf16[64,48,128]{2,1,0:T(8,128)(2,1)S(1)}, bf16[64,48,128]{2,1,0:T(8,128)(2,1)S(1)}, u32[]{:S(2)}, u32[]{:S(2)}) collective-permute-start(bf16[64,48,128]{2,1,0:T(8,128)(2,1)S(1)} %get-tuple-element.40.own_ref), channel_id=1, source_target_pairs={{0,1},{1,0},{2,3},{3,2},{4,5},{5,4},{6,7},{7,6},{8,9},{9,8},{10,11... | collective-permute-start | bytes 2359304 | tf_op jit(solution)/shard_map/ppermute | solution.py:371
  97.1 12.7 %collective-permute-start.16 = (bf16[48,48,128]{2,1,0:T(8,128)(2,1)S(1)}, bf16[48,48,128]{2,1,0:T(8,128)(2,1)S(1)}, u32[]{:S(2)}, u32[]{:S(2)}) collective-permute-start(bf16[48,48,128]{2,1,0:T(8,128)(2,1)S(1)} %get-tuple-element.41), channel_id=1, source_target_pairs={{0,7},{1,2},{2,1},{3,4},{4,3},{5,6},{6,5},{7,0},{8,15},{9,10},{10,... | collective-permute-start | bytes 1769480 | tf_op jit(solution)/shard_map/ppermute | solution.py:371
  98.7 11.1 %collective-permute-start.17 = (bf16[16,48,128]{2,1,0:T(8,128)(2,1)S(1)}, bf16[16,48,128]{2,1,0:T(8,128)(2,1)S(1)}, u32[]{:S(2)}, u32[]{:S(2)}) collective-permute-start(bf16[16,48,128]{2,1,0:T(8,128)(2,1)S(1)} %get-tuple-element.42), channel_id=1, source_target_pairs={{0,7},{1,2},{2,1},{3,4},{4,3},{5,6},{6,5},{7,0},{8,15},{9,10},{10,... | collective-permute-start | bytes 589832 | tf_op jit(solution)/shard_map/ppermute | solution.py:371
